TPU v7x, 32 devices: a whole 2x2x4 slice. The times are simulated.
32 devices in a mesh: row: 8 (over z, y), col: 4 (over x, core).
Axes of the slice: x: 2, y: 2, z: 4, core: 2. Of those that a mesh axis runs over, the one named last changes fastest.
Arguments:
- atom_feats: bfloat16 [2048, 128], P(('row', 'col')), may hold values from -6 to 6
- key_starts: int32 [64], P(('row', 'col')), may hold values from -64 to 1984, as said below
- atom_counts: int32 [128], replicated, may hold values from 8 to 24, as said below
- atom_gain: float32 [128], replicated, may hold values from 0.1 to 1.9
- w_query: bfloat16 [128, 128], replicated, may hold values from -0.5 to 0.5
- w_key: bfloat16 [128, 128], replicated, may hold values from -0.5 to 0.5
- w_value: bfloat16 [128, 128], replicated, may hold values from -0.5 to 0.5
- w_out: bfloat16 [128, 128], replicated, may hold values from -0.5 to 0.5
- w_pool: bfloat16 [128, 384], replicated, may hold values from -0.5 to 0.5
- w_back: bfloat16 [384, 128], replicated, may hold values from -0.3125 to 0.3125
- pair_state: bfloat16 [128, 128, 128], P('row', 'col'), may hold values from -6 to 6
- w_left: bfloat16 [384, 32], replicated, may hold values from -0.3125 to 0.3125
- w_right: bfloat16 [384, 32], replicated, may hold values from -0.3125 to 0.3125
- w_outer: bfloat16 [32, 32, 128], replicated, may hold values from -0.1875 to 0.1875
- pair_gain: float32 [128], replicated, may hold values from 0.1 to 1.9
- w_gate: bfloat16 [128, 512], replicated, may hold values from -0.5 to 0.5
- w_lift: bfloat16 [128, 512], replicated, may hold values from -0.5 to 0.5
- w_drop: bfloat16 [512, 128], replicated, may hold values from -0.25 to 0.25
Outputs:
- atom_out: bfloat16 [2048, 128], P(('row', 'col'))
- token_single: bfloat16 [128, 384], P(('row', 'col'))
- pair_out: bfloat16 [128, 128, 128], P('row', 'col')
Inputs may be any that keep to these rules, and one draw needn't show every extreme that they name: key_starts[b] = 32 * b - 64 + offset, with offset a whole number from 0 to 32; the offset is 0 for the first block and 32 for the last. `atom_counts`: the counts sum to 2048.
All inputs are finite; a program needn't handle non-finite values.
Results may differ from a plain program's by a relative error of at most 0.007.
Values may be sent and summed in bfloat16 or wider, within the bound.
No kernel may reach another device: no remote copies, remote signals or barrier semaphores. Data moves between devices by JAX's collectives and lax.ppermute only.
A program may use at most 64 MiB of HBM per device.

v0:
```python
import math

import jax
import jax.numpy as jnp
from jax import lax
from jax.sharding import PartitionSpec as P

HEADS = 4
QB = 32
KW = 128
FEWEST = 8


EPSILON = 1e-05


def with_halo(block, sides, width):
    for axis, dim in sides:
        count = lax.axis_size(axis)
        forward = [(i, i + 1) for i in range(count - 1)]
        backward = [(target, source) for source, target in forward]
        low = lax.ppermute(
            lax.slice_in_dim(block, block.shape[dim] - width, None, axis=dim), axis, forward
        )
        high = lax.ppermute(lax.slice_in_dim(block, 0, width, axis=dim), axis, backward)
        block = jnp.concatenate([low, block, high], axis=dim)
    return block


def shifted(block, axis, distance):
    devices = range(lax.axis_size(axis))
    route = [(i - distance, i) for i in devices if i - distance in devices]
    return lax.ppermute(block, axis, route)


def layer_norm(values, gain):
    mean_value = jnp.mean(values, axis=-1, keepdims=True)
    centred = values - mean_value
    variance = jnp.mean(centred * centred, axis=-1, keepdims=True)
    return centred * lax.rsqrt(variance + EPSILON) * gain


def project(source, weight):
    return jnp.dot(source, weight, preferred_element_type=jnp.float32).astype(jnp.bfloat16)


def per_device(
    atom_feats,
    key_starts,
    atom_counts,
    atom_gain,
    w_query,
    w_key,
    w_value,
    w_out,
    w_pool,
    w_back,
    pair_state,
    w_left,
    w_right,
    w_outer,
    pair_gain,
    w_gate,
    w_lift,
    w_drop,
):
    atom_rows, atom_width = atom_feats.shape
    devices = lax.axis_size(("row", "col"))
    position = lax.axis_index(("row", "col"))
    total_atoms = atom_rows * devices
    total_tokens = atom_counts.shape[0]
    own_tokens = total_tokens // devices
    rim_width = KW // 2
    first_atom = position * atom_rows
    atom_float = atom_feats.astype(jnp.float32)
    normed = layer_norm(atom_float, atom_gain).astype(jnp.bfloat16)
    queries = project(normed, w_query)
    w_keyval = jnp.concatenate([w_key, w_value], axis=1)
    keyvals = project(normed, w_keyval)
    extended = with_halo(keyvals, ((("row", "col"), 0),), rim_width)
    local_starts = key_starts - first_atom + rim_width
    windows = jax.vmap(lambda first_row: lax.dynamic_slice_in_dim(extended, first_row, KW, 0))(
        local_starts
    )
    head_size = atom_width // HEADS
    blocks = atom_rows // QB
    query_blocks = queries.reshape(blocks, QB, HEADS, head_size)
    key_blocks = windows[:, :, :atom_width].reshape(blocks, KW, HEADS, head_size)
    value_blocks = windows[:, :, atom_width:].reshape(blocks, KW, HEADS, head_size)
    key_index = key_starts[:, None] + jnp.arange(KW, dtype=jnp.int32)[None, :]
    in_range = (key_index >= 0) & (key_index < total_atoms)
    scores = jnp.einsum(
        "bqhd,bkhd->bhqk", query_blocks, key_blocks, preferred_element_type=jnp.float32
    ) * head_size ** (-0.5)
    raised = jnp.where(in_range[:, None, None, :], jnp.exp(scores), 0.0)
    weights = (raised / jnp.sum(raised, axis=-1, keepdims=True)).astype(jnp.bfloat16)
    attended = (
        jnp.einsum("bhqk,bkhd->bqhd", weights, value_blocks, preferred_element_type=jnp.float32)
        .astype(jnp.bfloat16)
        .reshape(atom_rows, atom_width)
    )
    updated = (atom_float + jnp.dot(attended, w_out, preferred_element_type=jnp.float32)).astype(
        jnp.bfloat16
    )
    feature = jax.nn.relu(jnp.dot(updated, w_pool, preferred_element_type=jnp.float32)).astype(
        jnp.bfloat16
    )
    token_ends = jnp.cumsum(atom_counts, dtype=jnp.int32)
    atom_index = first_atom + jnp.arange(atom_rows, dtype=jnp.int32)
    token_of = jnp.sum((token_ends[None, :] <= atom_index[:, None]).astype(jnp.int32), axis=1)
    count_float = atom_counts.astype(jnp.float32)
    slots = atom_rows // FEWEST
    token_starts = token_ends - atom_counts
    base_token = jnp.sum((token_starts < first_atom).astype(jnp.int32))
    relative = token_of - base_token
    slot_range = jnp.arange(slots, dtype=jnp.int32)
    member = (relative[:, None] == slot_range[None, :]).astype(jnp.bfloat16)
    local_sums = jnp.einsum("as,ac->sc", member, feature, preferred_element_type=jnp.float32)
    carried = (relative < 0).astype(jnp.bfloat16)[None, :]
    edge_sum = jnp.dot(carried, feature, preferred_element_type=jnp.float32)
    from_next = shifted(edge_sum, ("row", "col"), -1)
    next_token = jnp.sum((token_ends <= first_atom + atom_rows).astype(jnp.int32))
    target = (slot_range == next_token - base_token).astype(jnp.float32)[:, None]
    pooled_slots = local_sums + target * from_next
    padded_counts = jnp.concatenate([count_float, jnp.ones((slots,), jnp.float32)])
    slot_counts = lax.dynamic_slice_in_dim(padded_counts, base_token, slots, 0)
    slot_single = (pooled_slots / slot_counts[:, None]).astype(jnp.bfloat16)
    owner = token_starts // atom_rows
    owner_first = jnp.searchsorted(token_starts, owner * atom_rows, side="left")
    row_of = owner * slots + jnp.arange(total_tokens, dtype=jnp.int32) - owner_first
    gathered = lax.all_gather(slot_single, ("row", "col"), axis=0, tiled=True)
    full_single = jnp.take(gathered, row_of, axis=0)
    left_all = project(full_single, w_left)
    right_all = project(full_single, w_right)
    back_all = project(full_single, w_back)
    token_single = lax.dynamic_slice_in_dim(full_single, position * own_tokens, own_tokens, 0)
    member_all = (token_of[:, None] == jnp.arange(total_tokens, dtype=jnp.int32)[None, :]).astype(
        jnp.bfloat16
    )
    lifted = jnp.dot(member_all, back_all, preferred_element_type=jnp.float32)
    atom_out = (updated.astype(jnp.float32) + lifted).astype(jnp.bfloat16)
    row_tokens, col_tokens, pair_width = pair_state.shape
    left_rows = lax.dynamic_slice_in_dim(
        left_all, lax.axis_index("row") * row_tokens, row_tokens, 0
    )
    right_cols = lax.dynamic_slice_in_dim(
        right_all, lax.axis_index("col") * col_tokens, col_tokens, 0
    )
    outer_table = jnp.einsum(
        "jb,abc->jac", right_cols, w_outer, preferred_element_type=jnp.float32
    ).astype(jnp.bfloat16)
    step_rows = math.gcd(row_tokens, 8)

    def pair_block(pieces):
        left_block, pair_piece = pieces
        outer_term = jnp.einsum(
            "ia,jac->ijc", left_block, outer_table, preferred_element_type=jnp.float32
        )
        summed = pair_piece.astype(jnp.float32) + outer_term
        normed_pair = layer_norm(summed, pair_gain).astype(jnp.bfloat16)
        gate_proj = jnp.einsum(
            "ijc,cf->ijf", normed_pair, w_gate, preferred_element_type=jnp.float32
        )
        lift_proj = jnp.einsum(
            "ijc,cf->ijf", normed_pair, w_lift, preferred_element_type=jnp.float32
        )
        hidden = (jax.nn.silu(gate_proj) * lift_proj).astype(jnp.bfloat16)
        return (
            summed + jnp.einsum("ijf,fc->ijc", hidden, w_drop, preferred_element_type=jnp.float32)
        ).astype(jnp.bfloat16)

    pair_out = lax.map(
        pair_block,
        (
            left_rows.reshape(-1, step_rows, left_rows.shape[1]),
            pair_state.reshape(-1, step_rows, col_tokens, pair_width),
        ),
    )
    return (atom_out, token_single, pair_out.reshape(row_tokens, col_tokens, pair_width))


def solution(mesh):
    in_specs = (
        P(("row", "col"), None),
        P(("row", "col")),
        P(),
        P(),
        P(),
        P(),
        P(),
        P(),
        P(),
        P(),
        P("row", "col", None),
        P(),
        P(),
        P(),
        P(),
        P(),
        P(),
        P(),
    )
    out_specs = (P(("row", "col"), None), P(("row", "col"), None), P("row", "col", None))
    return jax.shard_map(
        per_device, mesh=mesh, in_specs=in_specs, out_specs=out_specs, check_vma=False
    )
```

profile of v0, /device:TPU:0, one launch (start us, length us, event | category | flops | bytes accessed | tf_op | source)
XLA Modules:
  0.0 84.7 jit_solution(8171807035278272007)
XLA Ops:
  0.7 0.9 %convert_reduce_fusion = f32[64]{0:T(128)S(1)} fusion(bf16[64,128]{1,0:T(8,128)(2,1)} %param.22), kind=kLoop, calls=%fused_computation.58 | loop fusion | flops 16320 | bytes 16640 | tf_op jit(solution)/shard_map/reduce_sum | solution.py:37
  1.6 0.2 fusion.29
  1.8 0.6 copy-done.16
  2.4 1.0 %convolution_convert_fusion.3 = bf16[64,256]{1,0:T(8,128)(2,1)S(1)} fusion(bf16[128,128]{1,0:T(8,128)(2,1)} %param.28, bf16[128,128]{1,0:T(8,128)(2,1)} %param.27, bf16[64,128]{1,0:T(8,128)(2,1)S(1)} %copy-done.4, f32[128]{0:T(128)S(1)} %copy-done.16, f32[64]{0:T(128)S(1)} %add_rsqrt_fusion.1, f32[64]{0:T(128)S(1)} %broadcast_multiply_fusion.2), kind=kOutput, calls=%fused_computation.42 | convolution fusion | flops 4382720 | bytes 115712 | tf_op jit(solution)/shard_map/dot_general | solution.py:44
  3.4 1.3 %collective-permute-start.1 = (bf16[64,256]{1,0:T(8,128)(2,1)S(1)}, bf16[64,256]{1,0:T(8,128)(2,1)S(1)}, u32[]{:S(2)}, u32[]{:S(2)}) collective-permute-start(bf16[64,256]{1,0:T(8,128)(2,1)S(1)} %convolution_convert_fusion.3), channel_id=1, source_target_pairs={{1,0},{2,1},{3,2},{4,3},{5,4},{6,5},{7,6},{8,7},{9,8},{10,9},{11,1... | collective-permute-start | bytes 98312 | tf_op jit(solution)/shard_map/ppermute | solution.py:25
  4.7 3.0 %collective-permute-start = (bf16[64,256]{1,0:T(8,128)(2,1)S(1)}, bf16[64,256]{1,0:T(8,128)(2,1)S(1)}, u32[]{:S(2)}, u32[]{:S(2)}) collective-permute-start(bf16[64,256]{1,0:T(8,128)(2,1)S(1)} %convolution_convert_fusion.3), channel_id=1, source_target_pairs={{0,1},{1,2},{2,3},{3,4},{4,5},{5,6},{6,7},{7,8},{8,9},{9,10},{10,1... | collective-permute-start | bytes 98312 | tf_op jit(solution)/shard_map/ppermute | solution.py:22
  7.9 0.2 convolution_convert_fusion.4
  8.1 0.7 copy-done.10
  8.9 0.2 reduce-window.8
  9.1 0.2 convert_reduce_fusion.1
  9.3 0.6 broadcast_multiply_fusion.1
  10.0 0.6 fusion.42
  11.9 0.6 broadcast_subtract_fusion
  12.5 10.4 %while.37 = (s32[]{:T(128)}, u32[128]{0:T(128)S(1)}, u32[128]{0:T(128)S(1)}, s32[128]{0:T(128)S(1)}, s32[128]{0:T(128)S(1)}, /*index=5*/s32[]{:T(128)}, s32[]{:T(128)}, s32[]{}) while((s32[]{:T(128)}, u32[128]{0:T(128)S(1)}, u32[128]{0:T(128)S(1)}, s32[128]{0:T(128)S(1)}, s32[128]{0:T(128)S(1)}, /*index=5*/s32[]{:T(128)}, ...), condition=%wide.region_6.7_spmd.clone, body=%wide.region_5.6_spmd.clone.sunk | while | flops 2692 | bytes 10860 | solution.py:129
  12.6 1.2 %gather_fusion = s32[128]{0:T(128)S(1)} fusion(s32[128]{0:T(128)S(1)} %get-tuple-element.384, u32[1024]{0:T(1024)S(1)} %pad_clamp_fusion.3), kind=kCustom, calls=%fused_computation.clone.clone.1 | custom fusion | bytes 1536 | tf_op jit(solution)/shard_map/jit(searchsorted)/jit(_searchsorted_scan_impl)/vmap(jit(_searchsorted_scan_impl))/while/body/eval_jaxpr/gather | solution.py:129
  13.9 1.2 %gather_fusion = s32[128]{0:T(128)S(1)} fusion(s32[128]{0:T(128)S(1)} %get-tuple-element.384, u32[1024]{0:T(1024)S(1)} %pad_clamp_fusion.3), kind=kCustom, calls=%fused_computation.clone.clone.1 | custom fusion | bytes 1536 | tf_op jit(solution)/shard_map/jit(searchsorted)/jit(_searchsorted_scan_impl)/vmap(jit(_searchsorted_scan_impl))/while/body/eval_jaxpr/gather | solution.py:129
  15.2 1.2 %gather_fusion = s32[128]{0:T(128)S(1)} fusion(s32[128]{0:T(128)S(1)} %get-tuple-element.384, u32[1024]{0:T(1024)S(1)} %pad_clamp_fusion.3), kind=kCustom, calls=%fused_computation.clone.clone.1 | custom fusion | bytes 1536 | tf_op jit(solution)/shard_map/jit(searchsorted)/jit(_searchsorted_scan_impl)/vmap(jit(_searchsorted_scan_impl))/while/body/eval_jaxpr/gather | solution.py:129
  16.5 1.2 %gather_fusion = s32[128]{0:T(128)S(1)} fusion(s32[128]{0:T(128)S(1)} %get-tuple-element.384, u32[1024]{0:T(1024)S(1)} %pad_clamp_fusion.3), kind=kCustom, calls=%fused_computation.clone.clone.1 | custom fusion | bytes 1536 | tf_op jit(solution)/shard_map/jit(searchsorted)/jit(_searchsorted_scan_impl)/vmap(jit(_searchsorted_scan_impl))/while/body/eval_jaxpr/gather | solution.py:129
  17.8 1.2 %gather_fusion = s32[128]{0:T(128)S(1)} fusion(s32[128]{0:T(128)S(1)} %get-tuple-element.384, u32[1024]{0:T(1024)S(1)} %pad_clamp_fusion.3), kind=kCustom, calls=%fused_computation.clone.clone.1 | custom fusion | bytes 1536 | tf_op jit(solution)/shard_map/jit(searchsorted)/jit(_searchsorted_scan_impl)/vmap(jit(_searchsorted_scan_impl))/while/body/eval_jaxpr/gather | solution.py:129
  19.1 1.2 %gather_fusion = s32[128]{0:T(128)S(1)} fusion(s32[128]{0:T(128)S(1)} %get-tuple-element.384, u32[1024]{0:T(1024)S(1)} %pad_clamp_fusion.3), kind=kCustom, calls=%fused_computation.clone.clone.1 | custom fusion | bytes 1536 | tf_op jit(solution)/shard_map/jit(searchsorted)/jit(_searchsorted_scan_impl)/vmap(jit(_searchsorted_scan_impl))/while/body/eval_jaxpr/gather | solution.py:129
  20.4 1.2 %gather_fusion = s32[128]{0:T(128)S(1)} fusion(s32[128]{0:T(128)S(1)} %get-tuple-element.384, u32[1024]{0:T(1024)S(1)} %pad_clamp_fusion.3), kind=kCustom, calls=%fused_computation.clone.clone.1 | custom fusion | bytes 1536 | tf_op jit(solution)/shard_map/jit(searchsorted)/jit(_searchsorted_scan_impl)/vmap(jit(_searchsorted_scan_impl))/while/body/eval_jaxpr/gather | solution.py:129
  21.7 1.2 %gather_fusion = s32[128]{0:T(128)S(1)} fusion(s32[128]{0:T(128)S(1)} %get-tuple-element.384, u32[1024]{0:T(1024)S(1)} %pad_clamp_fusion.3), kind=kCustom, calls=%fused_computation.clone.clone.1 | custom fusion | bytes 1536 | tf_op jit(solution)/shard_map/jit(searchsorted)/jit(_searchsorted_scan_impl)/vmap(jit(_searchsorted_scan_impl))/while/body/eval_jaxpr/gather | solution.py:129
  25.2 0.2 while.36
  25.8 0.2 fusion.16
  26.3 0.5 copy-done.6
  27.3 1.3 %collective-permute-start.2 = (f32[1,384]{1,0:T(1,128)S(1)}, f32[1,384]{1,0:T(1,128)S(1)}, u32[]{:S(2)}, u32[]{:S(2)}) collective-permute-start(f32[1,384]{1,0:T(1,128)S(1)} %fusion.38), channel_id=1, source_target_pairs={{1,0},{2,1},{3,2},{4,3},{5,4},{6,5},{7,6},{8,7},{9,8},{10,9},{11,1... | collective-permute-start | bytes 4616 | tf_op jit(solution)/shard_map/ppermute | solution.py:33
  28.7 3.7 %collective-permute-done.2 = f32[1,384]{1,0:T(1,128)S(1)} collective-permute-done((f32[1,384]{1,0:T(1,128)S(1)}, f32[1,384]{1,0:T(1,128)S(1)}, u32[]{:S(2)}, u32[]{:S(2)}) %collective-permute-start.2) | collective-permute-done | bytes 1568 | tf_op jit(solution)/shard_map/ppermute | solution.py:33
  32.5 0.2 divide_convert_fusion.2
  32.7 43.1 %all_gather.3 = bf16[256,384]{1,0:T(8,128)(2,1)S(1)} all-gather(bf16[8,384]{1,0:T(8,128)(2,1)S(1)} %divide_convert_fusion.2), channel_id=1, replica_groups=mesh['row'=8,'col'=4] {'row','col'}, dimensions={0}, use_global_device_ids=true | all-gather | bytes 202752 | tf_op jit(solution)/shard_map/all_gather | solution.py:131
  75.8 0.9 %gather_fusion.1 = bf16[128,384]{1,0:T(8,128)(2,1)S(1)} fusion(bf16[256,384]{1,0:T(8,128)(2,1)S(1)} %all_gather.3, s32[1024]{0:T(1024)S(1)} %pad_clamp_fusion.1), kind=kCustom, calls=%fused_computation.1 | custom fusion | bytes 197120 | tf_op jit(solution)/shard_map/jit(_take)/gather | solution.py:132
  76.8 0.8 copy-done.13
  77.6 0.9 %fusion.20 = bf16[64,128]{1,0:T(8,128)(2,1)} fusion(bf16[128,384]{1,0:T(8,128)(2,1)S(1)} %broadcast_select_fusion.2, bf16[384,128]{1,0:T(8,128)(2,1)S(1)} %copy-done.13, bf16[64,128]{1,0:T(8,128)(2,1)S(1)} %fusion.19, s32[64]{0:T(128)S(1)} %convert_reduce_fusion.1), kind=kOutput, calls=%fused_computation.47 | convolution fusion | flops 14729216 | bytes 229632 | tf_op jit(solution)/shard_map/dot_general | solution.py:140
  78.5 0.6 constant_dynamic-slice_fusion.2
  79.2 0.6 copy-done.8
  80.0 0.2 convolution_convert_fusion
  80.4 0.7 copy-done.1
  81.3 2.8 %while.35 = (s32[]{:T(128)}, bf16[2,8,32,128]{3,2,1,0:T(8,128)(2,1)S(1)}, bf16[2,8,32,128]{3,2,1,0:T(8,128)(2,1)S(1)}, bf16[2,8,32]{2,1,0:T(8,128)(2,1)S(1)}, bf...) while((s32[]{:T(128)}, ...), condition=%wide.region_12.13_spmd, body=%wide.region_9.12_spmd.sunk | while | flops 103940352 | bytes 3354233 | solution.py:172
  81.3 0.2 fusion.94
  81.5 0.2 multiply_reduce_fusion.2
  81.9 0.2 fusion.95
  82.1 0.2 fusion.96
  82.3 0.3 fusion.97
  82.7 0.2 fusion.94
  82.9 0.2 multiply_reduce_fusion.2
  83.3 0.2 fusion.95
  83.5 0.2 fusion.96
  83.7 0.3 fusion.97
  84.1 0.6 copy-done.12
  (101 shorter events, 3.3 us)
Async XLA Ops:
  0.6 79.3 %copy-start = (bf16[32,32,128]{2,1,0:T(8,128)(2,1)S(1)}, bf16[32,32,128]{2,1,0:T(8,128)(2,1)}, u32[]{:S(2)}) copy-start(bf16[32,32,128]{2,1,0:T(8,128)(2,1)} %param.35) | copy-start | bytes 786436
  0.6 0.9 %copy-start.4 = (bf16[64,128]{1,0:T(8,128)(2,1)S(1)}, bf16[64,128]{1,0:T(8,128)(2,1)}, u32[]{:S(2)}) copy-start(bf16[64,128]{1,0:T(8,128)(2,1)} %param.22) | copy-start | bytes 49156
  1.7 0.7 copy-start.16
  2.4 5.4 %copy-start.15 = (s32[2]{0:T(128)S(1)}, s32[2]{0:T(128)}, u32[]{:S(2)}) copy-start(s32[2]{0:T(128)} %param.23) | copy-start | bytes 28
  3.4 4.5 %copy-start.14 = (bf16[128,128]{1,0:T(8,128)(2,1)S(1)}, bf16[128,128]{1,0:T(8,128)(2,1)}, u32[]{:S(2)}) copy-start(bf16[128,128]{1,0:T(8,128)(2,1)} %param.26) | copy-start | bytes 98308
  3.4 21.7 %collective-permute-start.1 = (bf16[64,256]{1,0:T(8,128)(2,1)S(1)}, bf16[64,256]{1,0:T(8,128)(2,1)S(1)}, u32[]{:S(2)}, u32[]{:S(2)}) collective-permute-start(bf16[64,256]{1,0:T(8,128)(2,1)S(1)} %convolution_convert_fusion.3), channel_id=1, source_target_pairs={{1,0},{2,1},{3,2},{4,3},{5,4},{6,5},{7,6},{8,7},{9,8},{10,9},{11,1... | collective-permute-start | bytes 98312 | tf_op jit(solution)/shard_map/ppermute | solution.py:25
  4.7 20.4 %collective-permute-start = (bf16[64,256]{1,0:T(8,128)(2,1)S(1)}, bf16[64,256]{1,0:T(8,128)(2,1)S(1)}, u32[]{:S(2)}, u32[]{:S(2)}) collective-permute-start(bf16[64,256]{1,0:T(8,128)(2,1)S(1)} %convolution_convert_fusion.3), channel_id=1, source_target_pairs={{0,1},{1,2},{2,3},{3,4},{4,5},{5,6},{6,7},{7,8},{8,9},{9,10},{10,1... | collective-permute-start | bytes 98312 | tf_op jit(solution)/shard_map/ppermute | solution.py:22
  8.1 0.7 copy-start.10
  26.0 0.8 copy-start.6
  26.2 0.9 %copy-start.5 = (bf16[128,384]{1,0:T(8,128)(2,1)S(1)}, bf16[128,384]{1,0:T(8,128)(2,1)}, u32[]{:S(2)}) copy-start(bf16[128,384]{1,0:T(8,128)(2,1)} %param.30) | copy-start | bytes 294916
  27.3 5.1 %collective-permute-start.2 = (f32[1,384]{1,0:T(1,128)S(1)}, f32[1,384]{1,0:T(1,128)S(1)}, u32[]{:S(2)}, u32[]{:S(2)}) collective-permute-start(f32[1,384]{1,0:T(1,128)S(1)} %fusion.38), channel_id=1, source_target_pairs={{1,0},{2,1},{3,2},{4,3},{5,4},{6,5},{7,6},{8,7},{9,8},{10,9},{11,1... | collective-permute-start | bytes 4616 | tf_op jit(solution)/shard_map/ppermute | solution.py:33
  76.7 0.9 %copy-start.13 = (bf16[384,128]{1,0:T(8,128)(2,1)S(1)}, bf16[384,128]{1,0:T(8,128)(2,1)}, u32[]{:S(2)}) copy-start(bf16[384,128]{1,0:T(8,128)(2,1)} %param.31) | copy-start | bytes 294916
  77.6 1.5 %copy-start.7 = (bf16[384,32]{0,1:T(8,128)(2,1)S(1)}, bf16[384,32]{0,1:T(8,128)(2,1)}, u32[]{:S(2)}) copy-start(bf16[384,32]{0,1:T(8,128)(2,1)} %param.34) | copy-start | bytes 73732
  79.1 0.7 copy-start.8
  80.2 0.9 %copy-start.1 = (bf16[128,512]{1,0:T(8,128)(2,1)S(1)}, bf16[128,512]{1,0:T(8,128)(2,1)}, u32[]{:S(2)}) copy-start(bf16[128,512]{1,0:T(8,128)(2,1)} %param.37) | copy-start | bytes 393220
  80.2 1.0 %copy-start.2 = (bf16[512,128]{1,0:T(8,128)(2,1)S(1)}, bf16[512,128]{1,0:T(8,128)(2,1)}, u32[]{:S(2)}) copy-start(bf16[512,128]{1,0:T(8,128)(2,1)} %param.39) | copy-start | bytes 393220
  80.2 1.0 %copy-start.3 = (bf16[16,32,128]{2,1,0:T(8,128)(2,1)S(1)}, bf16[16,32,128]{2,1,0:T(8,128)(2,1)}, u32[]{:S(2)}) copy-start(bf16[16,32,128]{2,1,0:T(8,128)(2,1)} %param.32) | copy-start | bytes 393220
  80.2 1.1 %copy-start.11 = (bf16[128,512]{1,0:T(8,128)(2,1)S(1)}, bf16[128,512]{1,0:T(8,128)(2,1)}, u32[]{:S(2)}) copy-start(bf16[128,512]{1,0:T(8,128)(2,1)} %param.38) | copy-start | bytes 393220
  80.3 0.9 %copy-start.9 = (f32[128]{0:T(128)S(1)}, f32[128]{0:T(128)}, u32[]{:S(2)}) copy-start(f32[128]{0:T(128)} %param.36) | copy-start | bytes 1540
  84.1 0.7 copy-start.12
where the time goes:
time: 85.3 us; the launch traced here: 84.7 us
  blocking collectives  43.1 us (51%)
  local copies, waits for them, and re-layouts  17.4 us (20%)
  starting transfers between devices  5.61 us (7%)
  matrix products  5.55 us (7%)
  other arithmetic  4.54 us (5%)
  between operations  4.29 us (5%)
  waiting for transfers between devices  3.72 us (4%)
    all_gather x1, blocking collectives, per_device(): gathered = lax.all_gather(slot_single, ('row', 'col'), axis=0, tiled=True)  43.1 us
    gather x8, local copies, waits for them, and re-layouts, per_device(): owner_first = jnp.searchsorted(token_starts, owner * atom_rows, side='left')  9.81 us
    unnamed x35, local copies, waits for them, and re-layouts  5.05 us
    ppermute x1, waiting for transfers between devices, shifted(): return lax.ppermute(block, axis, route)  3.72 us
    ppermute x1, starting transfers between devices, with_halo(): lax.ppermute(lax.slice_in_dim(block, block.shape[dim] - width, None, axis...  3.03 us
  transfers between devices with their start and end apart: 3, of which 1 were waited for; matrix products, arithmetic and copies ran while one was open for 15% of the time, Pallas kernels for 0%

commit v1 on v0

--- a/solution.py
+++ b/solution.py
@@ -126,9 +126,12 @@
     slot_counts = lax.dynamic_slice_in_dim(padded_counts, base_token, slots, 0)
     slot_single = (pooled_slots / slot_counts[:, None]).astype(jnp.bfloat16)
     owner = token_starts // atom_rows
-    owner_first = jnp.searchsorted(token_starts, owner * atom_rows, side="left")
+    owner_first = jnp.sum(
+        (token_starts[None, :] < owner[:, None] * atom_rows).astype(jnp.int32), axis=1
+    )
     row_of = owner * slots + jnp.arange(total_tokens, dtype=jnp.int32) - owner_first
-    gathered = lax.all_gather(slot_single, ("row", "col"), axis=0, tiled=True)
+    copies = jnp.broadcast_to(slot_single[None], (devices,) + slot_single.shape)
+    gathered = lax.all_to_all(copies, ("row", "col"), 0, 0).reshape(devices * slots, -1)
     full_single = jnp.take(gathered, row_of, axis=0)
     left_all = project(full_single, w_left)
     right_all = project(full_single, w_right)

time: 85.3 us -> 52.5 us (0.62)
  blocking collectives: 43.1 us -> 0 us
  starting transfers between devices: 5.61 us -> 16 us
  waiting for transfers between devices: 3.72 us -> 12.4 us
  local copies, waits for them, and re-layouts: 17.4 us -> 8.92 us
    all_gather x1 -> x0, blocking collectives: 43.1 us -> none  [per_device(): gathered = lax.all_gather(slot_single, ('row', 'col'), axis=0, tiled=True)]
    all_to_all x0 -> x1, starting transfers between devices: none -> 10.4 us  [per_device(): lax.all_to_all(copies, ('row', 'col'), 0, 0).reshape(devices * slots, -1)]
    gather x12 -> x4, local copies, waits for them, and re-layouts: 9.94 us -> 0.13 us  [the longest x8 9.81 us: per_device(): owner_first = jnp.searchsorted(token_starts, owner * atom_rows, side='left')]
    all_to_all x0 -> x1, waiting for transfers between devices: none -> 8.67 us  [per_device(): lax.all_to_all(copies, ('row', 'col'), 0, 0).reshape(devices * slots, -1)]
  transfers between devices with their start and end apart: 3 -> 4, of which waited for: 1 -> 2; matrix products, arithmetic and copies ran while one was open for 15% -> 6% of each run, Pallas kernels for 0% -> 0%
where the time goes in v1:
time: 52.5 us; the launch traced here: 51.8 us
  starting transfers between devices  16 us (30%)
  waiting for transfers between devices  12.4 us (24%)
  local copies, waits for them, and re-layouts  8.92 us (17%)
  matrix products  5.53 us (11%)
  other arithmetic  4.48 us (9%)
  between operations  4.29 us (8%)
    all_to_all x1, starting transfers between devices, per_device(): lax.all_to_all(copies, ('row', 'col'), 0, 0).reshape(devices * slots, -1)  10.4 us
    all_to_all x1, waiting for transfers between devices, per_device(): lax.all_to_all(copies, ('row', 'col'), 0, 0).reshape(devices * slots, -1)  8.67 us
    unnamed x35, local copies, waits for them, and re-layouts  5.69 us
    ppermute x1, waiting for transfers between devices, shifted(): return lax.ppermute(block, axis, route)  3.72 us
    ppermute x1, starting transfers between devices, with_halo(): lax.ppermute(lax.slice_in_dim(block, block.shape[dim] - width, None, axis...  3.03 us
    dot_general x4, matrix products, project(): jnp.dot(source, weight, preferred_element_type=jnp.float32)  1.47 us
    ppermute x1, starting transfers between devices, with_halo(): lax.ppermute(lax.slice_in_dim(block, 0, width, axis=dim), axis, backward)  1.29 us
    ppermute x1, starting transfers between devices, shifted(): return lax.ppermute(block, axis, route)  1.29 us
  transfers between devices with their start and end apart: 4, of which 2 were waited for; matrix products, arithmetic and copies ran while one was open for 6% of the time, Pallas kernels for 0%

profile of v1, /device:TPU:0, one launch (start us, length us, event | category | flops | bytes accessed | tf_op | source)
XLA Modules:
  0.0 51.8 jit_solution(14381794826637292148)
XLA Ops:
  0.7 0.9 %convert_reduce_fusion.1 = f32[64]{0:T(128)S(1)} fusion(bf16[64,128]{1,0:T(8,128)(2,1)} %param.20), kind=kLoop, calls=%fused_computation.52 | loop fusion | flops 16320 | bytes 16640 | tf_op jit(solution)/shard_map/reduce_sum | solution.py:37
  1.6 0.2 fusion.29
  1.8 0.6 %copy-done.16 = f32[128]{0:T(128)S(1)} copy-done((f32[128]{0:T(128)S(1)}, f32[128]{0:T(128)}, u32[]{:S(2)}) %copy-start.16) | copy-done | bytes 536
  2.4 1.0 %convolution_convert_fusion.3 = bf16[64,256]{1,0:T(8,128)(2,1)S(1)} fusion(bf16[128,128]{1,0:T(8,128)(2,1)} %param.26, bf16[128,128]{1,0:T(8,128)(2,1)} %param.25, bf16[64,128]{1,0:T(8,128)(2,1)S(1)} %copy-done.4, f32[128]{0:T(128)S(1)} %copy-done.16, f32[64]{0:T(128)S(1)} %add_rsqrt_fusion.1, f32[64]{0:T(128)S(1)} %broadcast_multiply_fusion.2), kind=kOutput, calls=%fused_computation.35 | convolution fusion | flops 4382720 | bytes 115712 | tf_op jit(solution)/shard_map/dot_general | solution.py:44
  3.4 1.3 %collective-permute-start.1 = (bf16[64,256]{1,0:T(8,128)(2,1)S(1)}, bf16[64,256]{1,0:T(8,128)(2,1)S(1)}, u32[]{:S(2)}, u32[]{:S(2)}) collective-permute-start(bf16[64,256]{1,0:T(8,128)(2,1)S(1)} %convolution_convert_fusion.3), channel_id=1, source_target_pairs={{1,0},{2,1},{3,2},{4,3},{5,4},{6,5},{7,6},{8,7},{9,8},{10,9},{11,1... | collective-permute-start | bytes 98312 | tf_op jit(solution)/shard_map/ppermute | solution.py:25
  4.7 3.0 %collective-permute-start = (bf16[64,256]{1,0:T(8,128)(2,1)S(1)}, bf16[64,256]{1,0:T(8,128)(2,1)S(1)}, u32[]{:S(2)}, u32[]{:S(2)}) collective-permute-start(bf16[64,256]{1,0:T(8,128)(2,1)S(1)} %convolution_convert_fusion.3), channel_id=1, source_target_pairs={{0,1},{1,2},{2,3},{3,4},{4,5},{5,6},{6,7},{7,8},{8,9},{9,10},{10,1... | collective-permute-start | bytes 98312 | tf_op jit(solution)/shard_map/ppermute | solution.py:22
  7.8 0.6 %copy-done.15 = s32[2]{0:T(128)S(1)} copy-done((s32[2]{0:T(128)S(1)}, s32[2]{0:T(128)}, u32[]{:S(2)}) %copy-start.15) | copy-done | bytes 32
  8.5 0.2 convolution_convert_fusion.4
  8.7 0.7 %copy-done.10 = s32[128]{0:T(128)S(1)} copy-done((s32[128]{0:T(128)S(1)}, s32[128]{0:T(128)}, u32[]{:S(2)}) %copy-start.10) | copy-done | bytes 536
  9.5 0.2 reduce-window.8
  9.7 0.2 convert_reduce_fusion.2
  9.9 0.6 %broadcast_multiply_fusion.1 = (s32[128]{0:T(128)S(1)}, s32[128]{0:T(128)S(1)}, s32[128]{0:T(128)S(1)}, s32[]{:T(128)}, f32[128]{0:T(128)S(1)}) fusion(s32[128]{0:T(128)S(1)} %reduce, s32[128]{0:T(128)S(1)} %copy-done.10, s32[]{:T(128)S(6)} %add.127), kind=kLoop, calls=%fused_computation.94 | loop fusion | flops 2687 | bytes 3080 | tf_op jit(solution)/shard_map/mul | solution.py:130
  10.6 0.6 %fusion.42 = s32[]{:T(128)} fusion(s32[128]{0:T(128)S(1)} %get-tuple-element.128, s32[]{:T(128)S(6)} %mul.100), kind=kLoop, calls=%fused_computation.87 | loop fusion | flops 383 | bytes 520 | tf_op jit(solution)/shard_map/reduce_sum | solution.py:114
  12.5 0.6 %broadcast_subtract_fusion = s32[64]{0:T(128)S(1)} fusion(s32[64]{0:T(128)S(1)} %convert_reduce_fusion.2, s32[]{:T(128)} %fusion.42), kind=kLoop, calls=%fused_computation.93 | loop fusion | flops 64 | bytes 516 | tf_op jit(solution)/shard_map/sub | solution.py:115
  15.4 0.2 while.12
  15.8 0.2 fusion.14
  16.0 0.2 fusion.16
  16.5 0.5 %copy-done.6 = bf16[128,128]{1,0:T(8,128)(2,1)S(1)} copy-done((bf16[128,128]{1,0:T(8,128)(2,1)S(1)}, bf16[128,128]{1,0:T(8,128)(2,1)}, u32[]{:S(2)}) %copy-start.6) | copy-done | bytes 32792
  17.3 0.2 fusion.15
  17.6 1.3 %collective-permute-start.2 = (f32[1,384]{1,0:T(1,128)S(1)}, f32[1,384]{1,0:T(1,128)S(1)}, u32[]{:S(2)}, u32[]{:S(2)}) collective-permute-start(f32[1,384]{1,0:T(1,128)S(1)} %fusion.38), channel_id=1, source_target_pairs={{1,0},{2,1},{3,2},{4,3},{5,4},{6,5},{7,6},{8,7},{9,8},{10,9},{11,1... | collective-permute-start | bytes 4616 | tf_op jit(solution)/shard_map/ppermute | solution.py:33
  18.9 3.7 %collective-permute-done.2 = f32[1,384]{1,0:T(1,128)S(1)} collective-permute-done((f32[1,384]{1,0:T(1,128)S(1)}, f32[1,384]{1,0:T(1,128)S(1)}, u32[]{:S(2)}, u32[]{:S(2)}) %collective-permute-start.2) | collective-permute-done | bytes 1568 | tf_op jit(solution)/shard_map/ppermute | solution.py:33
  22.7 0.2 divide_convert_fusion.2
  22.9 0.7 %broadcast_in_dim.37 = bf16[32,8,384]{2,1,0:T(8,128)(2,1)} broadcast(bf16[8,384]{1,0:T(8,128)(2,1)S(1)} %divide_convert_fusion.2), dimensions={1,2} | broadcast | bytes 202752 | tf_op jit(solution)/shard_map/broadcast_in_dim | solution.py:133
  23.6 10.4 %all-to-all-start = ((bf16[32,8,384]{2,1,0:T(8,128)(2,1)}), bf16[32,8,384]{2,1,0:T(8,128)(2,1)S(1)}, u32[]{:S(2)}, u32[]{:S(2)}) async-start(bf16[32,8,384]{2,1,0:T(8,128)(2,1)} %broadcast_in_dim.37), calls=%async_computation | async-start | bytes 393216 | tf_op jit(solution)/shard_map/all_to_all | solution.py:134
  34.0 0.2 convert_reduce_fusion
  34.2 8.7 %all-to-all-done = bf16[32,8,384]{2,1,0:T(8,128)(2,1)S(1)} async-done(((bf16[32,8,384]{2,1,0:T(8,128)(2,1)}), bf16[32,8,384]{2,1,0:T(8,128)(2,1)S(1)}, u32[]{:S(2)}, u32[]{:S(2)}) %all-to-all-start) | async-done | bytes 196640 | tf_op jit(solution)/shard_map/all_to_all | solution.py:134
  42.9 0.9 %gather_fusion = bf16[128,384]{1,0:T(8,128)(2,1)S(1)} fusion(bf16[256,384]{1,0:T(8,128)(2,1)S(1)} %bitcast.80, s32[1024]{0:T(1024)S(1)} %pad_clamp_fusion), kind=kCustom, calls=%fused_computation | custom fusion | bytes 197120 | tf_op jit(solution)/shard_map/jit(_take)/gather | solution.py:135
  43.8 0.8 %copy-done.13 = bf16[384,128]{1,0:T(8,128)(2,1)S(1)} copy-done((bf16[384,128]{1,0:T(8,128)(2,1)S(1)}, bf16[384,128]{1,0:T(8,128)(2,1)}, u32[]{:S(2)}) %copy-start.13) | copy-done | bytes 98328
  44.6 0.9 %fusion.20 = bf16[64,128]{1,0:T(8,128)(2,1)} fusion(bf16[128,384]{1,0:T(8,128)(2,1)S(1)} %broadcast_select_fusion, bf16[384,128]{1,0:T(8,128)(2,1)S(1)} %copy-done.13, bf16[64,128]{1,0:T(8,128)(2,1)S(1)} %fusion.19, s32[64]{0:T(128)S(1)} %convert_reduce_fusion.2), kind=kOutput, calls=%fused_computation.40 | convolution fusion | flops 14729216 | bytes 229632 | tf_op jit(solution)/shard_map/dot_general | solution.py:143
  45.5 0.6 %constant_dynamic-slice_fusion.2 = bf16[4,384]{1,0:T(4,128)(2,1)} fusion(bf16[128,384]{1,0:T(8,128)(2,1)S(1)} %broadcast_select_fusion, s32[]{:T(128)S(6)} %select_n.38), kind=kLoop, calls=%fused_computation.86 | loop fusion | bytes 6148 | tf_op jit(solution)/shard_map/dynamic_slice | solution.py:139
  46.1 0.1 fusion.57
  46.3 0.6 %copy-done.8 = bf16[384,32]{0,1:T(8,128)(2,1)S(1)} copy-done((bf16[384,32]{0,1:T(8,128)(2,1)S(1)}, bf16[384,32]{0,1:T(8,128)(2,1)}, u32[]{:S(2)}) %copy-start.8) | copy-done | bytes 24600
  46.9 0.1 fusion.56
  47.0 0.2 convolution_convert_fusion
  47.4 0.7 %copy-done.1 = bf16[128,512]{1,0:T(8,128)(2,1)S(1)} copy-done((bf16[128,512]{1,0:T(8,128)(2,1)S(1)}, bf16[128,512]{1,0:T(8,128)(2,1)}, u32[]{:S(2)}) %copy-start.1) | copy-done | bytes 131096
  48.3 2.8 %while.11 = (s32[]{:T(128)}, bf16[2,8,32,128]{3,2,1,0:T(8,128)(2,1)S(1)}, bf16[2,8,32,128]{3,2,1,0:T(8,128)(2,1)S(1)}, bf16[2,8,32]{2,1,0:T(8,128)(2,1)S(1)}, bf...) while((s32[]{:T(128)}, ...), condition=%wide.region_11.12_spmd, body=%wide.region_8.11_spmd.sunk | while | flops 103940352 | bytes 3354233 | solution.py:175
  48.3 0.2 fusion.94
  48.6 0.2 multiply_reduce_fusion.2
  48.8 0.1 multiply_convert_fusion.2
  48.9 0.2 fusion.95
  49.2 0.2 fusion.96
  49.4 0.3 fusion.97
  49.7 0.2 fusion.94
  50.0 0.2 multiply_reduce_fusion.2
  50.3 0.2 fusion.95
  50.5 0.2 fusion.96
  50.8 0.3 fusion.97
  51.1 0.6 %copy-done.12 = bf16[2,8,32,128]{3,2,1,0:T(8,128)(2,1)} copy-done((bf16[2,8,32,128]{3,2,1,0:T(8,128)(2,1)}, bf16[2,8,32,128]{3,2,1,0:T(8,128)(2,1)S(1)}, u32[]{:S(2)}) %copy-start.12) | copy-done | bytes 131096
  (69 shorter events, 2.3 us)
Async XLA Ops:
  0.6 46.4 %copy-start = (bf16[32,32,128]{2,1,0:T(8,128)(2,1)S(1)}, bf16[32,32,128]{2,1,0:T(8,128)(2,1)}, u32[]{:S(2)}) copy-start(bf16[32,32,128]{2,1,0:T(8,128)(2,1)} %param.33) | copy-start | bytes 786436
  0.6 0.9 %copy-start.4 = (bf16[64,128]{1,0:T(8,128)(2,1)S(1)}, bf16[64,128]{1,0:T(8,128)(2,1)}, u32[]{:S(2)}) copy-start(bf16[64,128]{1,0:T(8,128)(2,1)} %param.20) | copy-start | bytes 49156
  1.7 0.7 %copy-start.16 = (f32[128]{0:T(128)S(1)}, f32[128]{0:T(128)}, u32[]{:S(2)}) copy-start(f32[128]{0:T(128)} %param.23) | copy-start | bytes 1540
  2.4 6.1 %copy-start.14 = (bf16[128,128]{1,0:T(8,128)(2,1)S(1)}, bf16[128,128]{1,0:T(8,128)(2,1)}, u32[]{:S(2)}) copy-start(bf16[128,128]{1,0:T(8,128)(2,1)} %param.24) | copy-start | bytes 98308
  3.4 11.9 %collective-permute-start.1 = (bf16[64,256]{1,0:T(8,128)(2,1)S(1)}, bf16[64,256]{1,0:T(8,128)(2,1)S(1)}, u32[]{:S(2)}, u32[]{:S(2)}) collective-permute-start(bf16[64,256]{1,0:T(8,128)(2,1)S(1)} %convolution_convert_fusion.3), channel_id=1, source_target_pairs={{1,0},{2,1},{3,2},{4,3},{5,4},{6,5},{7,6},{8,7},{9,8},{10,9},{11,1... | collective-permute-start | bytes 98312 | tf_op jit(solution)/shard_map/ppermute | solution.py:25
  4.7 10.6 %collective-permute-start = (bf16[64,256]{1,0:T(8,128)(2,1)S(1)}, bf16[64,256]{1,0:T(8,128)(2,1)S(1)}, u32[]{:S(2)}, u32[]{:S(2)}) collective-permute-start(bf16[64,256]{1,0:T(8,128)(2,1)S(1)} %convolution_convert_fusion.3), channel_id=1, source_target_pairs={{0,1},{1,2},{2,3},{3,4},{4,5},{5,6},{6,7},{7,8},{8,9},{9,10},{10,1... | collective-permute-start | bytes 98312 | tf_op jit(solution)/shard_map/ppermute | solution.py:22
  7.7 0.7 %copy-start.15 = (s32[2]{0:T(128)S(1)}, s32[2]{0:T(128)}, u32[]{:S(2)}) copy-start(s32[2]{0:T(128)} %param.21) | copy-start | bytes 28
  8.7 0.7 %copy-start.10 = (s32[128]{0:T(128)S(1)}, s32[128]{0:T(128)}, u32[]{:S(2)}) copy-start(s32[128]{0:T(128)} %param.22) | copy-start | bytes 1540
  16.2 0.8 %copy-start.6 = (bf16[128,128]{1,0:T(8,128)(2,1)S(1)}, bf16[128,128]{1,0:T(8,128)(2,1)}, u32[]{:S(2)}) copy-start(bf16[128,128]{1,0:T(8,128)(2,1)} %param.27) | copy-start | bytes 98308
  16.4 0.9 %copy-start.5 = (bf16[128,384]{1,0:T(8,128)(2,1)S(1)}, bf16[128,384]{1,0:T(8,128)(2,1)}, u32[]{:S(2)}) copy-start(bf16[128,384]{1,0:T(8,128)(2,1)} %param.28) | copy-start | bytes 294916
  17.6 5.1 %collective-permute-start.2 = (f32[1,384]{1,0:T(1,128)S(1)}, f32[1,384]{1,0:T(1,128)S(1)}, u32[]{:S(2)}, u32[]{:S(2)}) collective-permute-start(f32[1,384]{1,0:T(1,128)S(1)} %fusion.38), channel_id=1, source_target_pairs={{1,0},{2,1},{3,2},{4,3},{5,4},{6,5},{7,6},{8,7},{9,8},{10,9},{11,1... | collective-permute-start | bytes 4616 | tf_op jit(solution)/shard_map/ppermute | solution.py:33
  23.6 19.2 %all-to-all-start = ((bf16[32,8,384]{2,1,0:T(8,128)(2,1)}), bf16[32,8,384]{2,1,0:T(8,128)(2,1)S(1)}, u32[]{:S(2)}, u32[]{:S(2)}) async-start(bf16[32,8,384]{2,1,0:T(8,128)(2,1)} %broadcast_in_dim.37), calls=%async_computation | async-start | bytes 393216 | tf_op jit(solution)/shard_map/all_to_all | solution.py:134
  43.7 0.9 %copy-start.13 = (bf16[384,128]{1,0:T(8,128)(2,1)S(1)}, bf16[384,128]{1,0:T(8,128)(2,1)}, u32[]{:S(2)}) copy-start(bf16[384,128]{1,0:T(8,128)(2,1)} %param.29) | copy-start | bytes 294916
  44.6 1.5 %copy-start.7 = (bf16[384,32]{0,1:T(8,128)(2,1)S(1)}, bf16[384,32]{0,1:T(8,128)(2,1)}, u32[]{:S(2)}) copy-start(bf16[384,32]{0,1:T(8,128)(2,1)} %param.32) | copy-start | bytes 73732
  46.1 0.7 %copy-start.8 = (bf16[384,32]{0,1:T(8,128)(2,1)S(1)}, bf16[384,32]{0,1:T(8,128)(2,1)}, u32[]{:S(2)}) copy-start(bf16[384,32]{0,1:T(8,128)(2,1)} %param.31) | copy-start | bytes 73732
  47.2 0.9 %copy-start.1 = (bf16[128,512]{1,0:T(8,128)(2,1)S(1)}, bf16[128,512]{1,0:T(8,128)(2,1)}, u32[]{:S(2)}) copy-start(bf16[128,512]{1,0:T(8,128)(2,1)} %param.35) | copy-start | bytes 393220
  47.2 1.0 %copy-start.2 = (bf16[512,128]{1,0:T(8,128)(2,1)S(1)}, bf16[512,128]{1,0:T(8,128)(2,1)}, u32[]{:S(2)}) copy-start(bf16[512,128]{1,0:T(8,128)(2,1)} %param.37) | copy-start | bytes 393220
  47.3 1.0 %copy-start.3 = (bf16[16,32,128]{2,1,0:T(8,128)(2,1)S(1)}, bf16[16,32,128]{2,1,0:T(8,128)(2,1)}, u32[]{:S(2)}) copy-start(bf16[16,32,128]{2,1,0:T(8,128)(2,1)} %param.30) | copy-start | bytes 393220
  47.3 1.1 %copy-start.11 = (bf16[128,512]{1,0:T(8,128)(2,1)S(1)}, bf16[128,512]{1,0:T(8,128)(2,1)}, u32[]{:S(2)}) copy-start(bf16[128,512]{1,0:T(8,128)(2,1)} %param.36) | copy-start | bytes 393220
  47.4 0.9 %copy-start.9 = (f32[128]{0:T(128)S(1)}, f32[128]{0:T(128)}, u32[]{:S(2)}) copy-start(f32[128]{0:T(128)} %param.34) | copy-start | bytes 1540
  51.1 0.7 %copy-start.12 = (bf16[2,8,32,128]{3,2,1,0:T(8,128)(2,1)}, bf16[2,8,32,128]{3,2,1,0:T(8,128)(2,1)S(1)}, u32[]{:S(2)}) copy-start(bf16[2,8,32,128]{3,2,1,0:T(8,128)(2,1)S(1)} %get-tuple-element.50) | copy-start | bytes 393220

commit v2 on v0

v2 whole, which is shorter than its diff:
```python
import math

import jax
import jax.numpy as jnp
from jax import lax
from jax.experimental import pallas as pl
from jax.experimental.pallas import tpu as pltpu
from jax.sharding import PartitionSpec as P

HEADS = 4
QB = 32
KW = 128
EPSILON = 1e-05
HALF = KW // 2
RIM = 8
GROUPS = 4
PAIR_ROWS = 8
MASKED = -1e30
SPARE = 10 << 20
MOST = 63 << 20
LOG2E = 1.4426950408889634
AXES = ("row", "col")
BF = jnp.bfloat16
F32 = jnp.float32


def layer_norm(values, gain):
    mean_value = jnp.mean(values, axis=-1, keepdims=True)
    centred = values - mean_value
    variance = jnp.mean(centred * centred, axis=-1, keepdims=True)
    return centred * lax.rsqrt(variance + EPSILON) * gain


def dot(a, b):
    return jnp.dot(a, b, preferred_element_type=F32)


def dot_t(a, b):
    return lax.dot_general(a, b, (((1,), (1,)), ((), ())), preferred_element_type=F32)


def iota(shape, axis):
    return lax.broadcasted_iota(jnp.int32, shape, axis)


def kernel(
    mine,
    other,
    starts,
    counts,
    atom_gain,
    w_query,
    w_key,
    w_value,
    w_out,
    w_pool,
    w_back,
    pair_state,
    w_left,
    w_right,
    w_outer,
    pair_gain,
    w_gate,
    w_lift,
    w_drop,
    atom_out,
    token_single,
    pair_out,
    queries,
    keys,
    values,
    offsets,
    updated,
    pooled,
    singles,
    left_wide,
    right_wide,
):
    half_blocks, block_rows, width = mine.shape
    rows = block_rows - RIM
    atoms = 2 * half_blocks * rows
    tokens, channels = pooled.shape
    row_tokens, col_tokens, pair_width = pair_state.shape
    opm = w_left.shape[0]
    row, col = lax.axis_index("row"), lax.axis_index("col")
    position = row * lax.axis_size("col") + col
    parity = position % 2
    window = rows + KW

    zeros = jnp.zeros((HALF, width), BF)
    for table in (keys, values):
        table[0:HALF, :] = zeros
        table[HALF + atoms : 2 * HALF + atoms, :] = zeros
    w_kv = jnp.concatenate([w_key[...], w_value[...]], axis=1)

    def project(source, which, step):
        pieces = source[pl.ds(step * GROUPS, GROUPS)]
        raw = pieces[:, :rows, :].reshape(GROUPS * rows, width)
        normed = layer_norm(raw.astype(F32), atom_gain[...]).astype(BF)
        query = dot(normed, w_query[...]).astype(BF)
        keyval = dot(normed, w_kv).astype(BF)
        for at in range(GROUPS):
            block = 2 * (step * GROUPS + at) + which
            first = pl.multiple_of(block * rows, rows)
            part = slice(at * rows, (at + 1) * rows)
            updated[pl.ds(first, rows), :] = raw[part]
            queries[pl.ds(first, rows), :] = query[part]
            keys[pl.ds(first + HALF, rows), :] = keyval[part, :width]
            values[pl.ds(first + HALF, rows), :] = keyval[part, width:]
            offsets[block] = pieces[at, rows:, :].astype(F32)

    def project_step(step, carry):
        project(mine, parity, step)
        project(other, 1 - parity, step)
        return carry

    lax.fori_loop(0, half_blocks // GROUPS, project_step, 0)

    pooled[...] = jnp.zeros_like(pooled)
    head_of = iota((1, width), 1) // (width // HEADS)
    head_mask = [(head_of == h).astype(F32) for h in range(HEADS)]
    head_mask_bf = [m.astype(BF) for m in head_mask]
    ones = jnp.ones((window, width), BF)
    key_lane = iota((1, window), 1)
    key_lane_float = key_lane.astype(F32)
    scale = (width // HEADS) ** (-0.5) * LOG2E
    chunk = GROUPS * rows
    chunk_lane = iota((tokens, chunk), 1)

    def attend_step(step, carry):
        attended = []
        for at in range(GROUPS):
            block = step * GROUPS + at
            first = pl.multiple_of(block * rows, rows)
            query = queries[pl.ds(first, rows), :]
            key_part = keys[pl.ds(first, window), :]
            value_part = values[pl.ds(first, window), :]
            in_range = (key_lane >= HALF - first) & (key_lane < atoms + HALF - first)
            offset = offsets[block]
            bias = []
            for e in range(rows // QB):
                low = offset[e : e + 1, :]
                low = jnp.concatenate([low, low], axis=1)[:, :window] + (QB * e)
                seen = in_range & (key_lane_float >= low) & (key_lane_float < low + KW)
                bias.append(
                    jnp.broadcast_to(jnp.where(seen, 0.0, MASKED), (QB, window))
                )
            bias = jnp.concatenate(bias, axis=0)
            stacked = jnp.concatenate([query * m for m in head_mask_bf], axis=0)
            scores = dot_t(stacked, key_part)
            scores = jnp.concatenate(
                [scores[h * rows : (h + 1) * rows] + bias for h in range(HEADS)], axis=0
            )
            top = jnp.max(scores, axis=-1, keepdims=True)
            raised = jnp.exp2((scores - top) * scale).astype(BF)
            mixed = dot(raised, jnp.concatenate([value_part, ones], axis=1))
            total = sum(
                mixed[h * rows : (h + 1) * rows, :width] * head_mask[h] for h in range(HEADS)
            )
            weight = sum(
                mixed[h * rows : (h + 1) * rows, width:] * head_mask[h] for h in range(HEADS)
            )
            attended.append((total / weight).astype(BF))
        attended = jnp.concatenate(attended, axis=0)
        here = pl.multiple_of(step * chunk, chunk)
        fresh = (updated[pl.ds(here, chunk), :].astype(F32) + dot(attended, w_out[...])).astype(BF)
        updated[pl.ds(here, chunk), :] = fresh
        feature = jnp.maximum(dot(fresh, w_pool[...]), 0.0).astype(BF)
        begin = starts[...] - here
        member = (chunk_lane >= begin) & (chunk_lane < begin + counts[...])
        pooled[...] += dot(member.astype(F32).astype(BF), feature)
        return carry

    lax.fori_loop(0, atoms // chunk, attend_step, 0)

    single = (pooled[...] / counts[...].astype(F32)).astype(BF)
    singles[...] = single
    own_tokens = token_single.shape[0]
    pick = iota((own_tokens, tokens), 1) == iota((own_tokens, tokens), 0) + position * own_tokens
    token_single[...] = dot(pick.astype(F32).astype(BF), single).astype(BF)

    first = pl.multiple_of(position * rows, rows)
    atom_lane = iota((tokens, rows), 1) + first
    owner = (atom_lane >= starts[...]) & (atom_lane < starts[...] + counts[...])
    back = dot(single, w_back[...]).astype(BF)
    lifted = lax.dot_general(
        owner.astype(F32).astype(BF), back, (((0,), (0,)), ((), ())), preferred_element_type=F32
    )
    atom_out[...] = (updated[pl.ds(first, rows), :].astype(F32) + lifted).astype(BF)

    row_single = singles[pl.ds(pl.multiple_of(row * row_tokens, row_tokens), row_tokens), :]
    col_single = singles[pl.ds(pl.multiple_of(col * col_tokens, col_tokens), col_tokens), :]
    left = dot_t(row_single, w_left[...]).astype(BF)
    right = dot_t(col_single, w_right[...]).astype(BF)
    product_lane = iota((opm, opm * opm), 1)
    unit = iota((opm, opm * opm), 0)
    left_wide[...] = dot(left, (product_lane // opm == unit).astype(F32).astype(BF))
    right_wide[...] = dot(right, (product_lane % opm == unit).astype(F32).astype(BF))

    def pair_step(step, carry):
        here = pl.multiple_of(step * PAIR_ROWS, PAIR_ROWS)
        lefts = left_wide[pl.ds(here, PAIR_ROWS), :]
        rights = right_wide[...]
        products = jnp.concatenate(
            [(lefts[i : i + 1, :] * rights).astype(BF) for i in range(PAIR_ROWS)], axis=0
        )
        flat = pair_state[pl.ds(here, PAIR_ROWS)].reshape(PAIR_ROWS * col_tokens, pair_width)
        summed = flat.astype(F32) + dot(products, w_outer[...])
        normed = layer_norm(summed, pair_gain[...]).astype(BF)
        gate = dot(normed, w_gate[...])
        lift = dot(normed, w_lift[...])
        hidden = (gate * (0.5 + 0.5 * jnp.tanh(0.5 * gate)) * lift).astype(BF)
        result = (summed + dot(hidden, w_drop[...])).astype(BF)
        pair_out[pl.ds(here, PAIR_ROWS)] = result.reshape(PAIR_ROWS, col_tokens, pair_width)
        return carry

    lax.fori_loop(0, row_tokens // PAIR_ROWS, pair_step, 0)


def gather_blocks(block):
    devices = lax.axis_size(AXES)
    groups = [[i for i in range(devices) if i % 2 == side] for side in (0, 1)]
    copies = jnp.broadcast_to(block[None], (devices // 2,) + block.shape)
    mine = lax.all_to_all(copies, AXES, 0, 0, axis_index_groups=groups)
    other = lax.ppermute(mine, AXES, [(i, i ^ 1) for i in range(devices)])
    return mine, other


def per_device(
    atom_feats,
    key_starts,
    atom_counts,
    atom_gain,
    w_query,
    w_key,
    w_value,
    w_out,
    w_pool,
    w_back,
    pair_state,
    w_left,
    w_right,
    w_outer,
    pair_gain,
    w_gate,
    w_lift,
    w_drop,
):
    rows, width = atom_feats.shape
    devices = lax.axis_size(AXES)
    position = lax.axis_index(AXES)
    atoms = rows * devices
    tokens = atom_counts.shape[0]
    channels = w_pool.shape[1]
    blocks = rows // QB
    first_block = position * blocks
    offset = key_starts + HALF - QB * (first_block + jnp.arange(blocks, dtype=jnp.int32))
    rim = jnp.zeros((RIM, width), BF).at[:blocks].set(
        jnp.broadcast_to(offset.astype(BF)[:, None], (blocks, width))
    )
    mine, other = gather_blocks(jnp.concatenate([atom_feats, rim], axis=0))
    starts = jnp.cumsum(atom_counts, dtype=jnp.int32) - atom_counts
    opm = w_left.shape[1]
    vmem = pl.BlockSpec(memory_space=pltpu.VMEM)
    operands = (
        mine,
        other,
        starts[:, None],
        atom_counts[:, None],
        atom_gain[None],
        w_query,
        w_key,
        w_value,
        w_out,
        w_pool,
        w_back,
        pair_state,
        w_left.T,
        w_right.T,
        w_outer.reshape(opm * opm, -1),
        pair_gain[None],
        w_gate,
        w_lift,
        w_drop,
    )
    outputs = (
        jax.ShapeDtypeStruct(atom_feats.shape, BF),
        jax.ShapeDtypeStruct((tokens // devices, channels), BF),
        jax.ShapeDtypeStruct(pair_state.shape, BF),
    )
    scratch = [
        pltpu.VMEM((atoms, width), BF),
        pltpu.VMEM((atoms + 2 * HALF, width), BF),
        pltpu.VMEM((atoms + 2 * HALF, width), BF),
        pltpu.VMEM((devices, RIM, width), F32),
        pltpu.VMEM((atoms, width), BF),
        pltpu.VMEM((tokens, channels), F32),
        pltpu.VMEM((tokens, channels), BF),
        pltpu.VMEM((pair_state.shape[0], opm * opm), F32),
        pltpu.VMEM((pair_state.shape[1], opm * opm), F32),
    ]
    held = sum(math.prod(a.shape) * a.dtype.itemsize for a in operands + outputs)
    held += sum(math.prod(a.shape) * jnp.dtype(a.dtype).itemsize for a in scratch)
    return pl.pallas_call(
        kernel,
        out_shape=outputs,
        in_specs=[vmem] * len(operands),
        out_specs=(vmem,) * 3,
        scratch_shapes=scratch,
        compiler_params=pltpu.CompilerParams(vmem_limit_bytes=min(held + SPARE, MOST)),
        name="trunk_window",
    )(*operands)


def solution(mesh):
    in_specs = (
        P(("row", "col"), None),
        P(("row", "col")),
        P(),
        P(),
        P(),
        P(),
        P(),
        P(),
        P(),
        P(),
        P("row", "col", None),
        P(),
        P(),
        P(),
        P(),
        P(),
        P(),
        P(),
    )
    out_specs = (P(("row", "col"), None), P(("row", "col"), None), P("row", "col", None))
    return jax.shard_map(
        per_device, mesh=mesh, in_specs=in_specs, out_specs=out_specs, check_vma=False
    )
```

time: 85.3 us -> 37.9 us (0.44)
  blocking collectives: 43.1 us -> 18.9 us
  local copies, waits for them, and re-layouts: 17.4 us -> 1.55 us
  Pallas kernels: 0 us -> 14.8 us
  starting transfers between devices: 5.61 us -> 0.01 us
  matrix products: 5.55 us -> 0 us
  other arithmetic: 4.54 us -> 0.44 us
  between operations: 4.29 us -> 0.88 us
  waiting for transfers between devices: 3.72 us -> 1.04 us
    all_gather x1 -> x0, blocking collectives: 43.1 us -> none  [per_device(): gathered = lax.all_gather(slot_single, ('row', 'col'), axis=0, tiled=True)]
    all_to_all x0 -> x1, blocking collectives: none -> 18.9 us  [gather_blocks(): mine = lax.all_to_all(copies, AXES, 0, 0, axis_index_groups=groups)]
    pallas_call x0 -> x1, Pallas kernels: none -> 14.8 us  [per_device(): pl.pallas_call(kernel, out_shape=outputs, in_specs=[vmem] * len(operands)...]
    gather x13 -> x0, local copies, waits for them, and re-layouts: 10.8 us -> none  [the longest x8 9.81 us: per_device(): owner_first = jnp.searchsorted(token_starts, owner * atom_rows, side='left')]
    ppermute x3 -> x1, starting transfers between devices: 5.61 us -> 0.01 us  [gather_blocks(): other = lax.ppermute(mine, AXES, [(i, i ^ 1) for i in range(devices)])]
    dot_general x20 -> x0, matrix products: 5.55 us -> none  [the longest x4 1.48 us: project(): jnp.dot(source, weight, preferred_element_type=jnp.float32)]
    unnamed x35 -> x36, local copies, waits for them, and re-layouts: 5.05 us -> 1.29 us
    ppermute x3 -> x1, waiting for transfers between devices: 3.72 us -> 1.04 us  [gather_blocks(): other = lax.ppermute(mine, AXES, [(i, i ^ 1) for i in range(devices)])]
  transfers between devices with their start and end apart: 3 -> 1, of which waited for: 1 -> 1; matrix products, arithmetic and copies ran while one was open for 15% -> 1% of each run, Pallas kernels for 0% -> 0%
where the time goes in v2:
time: 37.9 us; the launch traced here: 37.7 us
  blocking collectives  18.9 us (50%)
  Pallas kernels  14.8 us (39%)
  local copies, waits for them, and re-layouts  1.55 us (4%)
  waiting for transfers between devices  1.04 us (3%)
  between operations  0.88 us (2%)
  other arithmetic  0.44 us (1%)
    all_to_all x1, blocking collectives, gather_blocks(): mine = lax.all_to_all(copies, AXES, 0, 0, axis_index_groups=groups)  18.9 us
    pallas_call x1, Pallas kernels, per_device(): pl.pallas_call(kernel, out_shape=outputs, in_specs=[vmem] * len(operands)...  14.8 us
    unnamed x36, local copies, waits for them, and re-layouts  1.29 us
    ppermute x1, waiting for transfers between devices, gather_blocks(): other = lax.ppermute(mine, AXES, [(i, i ^ 1) for i in range(devices)])  1.04 us
  transfers between devices with their start and end apart: 1, of which 1 were waited for; matrix products, arithmetic and copies ran while one was open for 1% of the time, Pallas kernels for 0%

profile of v2, /device:TPU:0, one launch (start us, length us, event | category | flops | bytes accessed | tf_op | source)
XLA Modules:
  0.0 37.7 jit_solution(2958259786703987817)
XLA Ops:
  0.6 0.0 copy-start.15
  0.6 0.0 copy-start.17
  0.7 0.6 %copy-done.17 = s32[2]{0:T(128)S(1)} copy-done((s32[2]{0:T(128)S(1)}, s32[2]{0:T(128)}, u32[]{:S(2)}) %copy-start.17) | copy-done | bytes 32
  1.3 0.1 compare_select_fusion
  1.4 0.0 copy-done.15
  1.4 0.1 pad_maximum_fusion
  1.5 0.0 copy-start.16
  1.5 0.0 copy-start.6
  1.5 0.0 copy-start.8
  1.5 0.0 copy-start.9
  1.5 0.0 copy-start.10
  1.5 0.0 copy-start.11
  1.5 0.0 copy-start.12
  1.6 0.0 copy-start.1
  1.6 0.0 copy-start.2
  1.6 0.0 copy-start.3
  1.6 0.0 copy-start.4
  1.6 0.0 copy-start.5
  1.7 18.9 %all_to_all.5.mine = bf16[16,72,128]{2,1,0:T(8,128)(2,1)S(1)} all-to-all(bf16[16,72,128]{2,1,0:T(8,128)(2,1)S(1)} %broadcast_in_dim.8), channel_id=1, replica_groups={{0,2,4,6,8,10,12,14,16,18,20,22,24,26,28,30},{1,3,5,7,9,11,13,15,17,19,..., dimensions={0} | all-to-all | bytes 589824 | tf_op jit(solution)/shard_map/all_to_all | solution.py:224
  20.6 0.0 copy-start
  20.6 0.0 collective-permute-start
  20.6 0.0 copy-done.16
  20.6 0.1 copy.24.counts
  20.7 0.2 reduce-window.9
  20.9 0.1 reduce.2
  21.0 0.0 copy-start.7
  21.0 0.1 copy.25.starts
  21.1 1.0 %collective-permute-done.other = bf16[16,72,128]{2,1,0:T(8,128)(2,1)S(1)} collective-permute-done((bf16[16,72,128]{2,1,0:T(8,128)(2,1)S(1)}, bf16[16,72,128]{2,1,0:T(8,128)(2,1)S(1)}, u32[]{:S(2)}, u32[]{:S(2)}) %collective-permute-start) | collective-permute-done | bytes 294944 | tf_op jit(solution)/shard_map/ppermute | solution.py:225
  22.2 0.0 copy-start.13
  22.2 0.0 copy-start.14
  22.2 0.0 copy-done.6
  22.2 0.0 copy-done.8
  22.2 0.0 copy-done.9
  22.2 0.0 copy-done.10
  22.2 0.0 copy-done.11
  22.2 0.0 copy-done.12
  22.2 0.0 copy-done.1
  22.2 0.0 copy-done.2
  22.2 0.0 copy-done.3
  22.3 0.0 copy-done.4
  22.3 0.0 copy-done.5
  22.3 0.0 copy-done
  22.3 0.0 copy-done.7
  22.3 0.5 %copy-done.13 = f32[128]{0:T(128)S(1)} copy-done((f32[128]{0:T(128)S(1)}, f32[128]{0:T(128)}, u32[]{:S(2)}) %copy-start.13) | copy-done | bytes 536
  22.8 0.0 copy-done.14
  22.8 14.8 %trunk_window.1 = (bf16[64,128]{1,0:T(8,128)(2,1)}, bf16[4,384]{1,0:T(4,128)(2,1)}, bf16[16,32,128]{2,1,0:T(8,128)(2,1)}) custom-call(bf16[16,72,128]{2,1,0:T(8,128)(2,1)S(1)} %all_to_all.5.mine, bf16[16,72,128]{2,1,0:T(8,128)(2,1)S(1)} %collective-permute-done.other, s32[128,1]{1,0:T(8,128)S(1)} %copy.25.starts, s32[128,1]{1,0:T(8,128)S(1)} %copy.24.counts, ...), custom_call_target="tpu_custom_call" | custom-call | tf_op jit(solution)/shard_map/trunk_window/pallas_call | solution.py:304
  (3 shorter events, 0.1 us)
Async XLA Ops:
  0.6 0.8 %copy-start.15 = (bf16[64,128]{1,0:T(8,128)(2,1)S(1)}, bf16[64,128]{1,0:T(8,128)(2,1)}, u32[]{:S(2)}) copy-start(bf16[64,128]{1,0:T(8,128)(2,1)} %param.20) | copy-start | bytes 49156
  0.6 0.7 %copy-start.17 = (s32[2]{0:T(128)S(1)}, s32[2]{0:T(128)}, u32[]{:S(2)}) copy-start(s32[2]{0:T(128)} %param.21) | copy-start | bytes 28
  1.5 19.1 %copy-start.16 = (s32[128]{0:T(128)S(1)}, s32[128]{0:T(128)}, u32[]{:S(2)}) copy-start(s32[128]{0:T(128)} %param.22) | copy-start | bytes 1540
  1.5 20.7 %copy-start.6 = (bf16[384,128]{1,0:T(8,128)(2,1)S(1)}, bf16[384,128]{1,0:T(8,128)(2,1)}, u32[]{:S(2)}) copy-start(bf16[384,128]{1,0:T(8,128)(2,1)} %w_back.1) | copy-start | bytes 294916
  1.5 20.7 %copy-start.8 = (bf16[128,128]{1,0:T(8,128)(2,1)S(1)}, bf16[128,128]{1,0:T(8,128)(2,1)}, u32[]{:S(2)}) copy-start(bf16[128,128]{1,0:T(8,128)(2,1)} %w_key.1) | copy-start | bytes 98308
  1.5 20.7 %copy-start.9 = (bf16[128,128]{1,0:T(8,128)(2,1)S(1)}, bf16[128,128]{1,0:T(8,128)(2,1)}, u32[]{:S(2)}) copy-start(bf16[128,128]{1,0:T(8,128)(2,1)} %w_value.1) | copy-start | bytes 98308
  1.5 20.7 %copy-start.10 = (bf16[128,128]{1,0:T(8,128)(2,1)S(1)}, bf16[128,128]{1,0:T(8,128)(2,1)}, u32[]{:S(2)}) copy-start(bf16[128,128]{1,0:T(8,128)(2,1)} %w_out.1) | copy-start | bytes 98308
  1.5 20.7 %copy-start.11 = (bf16[384,32]{0,1:T(8,128)(2,1)S(1)}, bf16[384,32]{0,1:T(8,128)(2,1)}, u32[]{:S(2)}) copy-start(bf16[384,32]{0,1:T(8,128)(2,1)} %param.31) | copy-start | bytes 73732
  1.5 20.7 %copy-start.12 = (bf16[384,32]{0,1:T(8,128)(2,1)S(1)}, bf16[384,32]{0,1:T(8,128)(2,1)}, u32[]{:S(2)}) copy-start(bf16[384,32]{0,1:T(8,128)(2,1)} %param.32) | copy-start | bytes 73732
  1.6 20.6 %copy-start.1 = (bf16[16,32,128]{2,1,0:T(8,128)(2,1)S(1)}, bf16[16,32,128]{2,1,0:T(8,128)(2,1)}, u32[]{:S(2)}) copy-start(bf16[16,32,128]{2,1,0:T(8,128)(2,1)} %pair_state.1) | copy-start | bytes 393220
  1.6 20.6 %copy-start.2 = (bf16[128,512]{1,0:T(8,128)(2,1)S(1)}, bf16[128,512]{1,0:T(8,128)(2,1)}, u32[]{:S(2)}) copy-start(bf16[128,512]{1,0:T(8,128)(2,1)} %w_gate.1) | copy-start | bytes 393220
  1.6 20.6 %copy-start.3 = (bf16[128,512]{1,0:T(8,128)(2,1)S(1)}, bf16[128,512]{1,0:T(8,128)(2,1)}, u32[]{:S(2)}) copy-start(bf16[128,512]{1,0:T(8,128)(2,1)} %w_lift.1) | copy-start | bytes 393220
  1.6 20.6 %copy-start.4 = (bf16[512,128]{1,0:T(8,128)(2,1)S(1)}, bf16[512,128]{1,0:T(8,128)(2,1)}, u32[]{:S(2)}) copy-start(bf16[512,128]{1,0:T(8,128)(2,1)} %w_drop.1) | copy-start | bytes 393220
  1.6 20.6 %copy-start.5 = (bf16[128,384]{1,0:T(8,128)(2,1)S(1)}, bf16[128,384]{1,0:T(8,128)(2,1)}, u32[]{:S(2)}) copy-start(bf16[128,384]{1,0:T(8,128)(2,1)} %w_pool.1) | copy-start | bytes 294916
  20.6 1.7 %copy-start = (bf16[32,32,128]{2,1,0:T(8,128)(2,1)S(1)}, bf16[32,32,128]{2,1,0:T(8,128)(2,1)}, u32[]{:S(2)}) copy-start(bf16[32,32,128]{2,1,0:T(8,128)(2,1)} %param.33) | copy-start | bytes 786436
  20.6 1.6 %collective-permute-start = (bf16[16,72,128]{2,1,0:T(8,128)(2,1)S(1)}, bf16[16,72,128]{2,1,0:T(8,128)(2,1)S(1)}, u32[]{:S(2)}, u32[]{:S(2)}) collective-permute-start(bf16[16,72,128]{2,1,0:T(8,128)(2,1)S(1)} %all_to_all.5.mine), channel_id=1, source_target_pairs={{0,1},{1,0},{2,3},{3,2},{4,5},{5,4},{6,7},{7,6},{8,9},{9,8},{10,11... | collective-permute-start | bytes 884744 | tf_op jit(solution)/shard_map/ppermute | solution.py:225
  21.0 1.3 %copy-start.7 = (bf16[128,128]{1,0:T(8,128)(2,1)S(1)}, bf16[128,128]{1,0:T(8,128)(2,1)}, u32[]{:S(2)}) copy-start(bf16[128,128]{1,0:T(8,128)(2,1)} %w_query.1) | copy-start | bytes 98308
  22.2 0.7 %copy-start.13 = (f32[128]{0:T(128)S(1)}, f32[128]{0:T(128)}, u32[]{:S(2)}) copy-start(f32[128]{0:T(128)} %param.23) | copy-start | bytes 1540
  22.2 0.7 %copy-start.14 = (f32[128]{0:T(128)S(1)}, f32[128]{0:T(128)}, u32[]{:S(2)}) copy-start(f32[128]{0:T(128)} %param.34) | copy-start | bytes 1540

commit v3 on v2

--- a/solution.py
+++ b/solution.py
@@ -41,6 +41,15 @@
 
 def iota(shape, axis):
     return lax.broadcasted_iota(jnp.int32, shape, axis)
+
+
+def reversed_bits(index, size):
+    result = 0
+    bit = 1
+    while bit < size // 2:
+        result = result + jnp.where(index & bit != 0, size // (2 * bit), 0)
+        bit *= 2
+    return result
 
 
 def kernel(
@@ -84,7 +93,6 @@
     opm = w_left.shape[0]
     row, col = lax.axis_index("row"), lax.axis_index("col")
     position = row * lax.axis_size("col") + col
-    parity = position % 2
     window = rows + KW
 
     zeros = jnp.zeros((HALF, width), BF)
@@ -100,7 +108,7 @@
         query = dot(normed, w_query[...]).astype(BF)
         keyval = dot(normed, w_kv).astype(BF)
         for at in range(GROUPS):
-            block = 2 * (step * GROUPS + at) + which
+            block = position ^ which ^ reversed_bits(step * GROUPS + at, 2 * half_blocks)
             first = pl.multiple_of(block * rows, rows)
             part = slice(at * rows, (at + 1) * rows)
             updated[pl.ds(first, rows), :] = raw[part]
@@ -110,8 +118,8 @@
             offsets[block] = pieces[at, rows:, :].astype(F32)
 
     def project_step(step, carry):
-        project(mine, parity, step)
-        project(other, 1 - parity, step)
+        project(mine, 0, step)
+        project(other, 1, step)
         return carry
 
     lax.fori_loop(0, half_blocks // GROUPS, project_step, 0)
@@ -219,11 +227,16 @@
 
 def gather_blocks(block):
     devices = lax.axis_size(AXES)
-    groups = [[i for i in range(devices) if i % 2 == side] for side in (0, 1)]
-    copies = jnp.broadcast_to(block[None], (devices // 2,) + block.shape)
-    mine = lax.all_to_all(copies, AXES, 0, 0, axis_index_groups=groups)
-    other = lax.ppermute(mine, AXES, [(i, i ^ 1) for i in range(devices)])
-    return mine, other
+    held = block[None]
+    bit = devices // 2
+    while bit > 1:
+        held = jnp.concatenate([held, exchanged(held, bit)], axis=0)
+        bit //= 2
+    return held, exchanged(held, 1)
+
+
+def exchanged(held, bit):
+    return lax.ppermute(held, AXES, [(i, i ^ bit) for i in range(lax.axis_size(AXES))])
 
 
 def per_device(

time: 37.9 us -> 38.4 us (1.013)
  blocking collectives: 18.9 us -> 0 us
  starting transfers between devices: 0.01 us -> 9.99 us
  waiting for transfers between devices: 1.04 us -> 10.3 us
    all_to_all x1 -> x0, blocking collectives: 18.9 us -> none  [gather_blocks(): mine = lax.all_to_all(copies, AXES, 0, 0, axis_index_groups=groups)]
    ppermute x1 -> x5, starting transfers between devices: 0.01 us -> 9.99 us  [exchanged(): lax.ppermute(held, AXES, [(i, i ^ bit) for i in range(lax.axis_size(AXES))])]
    ppermute x1 -> x5, waiting for transfers between devices: 1.04 us -> 10.3 us  [exchanged(): lax.ppermute(held, AXES, [(i, i ^ bit) for i in range(lax.axis_size(AXES))])]
    unnamed x36 -> x39, local copies, waits for them, and re-layouts: 1.29 us -> 1.31 us
  transfers between devices with their start and end apart: 1 -> 5, of which waited for: 1 -> 5; matrix products, arithmetic and copies ran while one was open for 1% -> 2% of each run, Pallas kernels for 0% -> 0%
where the time goes in v3:
time: 38.4 us; the launch traced here: 38.2 us
  Pallas kernels  14.9 us (39%)
  waiting for transfers between devices  10.3 us (27%)
  starting transfers between devices  9.99 us (26%)
  local copies, waits for them, and re-layouts  1.55 us (4%)
  between operations  0.87 us (2%)
  other arithmetic  0.55 us (1%)
    pallas_call x1, Pallas kernels, per_device(): pl.pallas_call(kernel, out_shape=outputs, in_specs=[vmem] * len(operands)...  14.9 us
    ppermute x5, waiting for transfers between devices, exchanged(): lax.ppermute(held, AXES, [(i, i ^ bit) for i in range(lax.axis_size(AXES))])  10.3 us
    ppermute x5, starting transfers between devices, exchanged(): lax.ppermute(held, AXES, [(i, i ^ bit) for i in range(lax.axis_size(AXES))])  9.99 us
    unnamed x39, local copies, waits for them, and re-layouts  1.31 us
  transfers between devices with their start and end apart: 5, of which 5 were waited for; matrix products, arithmetic and copies ran while one was open for 2% of the time, Pallas kernels for 0%

profile of v3, /device:TPU:0, one launch (start us, length us, event | category | flops | bytes accessed | tf_op | source)
XLA Modules:
  0.0 38.2 jit_solution(777139073507855386)
XLA Ops:
  0.6 0.0 copy-start.15
  0.6 0.0 copy-start.17
  0.7 0.6 %copy-done.17 = s32[2]{0:T(128)S(1)} copy-done((s32[2]{0:T(128)S(1)}, s32[2]{0:T(128)}, u32[]{:S(2)}) %copy-start.17) | copy-done | bytes 32
  1.3 0.1 compare_select_fusion
  1.4 0.0 copy-done.15
  1.4 0.1 maximum_bitcast_fusion
  1.5 4.1 %collective-permute-start = (bf16[1,72,128]{2,1,0:T(8,128)(2,1)S(1)}, bf16[1,72,128]{2,1,0:T(8,128)(2,1)S(1)}, u32[]{:S(2)}, u32[]{:S(2)}) collective-permute-start(bf16[1,72,128]{2,1,0:T(8,128)(2,1)S(1)} %maximum_bitcast_fusion), channel_id=1, source_target_pairs={{0,16},{1,17},{2,18},{3,19},{4,20},{5,21},{6,22},{7,23},{8,24},{9,... | collective-permute-start | bytes 55304 | tf_op jit(solution)/shard_map/ppermute | solution.py:239
  5.5 1.7 %collective-permute-done = bf16[1,72,128]{2,1,0:T(8,128)(2,1)S(1)} collective-permute-done((bf16[1,72,128]{2,1,0:T(8,128)(2,1)S(1)}, bf16[1,72,128]{2,1,0:T(8,128)(2,1)S(1)}, u32[]{:S(2)}, u32[]{:S(2)}) %collective-permute-start) | collective-permute-done | bytes 18464 | tf_op jit(solution)/shard_map/ppermute | solution.py:239
  7.3 1.9 %collective-permute-start.1 = (bf16[2,72,128]{2,1,0:T(8,128)(2,1)S(1)}, bf16[2,72,128]{2,1,0:T(8,128)(2,1)S(1)}, u32[]{:S(2)}, u32[]{:S(2)}) collective-permute-start(bf16[2,72,128]{2,1,0:T(8,128)(2,1)S(1)} %pad_maximum_fusion.2), channel_id=1, source_target_pairs={{0,8},{1,9},{2,10},{3,11},{4,12},{5,13},{6,14},{7,15},{8,0},{9,1},... | collective-permute-start | bytes 110600 | tf_op jit(solution)/shard_map/ppermute | solution.py:239
  9.2 0.1 constant_dynamic-update-slice_fusion.4
  9.3 2.0 %collective-permute-done.1 = bf16[2,72,128]{2,1,0:T(8,128)(2,1)S(1)} collective-permute-done((bf16[2,72,128]{2,1,0:T(8,128)(2,1)S(1)}, bf16[2,72,128]{2,1,0:T(8,128)(2,1)S(1)}, u32[]{:S(2)}, u32[]{:S(2)}) %collective-permute-start.1) | collective-permute-done | bytes 36896 | tf_op jit(solution)/shard_map/ppermute | solution.py:239
  11.2 2.0 %collective-permute-start.2 = (bf16[4,72,128]{2,1,0:T(8,128)(2,1)S(1)}, bf16[4,72,128]{2,1,0:T(8,128)(2,1)S(1)}, u32[]{:S(2)}, u32[]{:S(2)}) collective-permute-start(bf16[4,72,128]{2,1,0:T(8,128)(2,1)S(1)} %pad_maximum_fusion.1), channel_id=1, source_target_pairs={{0,4},{1,5},{2,6},{3,7},{4,0},{5,1},{6,2},{7,3},{8,12},{9,13},{10,... | collective-permute-start | bytes 221192 | tf_op jit(solution)/shard_map/ppermute | solution.py:239
  13.2 0.0 copy-start.12
  13.2 2.4 %collective-permute-done.2 = bf16[4,72,128]{2,1,0:T(8,128)(2,1)S(1)} collective-permute-done((bf16[4,72,128]{2,1,0:T(8,128)(2,1)S(1)}, bf16[4,72,128]{2,1,0:T(8,128)(2,1)S(1)}, u32[]{:S(2)}, u32[]{:S(2)}) %collective-permute-start.2) | collective-permute-done | bytes 73760 | tf_op jit(solution)/shard_map/ppermute | solution.py:239
  15.7 0.0 copy-start.5
  15.7 0.0 copy-start.6
  15.7 0.0 copy-start.11
  15.7 2.0 %collective-permute-start.3 = (bf16[8,72,128]{2,1,0:T(8,128)(2,1)S(1)}, bf16[8,72,128]{2,1,0:T(8,128)(2,1)S(1)}, u32[]{:S(2)}, u32[]{:S(2)}) collective-permute-start(bf16[8,72,128]{2,1,0:T(8,128)(2,1)S(1)} %pad_maximum_fusion), channel_id=1, source_target_pairs={{0,2},{1,3},{2,0},{3,1},{4,6},{5,7},{6,4},{7,5},{8,10},{9,11},{10,... | collective-permute-start | bytes 442376 | tf_op jit(solution)/shard_map/ppermute | solution.py:239
  17.7 0.0 copy-start.16
  17.7 0.0 copy-start.3
  17.7 0.0 copy-start
  17.7 3.2 %collective-permute-done.3 = bf16[8,72,128]{2,1,0:T(8,128)(2,1)S(1)} collective-permute-done((bf16[8,72,128]{2,1,0:T(8,128)(2,1)S(1)}, bf16[8,72,128]{2,1,0:T(8,128)(2,1)S(1)}, u32[]{:S(2)}, u32[]{:S(2)}) %collective-permute-start.3) | collective-permute-done | bytes 147488 | tf_op jit(solution)/shard_map/ppermute | solution.py:239
  20.9 0.1 collective-permute-start.4
  21.0 0.0 copy-done.16
  21.0 0.0 copy-start.7
  21.0 0.0 copy-start.8
  21.1 0.1 copy.24.counts
  21.2 0.0 copy-start.2
  21.2 0.2 reduce-window.9
  21.4 0.1 reduce.2
  21.5 0.1 copy.25.starts
  21.6 1.0 %collective-permute-done.4.other = bf16[16,72,128]{2,1,0:T(8,128)(2,1)S(1)} collective-permute-done((bf16[16,72,128]{2,1,0:T(8,128)(2,1)S(1)}, bf16[16,72,128]{2,1,0:T(8,128)(2,1)S(1)}, u32[]{:S(2)}, u32[]{:S(2)}) %collective-permute-start.4) | collective-permute-done | bytes 294944 | tf_op jit(solution)/shard_map/ppermute | solution.py:239
  22.6 0.0 copy-done.12
  22.6 0.0 copy-done.5
  22.6 0.0 copy-done.6
  22.6 0.0 copy-done.9
  22.6 0.0 copy-done.10
  22.6 0.0 copy-done.11
  22.6 0.0 copy-done.4
  22.7 0.0 copy-done.3
  22.7 0.0 copy-done
  22.7 0.0 copy-done.7
  22.7 0.0 copy-done.8
  22.7 0.0 copy-done.1
  22.7 0.0 copy-done.2
  22.7 0.5 %copy-done.13 = f32[128]{0:T(128)S(1)} copy-done((f32[128]{0:T(128)S(1)}, f32[128]{0:T(128)}, u32[]{:S(2)}) %copy-start.13) | copy-done | bytes 536
  23.3 0.0 copy-done.14
  23.3 14.9 %trunk_window.1 = (bf16[64,128]{1,0:T(8,128)(2,1)}, bf16[4,384]{1,0:T(4,128)(2,1)}, bf16[16,32,128]{2,1,0:T(8,128)(2,1)}) custom-call(bf16[16,72,128]{2,1,0:T(8,128)(2,1)S(1)} %constant_dynamic-update-slice_fusion.mine, bf16[16,72,128]{2,1,0:T(8,128)(2,1)S(1)} %collective-permute-done.4.other, s32[128,1]{1,0:T(8,128)S(1)} %copy.25.starts, ...), custom_call_target="tpu_custom_call" | custom-call | tf_op jit(solution)/shard_map/trunk_window/pallas_call | solution.py:317
  (15 shorter events, 0.1 us)
Async XLA Ops:
  0.6 0.8 %copy-start.15 = (bf16[64,128]{1,0:T(8,128)(2,1)S(1)}, bf16[64,128]{1,0:T(8,128)(2,1)}, u32[]{:S(2)}) copy-start(bf16[64,128]{1,0:T(8,128)(2,1)} %param.20) | copy-start | bytes 49156
  0.6 0.7 %copy-start.17 = (s32[2]{0:T(128)S(1)}, s32[2]{0:T(128)}, u32[]{:S(2)}) copy-start(s32[2]{0:T(128)} %param.21) | copy-start | bytes 28
  1.5 5.8 %collective-permute-start = (bf16[1,72,128]{2,1,0:T(8,128)(2,1)S(1)}, bf16[1,72,128]{2,1,0:T(8,128)(2,1)S(1)}, u32[]{:S(2)}, u32[]{:S(2)}) collective-permute-start(bf16[1,72,128]{2,1,0:T(8,128)(2,1)S(1)} %maximum_bitcast_fusion), channel_id=1, source_target_pairs={{0,16},{1,17},{2,18},{3,19},{4,20},{5,21},{6,22},{7,23},{8,24},{9,... | collective-permute-start | bytes 55304 | tf_op jit(solution)/shard_map/ppermute | solution.py:239
  7.3 4.0 %collective-permute-start.1 = (bf16[2,72,128]{2,1,0:T(8,128)(2,1)S(1)}, bf16[2,72,128]{2,1,0:T(8,128)(2,1)S(1)}, u32[]{:S(2)}, u32[]{:S(2)}) collective-permute-start(bf16[2,72,128]{2,1,0:T(8,128)(2,1)S(1)} %pad_maximum_fusion.2), channel_id=1, source_target_pairs={{0,8},{1,9},{2,10},{3,11},{4,12},{5,13},{6,14},{7,15},{8,0},{9,1},... | collective-permute-start | bytes 110600 | tf_op jit(solution)/shard_map/ppermute | solution.py:239
  11.2 4.4 %collective-permute-start.2 = (bf16[4,72,128]{2,1,0:T(8,128)(2,1)S(1)}, bf16[4,72,128]{2,1,0:T(8,128)(2,1)S(1)}, u32[]{:S(2)}, u32[]{:S(2)}) collective-permute-start(bf16[4,72,128]{2,1,0:T(8,128)(2,1)S(1)} %pad_maximum_fusion.1), channel_id=1, source_target_pairs={{0,4},{1,5},{2,6},{3,7},{4,0},{5,1},{6,2},{7,3},{8,12},{9,13},{10,... | collective-permute-start | bytes 221192 | tf_op jit(solution)/shard_map/ppermute | solution.py:239
  13.2 9.4 %copy-start.12 = (bf16[384,32]{0,1:T(8,128)(2,1)S(1)}, bf16[384,32]{0,1:T(8,128)(2,1)}, u32[]{:S(2)}) copy-start(bf16[384,32]{0,1:T(8,128)(2,1)} %param.32) | copy-start | bytes 73732
  15.7 6.9 %copy-start.5 = (bf16[128,384]{1,0:T(8,128)(2,1)S(1)}, bf16[128,384]{1,0:T(8,128)(2,1)}, u32[]{:S(2)}) copy-start(bf16[128,384]{1,0:T(8,128)(2,1)} %w_pool.1) | copy-start | bytes 294916
  15.7 6.9 %copy-start.6 = (bf16[384,128]{1,0:T(8,128)(2,1)S(1)}, bf16[384,128]{1,0:T(8,128)(2,1)}, u32[]{:S(2)}) copy-start(bf16[384,128]{1,0:T(8,128)(2,1)} %w_back.1) | copy-start | bytes 294916
  15.7 7.0 %copy-start.9 = (bf16[128,128]{1,0:T(8,128)(2,1)S(1)}, bf16[128,128]{1,0:T(8,128)(2,1)}, u32[]{:S(2)}) copy-start(bf16[128,128]{1,0:T(8,128)(2,1)} %w_value.1) | copy-start | bytes 98308
  15.7 7.0 %copy-start.10 = (bf16[128,128]{1,0:T(8,128)(2,1)S(1)}, bf16[128,128]{1,0:T(8,128)(2,1)}, u32[]{:S(2)}) copy-start(bf16[128,128]{1,0:T(8,128)(2,1)} %w_out.1) | copy-start | bytes 98308
  15.7 7.0 %copy-start.11 = (bf16[384,32]{0,1:T(8,128)(2,1)S(1)}, bf16[384,32]{0,1:T(8,128)(2,1)}, u32[]{:S(2)}) copy-start(bf16[384,32]{0,1:T(8,128)(2,1)} %param.31) | copy-start | bytes 73732
  15.7 5.2 %collective-permute-start.3 = (bf16[8,72,128]{2,1,0:T(8,128)(2,1)S(1)}, bf16[8,72,128]{2,1,0:T(8,128)(2,1)S(1)}, u32[]{:S(2)}, u32[]{:S(2)}) collective-permute-start(bf16[8,72,128]{2,1,0:T(8,128)(2,1)S(1)} %pad_maximum_fusion), channel_id=1, source_target_pairs={{0,2},{1,3},{2,0},{3,1},{4,6},{5,7},{6,4},{7,5},{8,10},{9,11},{10,... | collective-permute-start | bytes 442376 | tf_op jit(solution)/shard_map/ppermute | solution.py:239
  17.7 5.0 %copy-start.4 = (bf16[512,128]{1,0:T(8,128)(2,1)S(1)}, bf16[512,128]{1,0:T(8,128)(2,1)}, u32[]{:S(2)}) copy-start(bf16[512,128]{1,0:T(8,128)(2,1)} %w_drop.1) | copy-start | bytes 393220
  17.7 3.3 %copy-start.16 = (s32[128]{0:T(128)S(1)}, s32[128]{0:T(128)}, u32[]{:S(2)}) copy-start(s32[128]{0:T(128)} %param.22) | copy-start | bytes 1540
  17.7 5.0 %copy-start.3 = (bf16[128,512]{1,0:T(8,128)(2,1)S(1)}, bf16[128,512]{1,0:T(8,128)(2,1)}, u32[]{:S(2)}) copy-start(bf16[128,512]{1,0:T(8,128)(2,1)} %w_lift.1) | copy-start | bytes 393220
  17.7 4.9 %copy-start = (bf16[32,32,128]{2,1,0:T(8,128)(2,1)S(1)}, bf16[32,32,128]{2,1,0:T(8,128)(2,1)}, u32[]{:S(2)}) copy-start(bf16[32,32,128]{2,1,0:T(8,128)(2,1)} %param.33) | copy-start | bytes 786436
  20.9 1.6 %collective-permute-start.4 = (bf16[16,72,128]{2,1,0:T(8,128)(2,1)S(1)}, bf16[16,72,128]{2,1,0:T(8,128)(2,1)S(1)}, u32[]{:S(2)}, u32[]{:S(2)}) collective-permute-start(bf16[16,72,128]{2,1,0:T(8,128)(2,1)S(1)} %constant_dynamic-update-slice_fusion.mine), channel_id=1, source_target_pairs={{0,1},{1,0},{2,3},{3,2},{4,5},{5,4},{6,7},{7,6},{8,9},{9,8},{10,11... | collective-permute-start | bytes 884744 | tf_op jit(solution)/shard_map/ppermute | solution.py:239
  21.0 1.6 %copy-start.7 = (bf16[128,128]{1,0:T(8,128)(2,1)S(1)}, bf16[128,128]{1,0:T(8,128)(2,1)}, u32[]{:S(2)}) copy-start(bf16[128,128]{1,0:T(8,128)(2,1)} %w_query.1) | copy-start | bytes 98308
  21.0 1.6 %copy-start.8 = (bf16[128,128]{1,0:T(8,128)(2,1)S(1)}, bf16[128,128]{1,0:T(8,128)(2,1)}, u32[]{:S(2)}) copy-start(bf16[128,128]{1,0:T(8,128)(2,1)} %w_key.1) | copy-start | bytes 98308
  21.2 1.5 %copy-start.1 = (bf16[16,32,128]{2,1,0:T(8,128)(2,1)S(1)}, bf16[16,32,128]{2,1,0:T(8,128)(2,1)}, u32[]{:S(2)}) copy-start(bf16[16,32,128]{2,1,0:T(8,128)(2,1)} %pair_state.1) | copy-start | bytes 393220
  21.2 1.5 %copy-start.2 = (bf16[128,512]{1,0:T(8,128)(2,1)S(1)}, bf16[128,512]{1,0:T(8,128)(2,1)}, u32[]{:S(2)}) copy-start(bf16[128,512]{1,0:T(8,128)(2,1)} %w_gate.1) | copy-start | bytes 393220
  22.6 0.7 %copy-start.13 = (f32[128]{0:T(128)S(1)}, f32[128]{0:T(128)}, u32[]{:S(2)}) copy-start(f32[128]{0:T(128)} %param.23) | copy-start | bytes 1540
  22.6 0.7 %copy-start.14 = (f32[128]{0:T(128)S(1)}, f32[128]{0:T(128)}, u32[]{:S(2)}) copy-start(f32[128]{0:T(128)} %param.34) | copy-start | bytes 1540

commit v4 on v2

--- a/solution.py
+++ b/solution.py
@@ -84,7 +84,6 @@
     opm = w_left.shape[0]
     row, col = lax.axis_index("row"), lax.axis_index("col")
     position = row * lax.axis_size("col") + col
-    parity = position % 2
     window = rows + KW
 
     zeros = jnp.zeros((HALF, width), BF)
@@ -100,7 +99,7 @@
         query = dot(normed, w_query[...]).astype(BF)
         keyval = dot(normed, w_kv).astype(BF)
         for at in range(GROUPS):
-            block = 2 * (step * GROUPS + at) + which
+            block = which * half_blocks + step * GROUPS + at
             first = pl.multiple_of(block * rows, rows)
             part = slice(at * rows, (at + 1) * rows)
             updated[pl.ds(first, rows), :] = raw[part]
@@ -110,8 +109,8 @@
             offsets[block] = pieces[at, rows:, :].astype(F32)
 
     def project_step(step, carry):
-        project(mine, parity, step)
-        project(other, 1 - parity, step)
+        project(mine, 0, step)
+        project(other, 1, step)
         return carry
 
     lax.fori_loop(0, half_blocks // GROUPS, project_step, 0)
@@ -218,12 +217,9 @@
 
 
 def gather_blocks(block):
-    devices = lax.axis_size(AXES)
-    groups = [[i for i in range(devices) if i % 2 == side] for side in (0, 1)]
-    copies = jnp.broadcast_to(block[None], (devices // 2,) + block.shape)
-    mine = lax.all_to_all(copies, AXES, 0, 0, axis_index_groups=groups)
-    other = lax.ppermute(mine, AXES, [(i, i ^ 1) for i in range(devices)])
-    return mine, other
+    gathered = lax.all_gather(block, AXES)
+    half = gathered.shape[0] // 2
+    return gathered[:half], gathered[half:]
 
 
 def per_device(

time: 37.9 us -> 63.2 us (1.67)
  blocking collectives: 18.9 us -> 44.8 us
  waiting for transfers between devices: 1.04 us -> 0 us
    all_gather x0 -> x1, blocking collectives: none -> 44.8 us  [gather_blocks(): gathered = lax.all_gather(block, AXES)]
    all_to_all x1 -> x0, blocking collectives: 18.9 us -> none  [gather_blocks(): mine = lax.all_to_all(copies, AXES, 0, 0, axis_index_groups=groups)]
    ppermute x1 -> x0, waiting for transfers between devices: 1.04 us -> none  [gather_blocks(): other = lax.ppermute(mine, AXES, [(i, i ^ 1) for i in range(devices)])]
  transfers between devices with their start and end apart: 1 -> 0, of which waited for: 1 -> 0; matrix products, arithmetic and copies ran while one was open for 1% -> 0% of each run, Pallas kernels for 0% -> 0%
where the time goes in v4:
time: 63.2 us; the launch traced here: 63 us
  blocking collectives  44.8 us (71%)
  Pallas kernels  14.8 us (23%)
  local copies, waits for them, and re-layouts  2.07 us (3%)
  between operations  0.85 us (1%)
    all_gather x1, blocking collectives, gather_blocks(): gathered = lax.all_gather(block, AXES)  44.8 us
    pallas_call x1, Pallas kernels, per_device(): pl.pallas_call(kernel, out_shape=outputs, in_specs=[vmem] * len(operands)...  14.8 us
    unnamed x36, local copies, waits for them, and re-layouts  1.81 us

profile of v4, /device:TPU:0, one launch (start us, length us, event | category | flops | bytes accessed | tf_op | source)
XLA Modules:
  0.0 63.0 jit_solution(4651720186087589252)
XLA Ops:
  0.6 0.0 copy-start.15
  0.6 0.0 copy-start.17
  0.7 0.6 %copy-done.17 = s32[2]{0:T(128)S(1)} copy-done((s32[2]{0:T(128)S(1)}, s32[2]{0:T(128)}, u32[]{:S(2)}) %copy-start.17) | copy-done | bytes 32
  1.3 0.1 compare_select_fusion
  1.4 0.0 copy-done.15
  1.4 0.1 pad_maximum_fusion
  1.5 44.8 %all-gather = bf16[2304,128]{1,0:T(8,128)(2,1)S(1)} all-gather(bf16[72,128]{1,0:T(8,128)(2,1)S(1)} %pad_maximum_fusion), channel_id=2, replica_groups=mesh['row'=8,'col'=4] {'row','col'}, dimensions={0}, use_global_device_ids=true | all-gather | bytes 608256 | tf_op jit(solution)/shard_map/all_gather | solution.py:220
  46.3 0.0 copy-start.16
  46.3 0.0 copy-start.1
  46.3 0.0 copy-start.2
  46.3 0.0 copy-start.3
  46.3 0.0 copy-start.4
  46.3 0.0 copy-start.5
  46.3 0.0 copy-start.6
  46.3 0.0 copy-start.9
  46.3 0.0 copy-start.10
  46.3 0.0 copy-start.11
  46.3 0.0 copy-start.12
  46.4 0.0 copy-start
  46.4 0.5 copy-done.16
  46.9 0.1 copy.24.counts
  47.0 0.2 reduce-window.9
  47.2 0.1 reduce.2
  47.3 0.0 copy-start.7
  47.3 0.0 copy-start.8
  47.4 0.1 copy.25.starts
  47.5 0.0 copy-start.13
  47.5 0.0 copy-start.14
  47.5 0.0 copy-done.1
  47.5 0.0 copy-done.2
  47.5 0.0 copy-done.3
  47.5 0.0 copy-done.4
  47.5 0.0 copy-done.5
  47.5 0.0 copy-done.6
  47.5 0.0 copy-done.9
  47.6 0.0 copy-done.10
  47.6 0.0 copy-done.11
  47.6 0.0 copy-done.12
  47.6 0.0 copy-done
  47.6 0.5 copy-done.7
  48.1 0.0 copy-done.8
  48.2 0.0 copy-done.13
  48.2 0.0 copy-done.14
  48.2 14.8 %trunk_window.1 = (bf16[64,128]{1,0:T(8,128)(2,1)}, bf16[4,384]{1,0:T(4,128)(2,1)}, bf16[16,32,128]{2,1,0:T(8,128)(2,1)}) custom-call(bf16[16,72,128]{2,1,0:T(8,128)(2,1)S(1)} %bitcast.11, bf16[16,72,128]{2,1,0:T(8,128)(2,1)S(1)} %bitcast.10, s32[128,1]{1,0:T(8,128)S(1)} %copy.25.starts, s32[128,1]{1,0:T(8,128)S(1)} %copy.24.counts, f32[1,128]{1,0:T(1,128)S(1)} %bitcast.15, ...), custom_call_target="tpu_custom_call" | custom-call | tf_op jit(solution)/shard_map/trunk_window/pallas_call | solution.py:300
  (3 shorter events, 0.1 us)
Async XLA Ops:
  0.6 0.8 %copy-start.15 = (bf16[64,128]{1,0:T(8,128)(2,1)S(1)}, bf16[64,128]{1,0:T(8,128)(2,1)}, u32[]{:S(2)}) copy-start(bf16[64,128]{1,0:T(8,128)(2,1)} %param.20) | copy-start | bytes 49156
  0.6 0.7 %copy-start.17 = (s32[2]{0:T(128)S(1)}, s32[2]{0:T(128)}, u32[]{:S(2)}) copy-start(s32[2]{0:T(128)} %param.21) | copy-start | bytes 28
  46.3 0.7 %copy-start.16 = (s32[128]{0:T(128)S(1)}, s32[128]{0:T(128)}, u32[]{:S(2)}) copy-start(s32[128]{0:T(128)} %param.22) | copy-start | bytes 1540
  46.3 1.2 %copy-start.1 = (bf16[16,32,128]{2,1,0:T(8,128)(2,1)S(1)}, bf16[16,32,128]{2,1,0:T(8,128)(2,1)}, u32[]{:S(2)}) copy-start(bf16[16,32,128]{2,1,0:T(8,128)(2,1)} %pair_state.1) | copy-start | bytes 393220
  46.3 1.2 %copy-start.2 = (bf16[128,512]{1,0:T(8,128)(2,1)S(1)}, bf16[128,512]{1,0:T(8,128)(2,1)}, u32[]{:S(2)}) copy-start(bf16[128,512]{1,0:T(8,128)(2,1)} %w_gate.1) | copy-start | bytes 393220
  46.3 1.2 %copy-start.3 = (bf16[128,512]{1,0:T(8,128)(2,1)S(1)}, bf16[128,512]{1,0:T(8,128)(2,1)}, u32[]{:S(2)}) copy-start(bf16[128,512]{1,0:T(8,128)(2,1)} %w_lift.1) | copy-start | bytes 393220
  46.3 1.2 %copy-start.4 = (bf16[512,128]{1,0:T(8,128)(2,1)S(1)}, bf16[512,128]{1,0:T(8,128)(2,1)}, u32[]{:S(2)}) copy-start(bf16[512,128]{1,0:T(8,128)(2,1)} %w_drop.1) | copy-start | bytes 393220
  46.3 1.2 %copy-start.5 = (bf16[128,384]{1,0:T(8,128)(2,1)S(1)}, bf16[128,384]{1,0:T(8,128)(2,1)}, u32[]{:S(2)}) copy-start(bf16[128,384]{1,0:T(8,128)(2,1)} %w_pool.1) | copy-start | bytes 294916
  46.3 1.2 %copy-start.6 = (bf16[384,128]{1,0:T(8,128)(2,1)S(1)}, bf16[384,128]{1,0:T(8,128)(2,1)}, u32[]{:S(2)}) copy-start(bf16[384,128]{1,0:T(8,128)(2,1)} %w_back.1) | copy-start | bytes 294916
  46.3 1.2 %copy-start.9 = (bf16[128,128]{1,0:T(8,128)(2,1)S(1)}, bf16[128,128]{1,0:T(8,128)(2,1)}, u32[]{:S(2)}) copy-start(bf16[128,128]{1,0:T(8,128)(2,1)} %w_value.1) | copy-start | bytes 98308
  46.3 1.2 %copy-start.10 = (bf16[128,128]{1,0:T(8,128)(2,1)S(1)}, bf16[128,128]{1,0:T(8,128)(2,1)}, u32[]{:S(2)}) copy-start(bf16[128,128]{1,0:T(8,128)(2,1)} %w_out.1) | copy-start | bytes 98308
  46.3 1.2 %copy-start.11 = (bf16[384,32]{0,1:T(8,128)(2,1)S(1)}, bf16[384,32]{0,1:T(8,128)(2,1)}, u32[]{:S(2)}) copy-start(bf16[384,32]{0,1:T(8,128)(2,1)} %param.31) | copy-start | bytes 73732
  46.3 1.2 %copy-start.12 = (bf16[384,32]{0,1:T(8,128)(2,1)S(1)}, bf16[384,32]{0,1:T(8,128)(2,1)}, u32[]{:S(2)}) copy-start(bf16[384,32]{0,1:T(8,128)(2,1)} %param.32) | copy-start | bytes 73732
  46.4 1.2 %copy-start = (bf16[32,32,128]{2,1,0:T(8,128)(2,1)S(1)}, bf16[32,32,128]{2,1,0:T(8,128)(2,1)}, u32[]{:S(2)}) copy-start(bf16[32,32,128]{2,1,0:T(8,128)(2,1)} %param.33) | copy-start | bytes 786436
  47.3 0.8 %copy-start.7 = (bf16[128,128]{1,0:T(8,128)(2,1)S(1)}, bf16[128,128]{1,0:T(8,128)(2,1)}, u32[]{:S(2)}) copy-start(bf16[128,128]{1,0:T(8,128)(2,1)} %w_query.1) | copy-start | bytes 98308
  47.3 0.8 %copy-start.8 = (bf16[128,128]{1,0:T(8,128)(2,1)S(1)}, bf16[128,128]{1,0:T(8,128)(2,1)}, u32[]{:S(2)}) copy-start(bf16[128,128]{1,0:T(8,128)(2,1)} %w_key.1) | copy-start | bytes 98308
  47.5 0.7 %copy-start.13 = (f32[128]{0:T(128)S(1)}, f32[128]{0:T(128)}, u32[]{:S(2)}) copy-start(f32[128]{0:T(128)} %param.23) | copy-start | bytes 1540
  47.5 0.7 %copy-start.14 = (f32[128]{0:T(128)S(1)}, f32[128]{0:T(128)}, u32[]{:S(2)}) copy-start(f32[128]{0:T(128)} %param.34) | copy-start | bytes 1540

commit v5 on v0

v5 whole, which is shorter than its diff:
```python
import math

import jax
import jax.numpy as jnp
from jax import lax
from jax.experimental import pallas as pl
from jax.experimental.pallas import tpu as pltpu
from jax.sharding import PartitionSpec as P

HEADS = 4
QB = 32
KW = 128
EPSILON = 1e-05
HALF = KW // 2
FEWEST = 8
LANES = 128
SLOTS = 16
BLOCK = 24
DESTS = 32
PAIR_ROWS = 8
MASKED = -1e30
SPARE = 12 << 20
MOST = 60 << 20
LOG2E = 1.4426950408889634
AXES = ("row", "col")
BF = jnp.bfloat16
F32 = jnp.float32


def layer_norm(values, gain):
    mean_value = jnp.mean(values, axis=-1, keepdims=True)
    centred = values - mean_value
    variance = jnp.mean(centred * centred, axis=-1, keepdims=True)
    return centred * lax.rsqrt(variance + EPSILON) * gain


def dot(a, b):
    return jnp.dot(a, b, preferred_element_type=F32)


def dot_t(a, b):
    return lax.dot_general(a, b, (((1,), (1,)), ((), ())), preferred_element_type=F32)


def iota(shape, axis):
    return lax.broadcasted_iota(jnp.int32, shape, axis)


def flag(mask):
    return jnp.where(mask, 1.0, 0.0).astype(BF)


def atom_kernel(
    own,
    sibling,
    neighbour,
    key_starts,
    counts,
    counts_folded,
    atom_gain,
    w_query,
    w_key,
    w_value,
    w_out,
    w_pool,
    w_back,
    w_left,
    w_right,
    payload,
    updated,
    slot_back,
    slot_last,
    slot_member,
):
    rows, width = own.shape
    tokens = counts.shape[1]
    channels = w_pool.shape[1]
    tiles = channels // LANES
    opm = w_left.shape[0]
    devices = payload.shape[0] // BLOCK
    atoms = rows * devices
    own_tokens = tokens // devices
    token_rows = own_tokens * tiles
    slots = rows // FEWEST + 1
    position = lax.axis_index("row") * lax.axis_size("col") + lax.axis_index("col")
    first = position * rows
    even = position % 2 == 0

    own_float = own[...].astype(F32)
    sibling_float = sibling[...].astype(F32)
    neighbour_float = neighbour[...].astype(F32)
    low = jnp.where(even, neighbour_float, sibling_float)
    high = jnp.where(even, sibling_float, neighbour_float)
    extended = jnp.concatenate([low, own_float, high], axis=0)
    normed = layer_norm(extended, atom_gain[...]).astype(BF)
    keyval = dot(normed, jnp.concatenate([w_key[...], w_value[...]], axis=1)).astype(BF)
    query = dot(normed[rows : 2 * rows], w_query[...]).astype(BF)
    window = rows + KW
    key_lane = iota((1, window), 1)
    key_index = key_lane + (first - HALF)
    in_range = (key_index >= 0) & (key_index < atoms)
    bias = []
    for e in range(rows // QB):
        low_key = key_starts[0:1, e : e + 1]
        seen = in_range & (key_index >= low_key) & (key_index < low_key + KW)
        bias.append(jnp.broadcast_to(jnp.where(seen, 0.0, MASKED), (QB, window)))
    bias = jnp.concatenate(bias, axis=0)
    head_of = iota((1, width), 1) // (width // HEADS)
    head_mask = [(head_of == h).astype(F32) for h in range(HEADS)]
    stacked = jnp.concatenate([query * m.astype(BF) for m in head_mask], axis=0)
    scores = dot_t(stacked, keyval[:, :width])
    scores = scores + jnp.concatenate([bias] * HEADS, axis=0)
    top = jnp.max(scores, axis=-1, keepdims=True)
    scale = (width // HEADS) ** (-0.5) * LOG2E
    raised = jnp.exp2((scores - top) * scale).astype(BF)
    ones = jnp.ones((window, width), BF)
    mixed = dot(raised, jnp.concatenate([keyval[:, width:], ones], axis=1))
    total = sum(mixed[h * rows : (h + 1) * rows, :width] * head_mask[h] for h in range(HEADS))
    weight = sum(mixed[h * rows : (h + 1) * rows, width:] * head_mask[h] for h in range(HEADS))
    attended = (total / weight).astype(BF)
    fresh = (own_float + dot(attended, w_out[...])).astype(BF)
    updated[...] = fresh
    feature = jnp.maximum(dot(fresh, w_pool[...]), 0.0).astype(BF)

    counts_wide = jnp.broadcast_to(counts[...].astype(F32), (tiles * rows, tokens)).astype(BF)
    counts_lane = counts_wide[:LANES]
    folded = counts_folded[...].astype(F32).astype(BF)
    folds = folded.shape[0]
    upper = flag(iota((LANES, LANES), 0) <= iota((LANES, LANES), 1))
    within = dot(folded, upper)
    whole = dot(folded, jnp.ones((LANES, LANES), BF))
    base = jnp.zeros((1, 1), F32)
    before = jnp.zeros((1, LANES), F32)
    first_float = first.astype(F32)
    for fold in range(folds):
        ended = within[fold : fold + 1] + before <= first_float
        base = base + jnp.sum(jnp.where(ended, 1.0, 0.0), axis=1, keepdims=True)
        before = before + whole[fold : fold + 1]

    token_lane = iota((SLOTS, tokens), 1).astype(F32)
    slot_token = iota((SLOTS, tokens), 0).astype(F32) + base
    slot_end = dot_t(flag(token_lane <= slot_token), counts_lane)
    slot_start = dot_t(flag(token_lane < slot_token), counts_lane)
    atom_lane = iota((SLOTS, rows), 1).astype(F32) + first_float
    member = flag((atom_lane >= slot_start[:, :rows]) & (atom_lane < slot_end[:, :rows]))
    slot_member[...] = member
    slot_count = jnp.maximum(slot_end - slot_start, 1.0)
    slot_single = (
        dot(member, feature) / jnp.concatenate([slot_count] * tiles, axis=1)
    ).astype(BF)
    w_sides = jnp.concatenate(
        [w_left[...], w_right[...], jnp.zeros((LANES - 2 * opm, channels), BF)], axis=0
    )
    sides = dot_t(slot_single, w_sides).astype(BF)
    backs = dot(slot_single, w_back[...])
    slot_back[...] = backs
    last_atom = first_float + (rows - 1)
    last = jnp.where((slot_start <= last_atom) & (slot_end > last_atom), 1.0, 0.0)
    slot_last[...] = last
    to_before = backs[0:1] * jnp.where(slot_start[0:1] < first_float, 1.0, 0.0)
    goes_on = last * jnp.where(slot_end > first_float + rows, 1.0, 0.0)
    to_after = jnp.sum(backs * goes_on, axis=0, keepdims=True)
    spot = iota((SLOTS, LANES), 0)
    edges = jnp.where(spot == 0, to_before, jnp.where(spot == 1, to_after, 0.0)).astype(BF)
    shared = jnp.concatenate([sides, edges], axis=0)
    feature_tiles = jnp.concatenate(
        [feature[:, k * LANES : (k + 1) * LANES] for k in range(tiles)], axis=0
    )

    def send_step(step, carry):
        def place(lanes, axis):
            return iota((DESTS, BLOCK, lanes), axis).reshape(DESTS * BLOCK, lanes)

        def token_of(lanes):
            return (place(lanes, 0) + step * DESTS) * own_tokens + place(lanes, 1) % own_tokens

        token_at = iota((DESTS * BLOCK, tokens), 1)
        row_token = token_of(tokens)
        row_end = dot_t(flag(token_at <= row_token), counts_wide)
        row_start = dot_t(flag(token_at < row_token), counts_wide)
        lanes = tiles * rows
        lane = iota((DESTS * BLOCK, lanes), 1)
        atom = (lane % rows + first).astype(F32)
        tile_fits = place(lanes, 1) // own_tokens == lane // rows
        picks = flag(tile_fits & (atom >= row_start) & (atom < row_end))
        row_count = jnp.maximum(row_end - row_start, 1.0)[:, :LANES]
        singles = dot(picks, feature_tiles) / row_count
        dest, spot = place(2 * SLOTS, 0) + step * DESTS, place(2 * SLOTS, 1)
        source = iota((DESTS * BLOCK, 2 * SLOTS), 1)
        is_slot = (source < slots) & (spot == token_rows + source)
        edge = spot == token_rows + slots
        is_before = (source == SLOTS) & edge & (dest == position - 1)
        is_after = (source == SLOTS + 1) & edge & (dest == position + 1)
        part = (singles + dot(flag(is_slot | is_before | is_after), shared)).astype(BF)
        if devices == DESTS:
            payload[...] = part
        else:
            here = pl.multiple_of(step * (DESTS * BLOCK), DESTS * BLOCK)
            payload[pl.ds(here, DESTS * BLOCK), :] = part
        return carry

    if devices == DESTS:
        send_step(0, 0)
    else:
        lax.fori_loop(0, devices // DESTS, send_step, 0)


def pair_kernel(
    arrived,
    adder,
    updated,
    slot_back,
    slot_last,
    slot_member,
    pair_state,
    w_outer,
    pair_gain,
    w_gate,
    w_lift,
    w_drop,
    atom_out,
    token_single,
    pair_out,
):
    row_tokens, col_tokens, pair_width = pair_state.shape
    own_tokens, channels = token_single.shape
    tiles = channels // LANES
    token_rows = own_tokens * tiles
    opm = math.isqrt(w_outer.shape[0])
    added = dot(adder[...], arrived[...])
    left = added[SLOTS : SLOTS + row_tokens, :opm].astype(BF)
    right = added[SLOTS + row_tokens :, opm : 2 * opm].astype(BF)
    product_lane = iota((opm, opm * opm), 1)
    unit = iota((opm, opm * opm), 0)
    left_wide = dot(left, flag(product_lane // opm == unit))
    right_wide = dot(right, flag(product_lane % opm == unit))

    def pair_rows(lefts, here):
        products = jnp.concatenate(
            [(lefts[i : i + 1, :] * right_wide).astype(BF) for i in range(PAIR_ROWS)], axis=0
        )
        flat = pair_state[pl.ds(here, PAIR_ROWS)].reshape(PAIR_ROWS * col_tokens, pair_width)
        summed = flat.astype(F32) + dot(products, w_outer[...])
        normed = layer_norm(summed, pair_gain[...]).astype(BF)
        gate = dot(normed, w_gate[...])
        lift = dot(normed, w_lift[...])
        hidden = (gate * (0.5 + 0.5 * jnp.tanh(0.5 * gate)) * lift).astype(BF)
        result = (summed + dot(hidden, w_drop[...])).astype(BF)
        pair_out[pl.ds(here, PAIR_ROWS)] = result.reshape(PAIR_ROWS, col_tokens, pair_width)

    for step in range(row_tokens // PAIR_ROWS):
        here = step * PAIR_ROWS
        pair_rows(left_wide[here : here + PAIR_ROWS], here)

    token_single[...] = jnp.concatenate(
        [added[k * own_tokens : (k + 1) * own_tokens] for k in range(tiles)], axis=1
    ).astype(BF)
    spot = iota((SLOTS, LANES), 0)
    from_before = jnp.where(spot == 0, added[token_rows : token_rows + 1], 0.0)
    from_after = slot_last[...] * added[token_rows + 1 : token_rows + 2]
    back = (slot_back[...] + from_before + from_after).astype(BF)
    lifted = lax.dot_general(
        slot_member[...], back, (((0,), (0,)), ((), ())), preferred_element_type=F32
    )
    atom_out[...] = (updated[...].astype(F32) + lifted).astype(BF)


def adder_matrix(atom_counts, devices, rows, token_rows, row_tokens, col_tokens):
    position = lax.axis_index(AXES)
    slots = rows // FEWEST + 1
    ends = jnp.cumsum(atom_counts, dtype=jnp.int32)
    block = jnp.arange(devices, dtype=jnp.int32)
    base = jnp.sum((ends[None, :] <= (block * rows)[:, None]).astype(jnp.int32), axis=1)
    spot = jnp.arange(BLOCK, dtype=jnp.int32)
    is_slot = (spot >= token_rows) & (spot < token_rows + slots)
    token = jnp.where(is_slot[None, :], base[:, None] + (spot - token_rows)[None, :], -1)
    token = token.reshape(1, -1)
    place = jnp.arange(devices * BLOCK, dtype=jnp.int32)[None, :]
    line = jnp.arange(SLOTS, dtype=jnp.int32)[:, None]
    side = jnp.where(line == token_rows, position - 1, position + 1)
    edge = (line >= token_rows) & (line < token_rows + 2)
    fixed = jnp.where(
        edge,
        place == side * BLOCK + token_rows + slots,
        (place % BLOCK == line) & (line < token_rows),
    )
    first_row = lax.axis_index("row") * row_tokens
    first_col = lax.axis_index("col") * col_tokens
    lefts = token == (first_row + jnp.arange(row_tokens, dtype=jnp.int32))[:, None]
    rights = token == (first_col + jnp.arange(col_tokens, dtype=jnp.int32))[:, None]
    return jnp.concatenate([fixed, lefts, rights], axis=0).astype(BF)


def call(kernel, name, operands, outputs):
    vmem = pl.BlockSpec(memory_space=pltpu.VMEM)
    held = sum(math.prod(a.shape) * a.dtype.itemsize for a in operands + outputs)
    return pl.pallas_call(
        kernel,
        out_shape=outputs,
        in_specs=[vmem] * len(operands),
        out_specs=(vmem,) * len(outputs),
        compiler_params=pltpu.CompilerParams(vmem_limit_bytes=min(2 * held + SPARE, MOST)),
        name=name,
    )(*operands)


def per_device(
    atom_feats,
    key_starts,
    atom_counts,
    atom_gain,
    w_query,
    w_key,
    w_value,
    w_out,
    w_pool,
    w_back,
    pair_state,
    w_left,
    w_right,
    w_outer,
    pair_gain,
    w_gate,
    w_lift,
    w_drop,
):
    rows, width = atom_feats.shape
    devices = lax.axis_size(AXES)
    tokens = atom_counts.shape[0]
    channels = w_pool.shape[1]
    opm = w_left.shape[1]
    own_tokens = tokens // devices
    row_tokens, col_tokens, _ = pair_state.shape
    token_rows = own_tokens * channels // LANES
    sibling = lax.ppermute(atom_feats, AXES, [(i, i ^ 1) for i in range(devices)])
    across = [(i, i + 1) for i in range(1, devices - 1, 2)]
    neighbour = lax.ppermute(atom_feats, AXES, across + [(j, i) for i, j in across])
    payload, updated, slot_back, slot_last, slot_member = call(
        atom_kernel,
        "atoms",
        (
            atom_feats,
            sibling,
            neighbour,
            key_starts[None],
            atom_counts[None],
            atom_counts.reshape(-1, LANES),
            atom_gain[None],
            w_query,
            w_key,
            w_value,
            w_out,
            w_pool,
            w_back,
            w_left.T,
            w_right.T,
        ),
        (
            jax.ShapeDtypeStruct((devices * BLOCK, LANES), BF),
            jax.ShapeDtypeStruct((rows, width), BF),
            jax.ShapeDtypeStruct((SLOTS, width), F32),
            jax.ShapeDtypeStruct((SLOTS, width), F32),
            jax.ShapeDtypeStruct((SLOTS, rows), BF),
        ),
    )
    arrived = lax.all_to_all(payload.reshape(devices, BLOCK, LANES), AXES, 0, 0)
    adder = adder_matrix(atom_counts, devices, rows, token_rows, row_tokens, col_tokens)
    return call(
        pair_kernel,
        "pairs",
        (
            arrived.reshape(devices * BLOCK, LANES),
            adder,
            updated,
            slot_back,
            slot_last,
            slot_member,
            pair_state,
            w_outer.reshape(opm * opm, -1),
            pair_gain[None],
            w_gate,
            w_lift,
            w_drop,
        ),
        (
            jax.ShapeDtypeStruct(atom_feats.shape, BF),
            jax.ShapeDtypeStruct((own_tokens, channels), BF),
            jax.ShapeDtypeStruct(pair_state.shape, BF),
        ),
    )


def solution(mesh):
    in_specs = (
        P(("row", "col"), None),
        P(("row", "col")),
        P(),
        P(),
        P(),
        P(),
        P(),
        P(),
        P(),
        P(),
        P("row", "col", None),
        P(),
        P(),
        P(),
        P(),
        P(),
        P(),
        P(),
    )
    out_specs = (P(("row", "col"), None), P(("row", "col"), None), P("row", "col", None))
    return jax.shard_map(
        per_device, mesh=mesh, in_specs=in_specs, out_specs=out_specs, check_vma=False
    )
```

time: 85.3 us -> 30.3 us (0.36)
  blocking collectives: 43.1 us -> 0 us
  local copies, waits for them, and re-layouts: 17.4 us -> 2.77 us
  starting transfers between devices: 5.61 us -> 11.3 us
  matrix products: 5.55 us -> 0 us
  Pallas kernels: 0 us -> 5.28 us
  waiting for transfers between devices: 3.72 us -> 8.76 us
  other arithmetic: 4.54 us -> 0.83 us
  between operations: 4.29 us -> 0.89 us
    all_gather x1 -> x0, blocking collectives: 43.1 us -> none  [per_device(): gathered = lax.all_gather(slot_single, ('row', 'col'), axis=0, tiled=True)]
    gather x13 -> x0, local copies, waits for them, and re-layouts: 10.8 us -> none  [the longest x8 9.81 us: per_device(): owner_first = jnp.searchsorted(token_starts, owner * atom_rows, side='left')]
    all_to_all x0 -> x1, starting transfers between devices: none -> 10.1 us  [per_device(): arrived = lax.all_to_all(payload.reshape(devices, BLOCK, LANES), AXES, 0, 0)]
    all_to_all x0 -> x1, waiting for transfers between devices: none -> 8.76 us  [per_device(): arrived = lax.all_to_all(payload.reshape(devices, BLOCK, LANES), AXES, 0, 0)]
    dot_general x20 -> x0, matrix products: 5.55 us -> none  [the longest x4 1.48 us: project(): jnp.dot(source, weight, preferred_element_type=jnp.float32)]
    pallas_call x0 -> x2, Pallas kernels: none -> 5.28 us  [call(): pl.pallas_call(kernel, out_shape=outputs, in_specs=[vmem] * len(operands)...]
    ppermute x3 -> x2, starting transfers between devices: 5.61 us -> 1.17 us  [the longest x1 0.65 us: per_device(): lax.ppermute(atom_feats, AXES, across + [(j, i) for i, j in across])]
    ppermute x3 -> x2, waiting for transfers between devices: 3.72 us -> 0.01 us  [the longest x1 0.01 us: per_device(): lax.ppermute(atom_feats, AXES, [(i, i ^ 1) for i in range(devices)])]
  transfers between devices with their start and end apart: 3 -> 3, of which waited for: 1 -> 1; matrix products, arithmetic and copies ran while one was open for 15% -> 3% of each run, Pallas kernels for 0% -> 0%
where the time goes in v5:
time: 30.3 us; the launch traced here: 29.8 us
  starting transfers between devices  11.3 us (37%)
  waiting for transfers between devices  8.76 us (29%)
  Pallas kernels  5.28 us (17%)
  local copies, waits for them, and re-layouts  2.77 us (9%)
  between operations  0.89 us (3%)
  other arithmetic  0.83 us (3%)
    all_to_all x1, starting transfers between devices, per_device(): arrived = lax.all_to_all(payload.reshape(devices, BLOCK, LANES), AXES, 0, 0)  10.1 us
    all_to_all x1, waiting for transfers between devices, per_device(): arrived = lax.all_to_all(payload.reshape(devices, BLOCK, LANES), AXES, 0, 0)  8.76 us
    pallas_call x2, Pallas kernels, call(): pl.pallas_call(kernel, out_shape=outputs, in_specs=[vmem] * len(operands)...  5.28 us
    unnamed x36, local copies, waits for them, and re-layouts  2.57 us
    ppermute x1, starting transfers between devices, per_device(): lax.ppermute(atom_feats, AXES, across + [(j, i) for i, j in across])  0.65 us
  transfers between devices with their start and end apart: 3, of which 1 were waited for; matrix products, arithmetic and copies ran while one was open for 3% of the time, Pallas kernels for 0%

profile of v5, /device:TPU:0, one launch (start us, length us, event | category | flops | bytes accessed | tf_op | source)
XLA Modules:
  0.0 29.8 jit_solution(17302902545616297074)
XLA Ops:
  0.6 0.5 %collective-permute-start = (bf16[64,128]{1,0:T(8,128)(2,1)}, bf16[64,128]{1,0:T(8,128)(2,1)S(1)}, u32[]{:S(2)}, u32[]{:S(2)}) collective-permute-start(bf16[64,128]{1,0:T(8,128)(2,1)} %own.1), channel_id=1, source_target_pairs={{0,1},{1,0},{2,3},{3,2},{4,5},{5,4},{6,7},{7,6},{8,9},{9,8},{10,11... | collective-permute-start | bytes 49160 | tf_op jit(solution)/shard_map/ppermute | solution.py:335
  1.1 0.7 %collective-permute-start.1 = (bf16[64,128]{1,0:T(8,128)(2,1)}, bf16[64,128]{1,0:T(8,128)(2,1)S(1)}, u32[]{:S(2)}, u32[]{:S(2)}) collective-permute-start(bf16[64,128]{1,0:T(8,128)(2,1)} %own.1), channel_id=1, source_target_pairs={{1,2},{3,4},{5,6},{7,8},{9,10},{11,12},{13,14},{15,16},{17,18},{19... | collective-permute-start | bytes 49160 | tf_op jit(solution)/shard_map/ppermute | solution.py:337
  1.9 0.0 copy-start.14
  1.9 0.6 %copy-done.14 = s32[128]{0:T(128)S(1)} copy-done((s32[128]{0:T(128)S(1)}, s32[128]{0:T(128)}, u32[]{:S(2)}) %copy-start.14) | copy-done | bytes 536
  2.5 0.0 copy-start.10
  2.5 0.0 copy-start.11
  2.5 0.0 copy-start.12
  2.5 0.1 copy.23
  2.6 0.0 copy-start.6
  2.7 0.0 copy-start.9
  2.7 0.2 reduce-window.8
  2.8 0.0 copy-start.5
  2.8 0.1 reduce
  2.9 0.2 convert_reduce_fusion
  3.1 0.1 add_select_fusion
  3.2 0.1 select_n.40
  3.3 0.0 copy-start.15
  3.3 0.0 copy-start.16
  3.3 0.0 copy-start.7
  3.3 0.0 copy-start.8
  3.4 0.1 fusion
  3.5 0.1 broadcast_compare_fusion.1
  3.6 0.0 collective-permute-done.sibling
  3.6 0.0 collective-permute-done.1.neighbour
  3.6 0.0 copy-done.10
  3.6 0.0 copy-done.11
  3.6 0.0 copy-done.12
  3.6 0.0 copy-done.6
  3.6 0.0 copy-done.9
  3.6 0.1 copy-done.5
  3.8 0.2 copy-done.15
  4.0 0.0 copy-done.16
  4.0 0.1 copy-done.7
  4.1 0.0 copy-done.8
  4.1 0.7 %copy-done.13 = bf16[64,128]{1,0:T(8,128)(2,1)S(1)} copy-done((bf16[64,128]{1,0:T(8,128)(2,1)S(1)}, bf16[64,128]{1,0:T(8,128)(2,1)}, u32[]{:S(2)}) %copy-start.13) | copy-done | bytes 16408
  4.9 0.0 copy-start.3
  4.9 2.7 %atoms.1 = (bf16[768,128]{1,0:T(8,128)(2,1)}, bf16[64,128]{1,0:T(8,128)(2,1)S(1)}, f32[16,128]{1,0:T(8,128)S(1)}, f32[16,128]{1,0:T(8,128)S(1)}, bf16[16,64]{1,0:T(8,128)(2,1)S(1)}) custom-call(bf16[64,128]{1,0:T(8,128)(2,1)S(1)} %copy-done.13, bf16[64,128]{1,0:T(8,128)(2,1)S(1)} %collective-permute-done.sibling, ...), custom_call_target="tpu_custom_call" | custom-call | tf_op jit(solution)/shard_map/atoms/pallas_call | solution.py:297
  7.5 10.1 %all-to-all-start = ((bf16[32,24,128]{2,1,0:T(8,128)(2,1)}), bf16[32,24,128]{2,1,0:T(8,128)(2,1)S(1)}, u32[]{:S(2)}, u32[]{:S(2)}) async-start(bf16[32,24,128]{2,1,0:T(8,128)(2,1)} %bitcast.5), calls=%async_computation | async-start | bytes 393216 | tf_op jit(solution)/shard_map/all_to_all | solution.py:366
  17.6 0.0 copy-start.1
  17.7 0.1 broadcast_compare_fusion
  17.8 8.8 %all-to-all-done = bf16[32,24,128]{2,1,0:T(8,128)(2,1)S(1)} async-done(((bf16[32,24,128]{2,1,0:T(8,128)(2,1)}), bf16[32,24,128]{2,1,0:T(8,128)(2,1)S(1)}, u32[]{:S(2)}, u32[]{:S(2)}) %all-to-all-start) | async-done | bytes 196640 | tf_op jit(solution)/shard_map/all_to_all | solution.py:366
  26.5 0.0 copy-done.3
  26.5 0.0 copy-done.4
  26.5 0.0 copy-done
  26.5 0.0 copy-done.2
  26.6 0.0 copy-done.1
  26.6 0.6 %copy-done.17 = f32[128]{0:T(128)S(1)} copy-done((f32[128]{0:T(128)S(1)}, f32[128]{0:T(128)}, u32[]{:S(2)}) %copy-start.17) | copy-done | bytes 536
  27.2 2.6 %pairs.1 = (bf16[64,128]{1,0:T(8,128)(2,1)}, bf16[4,384]{1,0:T(4,128)(2,1)}, bf16[16,32,128]{2,1,0:T(8,128)(2,1)}) custom-call(bf16[768,128]{1,0:T(8,128)(2,1)S(1)} %bitcast.10, bf16[64,768]{1,0:T(8,128)(2,1)S(1)} %add_convert_fusion.adder, bf16[64,128]{1,0:T(8,128)(2,1)S(1)} %get-tuple-element.9.updated, f32[16,128]{1,0:T(8,128)S(1)} %get-tuple-element.10.slot_back, ...), custom_call_target="tpu_custom_call" | custom-call | tf_op jit(solution)/shard_map/pairs/pallas_call | solution.py:297
  (14 shorter events, 0.1 us)
Async XLA Ops:
  0.6 2.9 %collective-permute-start = (bf16[64,128]{1,0:T(8,128)(2,1)}, bf16[64,128]{1,0:T(8,128)(2,1)S(1)}, u32[]{:S(2)}, u32[]{:S(2)}) collective-permute-start(bf16[64,128]{1,0:T(8,128)(2,1)} %own.1), channel_id=1, source_target_pairs={{0,1},{1,0},{2,3},{3,2},{4,5},{5,4},{6,7},{7,6},{8,9},{9,8},{10,11... | collective-permute-start | bytes 49160 | tf_op jit(solution)/shard_map/ppermute | solution.py:335
  1.1 2.4 %collective-permute-start.1 = (bf16[64,128]{1,0:T(8,128)(2,1)}, bf16[64,128]{1,0:T(8,128)(2,1)S(1)}, u32[]{:S(2)}, u32[]{:S(2)}) collective-permute-start(bf16[64,128]{1,0:T(8,128)(2,1)} %own.1), channel_id=1, source_target_pairs={{1,2},{3,4},{5,6},{7,8},{9,10},{11,12},{13,14},{15,16},{17,18},{19... | collective-permute-start | bytes 49160 | tf_op jit(solution)/shard_map/ppermute | solution.py:337
  1.9 0.7 %copy-start.14 = (s32[128]{0:T(128)S(1)}, s32[128]{0:T(128)}, u32[]{:S(2)}) copy-start(s32[128]{0:T(128)} %param.20) | copy-start | bytes 1540
  2.5 1.0 %copy-start.10 = (bf16[128,128]{1,0:T(8,128)(2,1)S(1)}, bf16[128,128]{1,0:T(8,128)(2,1)}, u32[]{:S(2)}) copy-start(bf16[128,128]{1,0:T(8,128)(2,1)} %w_out.1) | copy-start | bytes 98308
  2.5 1.1 %copy-start.11 = (bf16[384,32]{0,1:T(8,128)(2,1)S(1)}, bf16[384,32]{0,1:T(8,128)(2,1)}, u32[]{:S(2)}) copy-start(bf16[384,32]{0,1:T(8,128)(2,1)} %param.29) | copy-start | bytes 73732
  2.5 1.1 %copy-start.12 = (bf16[384,32]{0,1:T(8,128)(2,1)S(1)}, bf16[384,32]{0,1:T(8,128)(2,1)}, u32[]{:S(2)}) copy-start(bf16[384,32]{0,1:T(8,128)(2,1)} %param.30) | copy-start | bytes 73732
  2.6 1.0 %copy-start.6 = (bf16[384,128]{1,0:T(8,128)(2,1)S(1)}, bf16[384,128]{1,0:T(8,128)(2,1)}, u32[]{:S(2)}) copy-start(bf16[384,128]{1,0:T(8,128)(2,1)} %w_back.1) | copy-start | bytes 294916
  2.7 1.0 %copy-start.9 = (bf16[128,128]{1,0:T(8,128)(2,1)S(1)}, bf16[128,128]{1,0:T(8,128)(2,1)}, u32[]{:S(2)}) copy-start(bf16[128,128]{1,0:T(8,128)(2,1)} %w_value.1) | copy-start | bytes 98308
  2.8 0.9 %copy-start.5 = (bf16[128,384]{1,0:T(8,128)(2,1)S(1)}, bf16[128,384]{1,0:T(8,128)(2,1)}, u32[]{:S(2)}) copy-start(bf16[128,384]{1,0:T(8,128)(2,1)} %w_pool.1) | copy-start | bytes 294916
  3.3 0.7 %copy-start.15 = (s32[2]{0:T(128)S(1)}, s32[2]{0:T(128)}, u32[]{:S(2)}) copy-start(s32[2]{0:T(128)} %param.19) | copy-start | bytes 28
  3.3 0.7 %copy-start.16 = (f32[128]{0:T(128)S(1)}, f32[128]{0:T(128)}, u32[]{:S(2)}) copy-start(f32[128]{0:T(128)} %param.21) | copy-start | bytes 1540
  3.3 0.8 %copy-start.7 = (bf16[128,128]{1,0:T(8,128)(2,1)S(1)}, bf16[128,128]{1,0:T(8,128)(2,1)}, u32[]{:S(2)}) copy-start(bf16[128,128]{1,0:T(8,128)(2,1)} %w_query.1) | copy-start | bytes 98308
  3.3 0.8 %copy-start.8 = (bf16[128,128]{1,0:T(8,128)(2,1)S(1)}, bf16[128,128]{1,0:T(8,128)(2,1)}, u32[]{:S(2)}) copy-start(bf16[128,128]{1,0:T(8,128)(2,1)} %w_key.1) | copy-start | bytes 98308
  4.1 0.7 %copy-start.13 = (bf16[64,128]{1,0:T(8,128)(2,1)S(1)}, bf16[64,128]{1,0:T(8,128)(2,1)}, u32[]{:S(2)}) copy-start(bf16[64,128]{1,0:T(8,128)(2,1)} %own.1) | copy-start | bytes 49156
  4.9 21.7 %copy-start.3 = (bf16[128,512]{1,0:T(8,128)(2,1)S(1)}, bf16[128,512]{1,0:T(8,128)(2,1)}, u32[]{:S(2)}) copy-start(bf16[128,512]{1,0:T(8,128)(2,1)} %w_lift.1) | copy-start | bytes 393220
  4.9 21.7 %copy-start.4 = (bf16[512,128]{1,0:T(8,128)(2,1)S(1)}, bf16[512,128]{1,0:T(8,128)(2,1)}, u32[]{:S(2)}) copy-start(bf16[512,128]{1,0:T(8,128)(2,1)} %w_drop.1) | copy-start | bytes 393220
  7.5 19.0 %copy-start = (bf16[32,32,128]{2,1,0:T(8,128)(2,1)S(1)}, bf16[32,32,128]{2,1,0:T(8,128)(2,1)}, u32[]{:S(2)}) copy-start(bf16[32,32,128]{2,1,0:T(8,128)(2,1)} %param.31) | copy-start | bytes 786436
  7.5 19.0 %copy-start.2 = (bf16[128,512]{1,0:T(8,128)(2,1)S(1)}, bf16[128,512]{1,0:T(8,128)(2,1)}, u32[]{:S(2)}) copy-start(bf16[128,512]{1,0:T(8,128)(2,1)} %w_gate.1) | copy-start | bytes 393220
  7.5 19.0 %all-to-all-start = ((bf16[32,24,128]{2,1,0:T(8,128)(2,1)}), bf16[32,24,128]{2,1,0:T(8,128)(2,1)S(1)}, u32[]{:S(2)}, u32[]{:S(2)}) async-start(bf16[32,24,128]{2,1,0:T(8,128)(2,1)} %bitcast.5), calls=%async_computation | async-start | bytes 393216 | tf_op jit(solution)/shard_map/all_to_all | solution.py:366
  17.6 8.9 %copy-start.1 = (bf16[16,32,128]{2,1,0:T(8,128)(2,1)S(1)}, bf16[16,32,128]{2,1,0:T(8,128)(2,1)}, u32[]{:S(2)}) copy-start(bf16[16,32,128]{2,1,0:T(8,128)(2,1)} %pair_state.1) | copy-start | bytes 393220
  26.5 0.7 %copy-start.17 = (f32[128]{0:T(128)S(1)}, f32[128]{0:T(128)}, u32[]{:S(2)}) copy-start(f32[128]{0:T(128)} %param.32) | copy-start | bytes 1540

commit v6 on v5

v6 whole, which is shorter than its diff:
```python
import math

import jax
import jax.numpy as jnp
from jax import lax
from jax.experimental import pallas as pl
from jax.experimental.pallas import tpu as pltpu
from jax.sharding import PartitionSpec as P

HEADS = 4
QB = 32
KW = 128
EPSILON = 1e-05
HALF = KW // 2
FEWEST = 8
LANES = 128
SLOTS = 16
BLOCK = 24
DESTS = 32
PAIR_ROWS = 8
MASKED = -1e30
SPARE = 12 << 20
MOST = 60 << 20
LOG2E = 1.4426950408889634
AXES = ("row", "col")
BF = jnp.bfloat16
F32 = jnp.float32


def layer_norm(values, gain):
    mean_value = jnp.mean(values, axis=-1, keepdims=True)
    centred = values - mean_value
    variance = jnp.mean(centred * centred, axis=-1, keepdims=True)
    return centred * lax.rsqrt(variance + EPSILON) * gain


def dot(a, b):
    return jnp.dot(a, b, preferred_element_type=F32)


def dot_t(a, b):
    return lax.dot_general(a, b, (((1,), (1,)), ((), ())), preferred_element_type=F32)


def iota(shape, axis):
    return lax.broadcasted_iota(jnp.int32, shape, axis)


def flag(mask):
    return jnp.where(mask, 1.0, 0.0).astype(BF)


def place():
    return lax.axis_index("row") * lax.axis_size("col") + lax.axis_index("col")


def each_part(devices, step):
    if devices == DESTS:
        step(0)
    else:

        def body(at, carry):
            step(at)
            return carry

        lax.fori_loop(0, devices // DESTS, body, 0)


def part_rows(devices, at):
    size = DESTS * BLOCK
    if devices == DESTS:
        return pl.ds(0, size)
    return pl.ds(pl.multiple_of(at * size, size), size)


def ready_kernel(
    own,
    sibling,
    key_starts,
    counts,
    counts_folded,
    atom_gain,
    pair_gain,
    w_query,
    w_key,
    w_value,
    own_float,
    keyval,
    stacked,
    scores,
    top,
    far_bias,
    picks,
    row_scale,
    selects,
    member,
    slot_scale,
    before,
    goes_on,
    last,
    atom_gain_kept,
    pair_gain_kept,
):
    rows, width = own.shape
    tokens = counts.shape[1]
    tiles = picks.shape[1] // rows
    devices = picks.shape[0] // BLOCK
    atoms = rows * devices
    own_tokens = tokens // devices
    token_rows = own_tokens * tiles
    slots = rows // FEWEST + 1
    position = place()
    first = position * rows
    even = position % 2 == 0

    atom_gain_kept[...] = atom_gain[...]
    pair_gain_kept[...] = pair_gain[...]
    raw = jnp.concatenate([own[...].astype(F32), sibling[...].astype(F32)], axis=0)
    own_float[...] = raw[:rows]
    normed = layer_norm(raw, atom_gain[...]).astype(BF)
    near = dot(normed, jnp.concatenate([w_key[...], w_value[...]], axis=1)).astype(BF)
    keyval[...] = near
    query = dot(normed[:rows], w_query[...]).astype(BF)
    head_of = iota((1, width), 1) // (width // HEADS)
    heads = jnp.concatenate([query * flag(head_of == h) for h in range(HEADS)], axis=0)
    stacked[...] = heads
    near_lane = iota((1, 2 * rows), 1)
    side = jnp.where(even, 0, -2 * rows)
    near_index = first + near_lane + jnp.where(near_lane < rows, 0, side)
    far_index = first + jnp.where(even, -rows, rows) + iota((1, rows), 1)
    near_bias, bias = [], []
    for e in range(rows // QB):
        low = key_starts[0:1, e : e + 1]
        seen = (near_index >= low) & (near_index < low + KW)
        near_bias.append(jnp.broadcast_to(jnp.where(seen, 0.0, MASKED), (QB, 2 * rows)))
        seen = (far_index >= low) & (far_index < low + KW)
        seen = seen & (far_index >= 0) & (far_index < atoms)
        bias.append(jnp.broadcast_to(jnp.where(seen, 0.0, MASKED), (QB, rows)))
    far_bias[...] = jnp.concatenate(bias, axis=0)
    raw_scores = dot_t(heads, near[:, :width]) + jnp.concatenate(near_bias * HEADS, axis=0)
    scores[...] = raw_scores
    top[...] = jnp.max(raw_scores, axis=-1, keepdims=True)

    counts_wide = jnp.broadcast_to(counts[...].astype(F32), (tiles * rows, tokens)).astype(BF)
    counts_lane = counts_wide[:LANES]
    folded = counts_folded[...].astype(F32).astype(BF)
    upper = flag(iota((LANES, LANES), 0) <= iota((LANES, LANES), 1))
    within = dot(folded, upper)
    whole = dot(folded, jnp.ones((LANES, LANES), BF))
    base = jnp.zeros((1, 1), F32)
    passed = jnp.zeros((1, LANES), F32)
    first_float = first.astype(F32)
    for fold in range(folded.shape[0]):
        ended = within[fold : fold + 1] + passed <= first_float
        base = base + jnp.sum(jnp.where(ended, 1.0, 0.0), axis=1, keepdims=True)
        passed = passed + whole[fold : fold + 1]

    token_lane = iota((SLOTS, tokens), 1).astype(F32)
    slot_token = iota((SLOTS, tokens), 0).astype(F32) + base
    slot_end = dot_t(flag(token_lane <= slot_token), counts_lane)
    slot_start = dot_t(flag(token_lane < slot_token), counts_lane)
    atom_lane = iota((SLOTS, rows), 1).astype(F32) + first_float
    member[...] = flag((atom_lane >= slot_start[:, :rows]) & (atom_lane < slot_end[:, :rows]))
    slot_scale[...] = 1.0 / jnp.maximum(slot_end - slot_start, 1.0)
    last_atom = first_float + (rows - 1)
    is_last = jnp.where((slot_start <= last_atom) & (slot_end > last_atom), 1.0, 0.0)
    last[...] = is_last
    goes_on[...] = is_last * jnp.where(slot_end > first_float + rows, 1.0, 0.0)
    is_first = iota((SLOTS, LANES), 0) == 0
    before[...] = jnp.where(is_first & (slot_start < first_float), 1.0, 0.0)

    def rows_step(at):
        def spread(lanes, axis):
            return iota((DESTS, BLOCK, lanes), axis).reshape(DESTS * BLOCK, lanes)

        here = part_rows(devices, at)
        token_at = iota((DESTS * BLOCK, tokens), 1)
        row_token = (spread(tokens, 0) + at * DESTS) * own_tokens + spread(tokens, 1) % own_tokens
        row_end = dot_t(flag(token_at <= row_token), counts_wide)
        row_start = dot_t(flag(token_at < row_token), counts_wide)
        lanes = tiles * rows
        lane = iota((DESTS * BLOCK, lanes), 1)
        atom = (lane % rows + first).astype(F32)
        tile_fits = spread(lanes, 1) // own_tokens == lane // rows
        picks[here, :] = flag(tile_fits & (atom >= row_start) & (atom < row_end))
        row_scale[here, :] = 1.0 / jnp.maximum(row_end - row_start, 1.0)[:, :LANES]
        dest, spot = spread(2 * SLOTS, 0) + at * DESTS, spread(2 * SLOTS, 1)
        source = iota((DESTS * BLOCK, 2 * SLOTS), 1)
        is_slot = (source < slots) & (spot == token_rows + source)
        edge = spot == token_rows + slots
        is_before = (source == SLOTS) & edge & (dest == position - 1)
        is_after = (source == SLOTS + 1) & edge & (dest == position + 1)
        selects[here, :] = flag(is_slot | is_before | is_after)

    each_part(devices, rows_step)


def atom_kernel(
    neighbour,
    own_float,
    keyval,
    stacked,
    scores,
    top,
    far_bias,
    picks,
    row_scale,
    selects,
    member,
    slot_scale,
    before,
    goes_on,
    atom_gain,
    w_key,
    w_value,
    w_out,
    w_pool,
    w_back,
    w_left,
    w_right,
    payload,
    updated,
    slot_back,
):
    rows, width = own_float.shape
    channels = w_pool.shape[1]
    tiles = channels // LANES
    opm = w_left.shape[0]
    devices = payload.shape[0] // BLOCK
    normed = layer_norm(neighbour[...].astype(F32), atom_gain[...]).astype(BF)
    far = dot(normed, jnp.concatenate([w_key[...], w_value[...]], axis=1)).astype(BF)
    far_scores = dot_t(stacked[...], far[:, :width])
    far_scores = far_scores + jnp.concatenate([far_bias[...]] * HEADS, axis=0)
    most = jnp.maximum(top[...], jnp.max(far_scores, axis=-1, keepdims=True))
    scale = (width // HEADS) ** (-0.5) * LOG2E
    raised = jnp.concatenate(
        [
            jnp.exp2((scores[...] - most) * scale).astype(BF),
            jnp.exp2((far_scores - most) * scale).astype(BF),
        ],
        axis=1,
    )
    values = jnp.concatenate([keyval[:, width:], far[:, width:]], axis=0)
    mixed = dot(raised, jnp.concatenate([values, jnp.ones((3 * rows, width), BF)], axis=1))
    head_of = iota((1, width), 1) // (width // HEADS)
    head_mask = [(head_of == h).astype(F32) for h in range(HEADS)]
    total = sum(mixed[h * rows : (h + 1) * rows, :width] * head_mask[h] for h in range(HEADS))
    weight = sum(mixed[h * rows : (h + 1) * rows, width:] * head_mask[h] for h in range(HEADS))
    attended = (total / weight).astype(BF)
    fresh = (own_float[...] + dot(attended, w_out[...])).astype(BF)
    updated[...] = fresh
    feature = jnp.maximum(dot(fresh, w_pool[...]), 0.0).astype(BF)
    feature_tiles = jnp.concatenate(
        [feature[:, k * LANES : (k + 1) * LANES] for k in range(tiles)], axis=0
    )
    slot_single = (
        dot(member[...], feature) * jnp.concatenate([slot_scale[...]] * tiles, axis=1)
    ).astype(BF)
    w_sides = jnp.concatenate(
        [w_left[...], w_right[...], jnp.zeros((LANES - 2 * opm, channels), BF)], axis=0
    )
    sides = dot_t(slot_single, w_sides).astype(BF)
    backs = dot(slot_single, w_back[...])
    slot_back[...] = backs
    to_before = jnp.sum(backs * before[...], axis=0, keepdims=True)
    to_after = jnp.sum(backs * goes_on[...], axis=0, keepdims=True)
    spot = iota((SLOTS, LANES), 0)
    edges = jnp.where(spot == 0, to_before, jnp.where(spot == 1, to_after, 0.0)).astype(BF)
    shared = jnp.concatenate([sides, edges], axis=0)

    def send_step(at):
        here = part_rows(devices, at)
        singles = dot(picks[here, :], feature_tiles) * row_scale[here, :]
        payload[here, :] = (singles + dot(selects[here, :], shared)).astype(BF)

    each_part(devices, send_step)


def pair_kernel(
    arrived,
    adder,
    updated,
    slot_back,
    slot_last,
    slot_member,
    pair_state,
    w_outer,
    pair_gain,
    w_gate,
    w_lift,
    w_drop,
    atom_out,
    token_single,
    pair_out,
):
    row_tokens, col_tokens, pair_width = pair_state.shape
    own_tokens, channels = token_single.shape
    tiles = channels // LANES
    token_rows = own_tokens * tiles
    opm = math.isqrt(w_outer.shape[0])
    added = dot(adder[...], arrived[...])
    half_gate = w_gate[...] * jnp.asarray(0.5, BF)
    left = added[SLOTS : SLOTS + row_tokens, :opm].astype(BF)
    right = added[SLOTS + row_tokens :, opm : 2 * opm].astype(BF)
    product_lane = iota((opm, opm * opm), 1)
    unit = iota((opm, opm * opm), 0)
    left_wide = dot(left, flag(product_lane // opm == unit))
    right_wide = dot(right, flag(product_lane % opm == unit))

    def pair_rows(lefts, here):
        products = jnp.concatenate(
            [(lefts[i : i + 1, :] * right_wide).astype(BF) for i in range(PAIR_ROWS)], axis=0
        )
        flat = pair_state[pl.ds(here, PAIR_ROWS)].reshape(PAIR_ROWS * col_tokens, pair_width)
        summed = flat.astype(F32) + dot(products, w_outer[...])
        normed = layer_norm(summed, pair_gain[...]).astype(BF)
        gate = dot(normed, half_gate)
        lift = dot(normed, w_lift[...])
        hidden = (gate * lift * (1.0 + jnp.tanh(gate))).astype(BF)
        result = (summed + dot(hidden, w_drop[...])).astype(BF)
        pair_out[pl.ds(here, PAIR_ROWS)] = result.reshape(PAIR_ROWS, col_tokens, pair_width)

    for step in range(row_tokens // PAIR_ROWS):
        here = step * PAIR_ROWS
        pair_rows(left_wide[here : here + PAIR_ROWS], here)

    token_single[...] = jnp.concatenate(
        [added[k * own_tokens : (k + 1) * own_tokens] for k in range(tiles)], axis=1
    ).astype(BF)
    spot = iota((SLOTS, LANES), 0)
    from_before = jnp.where(spot == 0, added[token_rows : token_rows + 1], 0.0)
    from_after = slot_last[...] * added[token_rows + 1 : token_rows + 2]
    back = (slot_back[...] + from_before + from_after).astype(BF)
    lifted = lax.dot_general(
        slot_member[...], back, (((0,), (0,)), ((), ())), preferred_element_type=F32
    )
    atom_out[...] = (updated[...].astype(F32) + lifted).astype(BF)


def adder_matrix(atom_counts, devices, rows, token_rows, row_tokens, col_tokens):
    position = lax.axis_index(AXES)
    slots = rows // FEWEST + 1
    ends = jnp.cumsum(atom_counts, dtype=jnp.int32)
    block = jnp.arange(devices, dtype=jnp.int32)
    base = jnp.sum((ends[None, :] <= (block * rows)[:, None]).astype(jnp.int32), axis=1)
    spot = jnp.arange(BLOCK, dtype=jnp.int32)
    is_slot = (spot >= token_rows) & (spot < token_rows + slots)
    token = jnp.where(is_slot[None, :], base[:, None] + (spot - token_rows)[None, :], -1)
    token = token.reshape(1, -1)
    place = jnp.arange(devices * BLOCK, dtype=jnp.int32)[None, :]
    line = jnp.arange(SLOTS, dtype=jnp.int32)[:, None]
    side = jnp.where(line == token_rows, position - 1, position + 1)
    edge = (line >= token_rows) & (line < token_rows + 2)
    fixed = jnp.where(
        edge,
        place == side * BLOCK + token_rows + slots,
        (place % BLOCK == line) & (line < token_rows),
    )
    first_row = lax.axis_index("row") * row_tokens
    first_col = lax.axis_index("col") * col_tokens
    lefts = token == (first_row + jnp.arange(row_tokens, dtype=jnp.int32))[:, None]
    rights = token == (first_col + jnp.arange(col_tokens, dtype=jnp.int32))[:, None]
    return jnp.concatenate([fixed, lefts, rights], axis=0).astype(BF)


def call(kernel, name, operands, outputs):
    vmem = pl.BlockSpec(memory_space=pltpu.VMEM)
    held = sum(math.prod(a.shape) * a.dtype.itemsize for a in operands + outputs)
    return pl.pallas_call(
        kernel,
        out_shape=outputs,
        in_specs=[vmem] * len(operands),
        out_specs=(vmem,) * len(outputs),
        compiler_params=pltpu.CompilerParams(vmem_limit_bytes=min(2 * held + SPARE, MOST)),
        name=name,
    )(*operands)


def per_device(
    atom_feats,
    key_starts,
    atom_counts,
    atom_gain,
    w_query,
    w_key,
    w_value,
    w_out,
    w_pool,
    w_back,
    pair_state,
    w_left,
    w_right,
    w_outer,
    pair_gain,
    w_gate,
    w_lift,
    w_drop,
):
    rows, width = atom_feats.shape
    devices = lax.axis_size(AXES)
    tokens = atom_counts.shape[0]
    channels = w_pool.shape[1]
    opm = w_left.shape[1]
    own_tokens = tokens // devices
    row_tokens, col_tokens, _ = pair_state.shape
    token_rows = own_tokens * channels // LANES
    across = [(i, i + 1) for i in range(1, devices - 1, 2)]
    neighbour = lax.ppermute(atom_feats, AXES, across + [(j, i) for i, j in across])
    sibling = lax.ppermute(atom_feats, AXES, [(i, i ^ 1) for i in range(devices)])
    tiles = channels // LANES

    def held(*shape, dtype=F32):
        return jax.ShapeDtypeStruct(shape, dtype)

    ready = call(
        ready_kernel,
        "ready",
        (
            atom_feats,
            sibling,
            key_starts[None],
            atom_counts[None],
            atom_counts.reshape(-1, LANES),
            atom_gain[None],
            pair_gain[None],
            w_query,
            w_key,
            w_value,
        ),
        (
            held(rows, width),
            held(2 * rows, 2 * width, dtype=BF),
            held(HEADS * rows, width, dtype=BF),
            held(HEADS * rows, 2 * rows),
            held(HEADS * rows, 1),
            held(rows, rows),
            held(devices * BLOCK, tiles * rows, dtype=BF),
            held(devices * BLOCK, LANES),
            held(devices * BLOCK, 2 * SLOTS, dtype=BF),
            held(SLOTS, rows, dtype=BF),
            held(SLOTS, LANES),
            held(SLOTS, LANES),
            held(SLOTS, LANES),
            held(SLOTS, LANES),
            held(1, width),
            held(1, LANES),
        ),
    )
    slot_member, slot_last, atom_gain_kept, pair_gain_kept = ready[9], ready[13], ready[14], ready[15]
    payload, updated, slot_back = call(
        atom_kernel,
        "atoms",
        (neighbour,)
        + tuple(ready[:13])
        + (atom_gain_kept, w_key, w_value, w_out, w_pool, w_back, w_left.T, w_right.T),
        (
            held(devices * BLOCK, LANES, dtype=BF),
            held(rows, width, dtype=BF),
            held(SLOTS, width),
        ),
    )
    counts_after, updated = lax.optimization_barrier((atom_counts, updated))
    arrived = lax.all_to_all(payload.reshape(devices, BLOCK, LANES), AXES, 0, 0)
    adder = adder_matrix(counts_after, devices, rows, token_rows, row_tokens, col_tokens)
    return call(
        pair_kernel,
        "pairs",
        (
            arrived.reshape(devices * BLOCK, LANES),
            adder,
            updated,
            slot_back,
            slot_last,
            slot_member,
            pair_state,
            w_outer.reshape(opm * opm, -1),
            pair_gain_kept,
            w_gate,
            w_lift,
            w_drop,
        ),
        (
            jax.ShapeDtypeStruct(atom_feats.shape, BF),
            jax.ShapeDtypeStruct((own_tokens, channels), BF),
            jax.ShapeDtypeStruct(pair_state.shape, BF),
        ),
    )


def solution(mesh):
    in_specs = (
        P(("row", "col"), None),
        P(("row", "col")),
        P(),
        P(),
        P(),
        P(),
        P(),
        P(),
        P(),
        P(),
        P("row", "col", None),
        P(),
        P(),
        P(),
        P(),
        P(),
        P(),
        P(),
    )
    out_specs = (P(("row", "col"), None), P(("row", "col"), None), P("row", "col", None))
    return jax.shard_map(
        per_device, mesh=mesh, in_specs=in_specs, out_specs=out_specs, check_vma=False
    )
```

time: 30.3 us -> 31.2 us (1.030)
  local copies, waits for them, and re-layouts: 2.77 us -> 4.53 us
  starting transfers between devices: 11.3 us -> 9.92 us
  Pallas kernels: 5.28 us -> 5.62 us
    unnamed x36, local copies, waits for them, and re-layouts: 2.57 us -> 4.33 us
    all_to_all x1, starting transfers between devices: 10.1 us -> 8.75 us  [per_device(): arrived = lax.all_to_all(payload.reshape(devices, BLOCK, LANES), AXES, 0, 0)]
    pallas_call x2 -> x3, Pallas kernels: 5.28 us -> 5.62 us  [call(): pl.pallas_call(kernel, out_shape=outputs, in_specs=[vmem] * len(operands)...]
  transfers between devices with their start and end apart: 3 -> 3, of which waited for: 1 -> 2; matrix products, arithmetic and copies ran while one was open for 3% -> 1% of each run, Pallas kernels for 0% -> 3%
where the time goes in v6:
time: 31.2 us; the launch traced here: 30.6 us
  starting transfers between devices  9.92 us (32%)
  waiting for transfers between devices  8.8 us (28%)
  Pallas kernels  5.62 us (18%)
  local copies, waits for them, and re-layouts  4.53 us (15%)
  between operations  0.9 us (3%)
  other arithmetic  0.83 us (3%)
    all_to_all x1, starting transfers between devices, per_device(): arrived = lax.all_to_all(payload.reshape(devices, BLOCK, LANES), AXES, 0, 0)  8.75 us
    all_to_all x1, waiting for transfers between devices, per_device(): arrived = lax.all_to_all(payload.reshape(devices, BLOCK, LANES), AXES, 0, 0)  8.69 us
    pallas_call x3, Pallas kernels, call(): pl.pallas_call(kernel, out_shape=outputs, in_specs=[vmem] * len(operands)...  5.62 us
    unnamed x36, local copies, waits for them, and re-layouts  4.33 us
    ppermute x1, starting transfers between devices, per_device(): lax.ppermute(atom_feats, AXES, across + [(j, i) for i, j in across])  0.65 us
  transfers between devices with their start and end apart: 3, of which 2 were waited for; matrix products, arithmetic and copies ran while one was open for 1% of the time, Pallas kernels for 3%

profile of v6, /device:TPU:0, one launch (start us, length us, event | category | flops | bytes accessed | tf_op | source)
XLA Modules:
  0.0 30.6 jit_solution(9448393639644326690)
XLA Ops:
  0.6 0.5 %collective-permute-start.1 = (bf16[64,128]{1,0:T(8,128)(2,1)}, bf16[64,128]{1,0:T(8,128)(2,1)S(1)}, u32[]{:S(2)}, u32[]{:S(2)}) collective-permute-start(bf16[64,128]{1,0:T(8,128)(2,1)} %own.1), channel_id=1, source_target_pairs={{0,1},{1,0},{2,3},{3,2},{4,5},{5,4},{6,7},{7,6},{8,9},{9,8},{10,11... | collective-permute-start | bytes 49160 | tf_op jit(solution)/shard_map/ppermute | solution.py:409
  1.1 0.7 %collective-permute-start = (bf16[64,128]{1,0:T(8,128)(2,1)}, bf16[64,128]{1,0:T(8,128)(2,1)S(1)}, u32[]{:S(2)}, u32[]{:S(2)}) collective-permute-start(bf16[64,128]{1,0:T(8,128)(2,1)} %own.1), channel_id=1, source_target_pairs={{1,2},{3,4},{5,6},{7,8},{9,10},{11,12},{13,14},{15,16},{17,18},{19... | collective-permute-start | bytes 49160 | tf_op jit(solution)/shard_map/ppermute | solution.py:408
  1.8 0.0 copy-start.17
  1.8 0.0 copy-start.14
  1.8 0.0 copy-start.15
  1.9 0.0 copy-start.16
  1.9 0.0 copy-start.2
  1.9 0.0 copy-start.1
  2.0 0.0 copy-start.7
  2.0 0.1 fusion
  2.1 0.1 collective-permute-done.1.sibling
  2.2 0.3 copy-done.17
  2.5 0.0 copy-done.14
  2.5 0.0 copy-done.15
  2.5 0.0 copy-done.16
  2.5 0.1 copy-done.2
  2.6 0.0 copy-done.1
  2.7 0.0 copy-start.10
  2.7 0.8 %copy-done.10 = bf16[128,128]{1,0:T(8,128)(2,1)S(1)} copy-done((bf16[128,128]{1,0:T(8,128)(2,1)S(1)}, bf16[128,128]{1,0:T(8,128)(2,1)}, u32[]{:S(2)}) %copy-start.10) | copy-done | bytes 32792
  3.4 0.7 %copy-done.13 = bf16[64,128]{1,0:T(8,128)(2,1)S(1)} copy-done((bf16[64,128]{1,0:T(8,128)(2,1)S(1)}, bf16[64,128]{1,0:T(8,128)(2,1)}, u32[]{:S(2)}) %copy-start.13) | copy-done | bytes 16408
  4.1 0.8 %ready.1 = (f32[64,128]{1,0:T(8,128)S(1)}, bf16[128,256]{1,0:T(8,128)(2,1)S(1)}, bf16[256,128]{1,0:T(8,128)(2,1)S(1)}, f32[256,128]{1,0:T(8,128)S(1)}, f32[256,1...) custom-call(bf16[64,128]{1,0:T(8,128)(2,1)S(1)} %copy-done.13, ...), custom_call_target="tpu_custom_call" | custom-call | tf_op jit(solution)/shard_map/ready/pallas_call | solution.py:369
  5.0 0.0 copy-start.11
  5.0 0.0 collective-permute-done.neighbour
  5.0 0.0 copy-done.7
  5.0 0.0 copy-done.9
  5.0 0.7 %copy-done.11 = bf16[384,32]{0,1:T(8,128)(2,1)S(1)} copy-done((bf16[384,32]{0,1:T(8,128)(2,1)S(1)}, bf16[384,32]{0,1:T(8,128)(2,1)}, u32[]{:S(2)}) %copy-start.11) | copy-done | bytes 24600
  5.7 0.9 %copy-done.8 = bf16[384,128]{1,0:T(8,128)(2,1)S(1)} copy-done((bf16[384,128]{1,0:T(8,128)(2,1)S(1)}, bf16[384,128]{1,0:T(8,128)(2,1)}, u32[]{:S(2)}) %copy-start.8) | copy-done | bytes 98328
  6.6 0.7 %copy-done.12 = bf16[384,32]{0,1:T(8,128)(2,1)S(1)} copy-done((bf16[384,32]{0,1:T(8,128)(2,1)S(1)}, bf16[384,32]{0,1:T(8,128)(2,1)}, u32[]{:S(2)}) %copy-start.12) | copy-done | bytes 24600
  7.4 2.2 %atoms.1 = (bf16[768,128]{1,0:T(8,128)(2,1)}, bf16[64,128]{1,0:T(8,128)(2,1)S(1)}, f32[16,128]{1,0:T(8,128)S(1)}) custom-call(bf16[64,128]{1,0:T(8,128)(2,1)S(1)} %collective-permute-done.neighbour, f32[64,128]{1,0:T(8,128)S(1)} %get-tuple-element.24.own_float, bf16[128,256]{1,0:T(8,128)(2,1)S(1)} %get-tuple-element.25.keyval, ...), custom_call_target="tpu_custom_call" | custom-call | tf_op jit(solution)/shard_map/atoms/pallas_call | solution.py:369
  9.6 0.1 copy.23
  9.7 0.2 reduce-window.8
  9.8 0.1 reduce
  10.0 0.2 convert_reduce_fusion
  10.1 0.1 add_select_fusion
  10.2 0.1 select_n.40
  10.3 0.0 copy-start
  10.3 0.0 copy-start.4
  10.3 8.7 %all-to-all-start = ((bf16[32,24,128]{2,1,0:T(8,128)(2,1)}), bf16[32,24,128]{2,1,0:T(8,128)(2,1)S(1)}, u32[]{:S(2)}, u32[]{:S(2)}) async-start(bf16[32,24,128]{2,1,0:T(8,128)(2,1)} %bitcast.6), calls=%async_computation | async-start | bytes 393216 | tf_op jit(solution)/shard_map/all_to_all | solution.py:463
  19.1 0.0 copy-start.3
  19.1 0.1 broadcast_compare_fusion.1
  19.2 0.1 broadcast_compare_fusion
  19.3 8.7 %all-to-all-done = bf16[32,24,128]{2,1,0:T(8,128)(2,1)S(1)} async-done(((bf16[32,24,128]{2,1,0:T(8,128)(2,1)}), bf16[32,24,128]{2,1,0:T(8,128)(2,1)S(1)}, u32[]{:S(2)}, u32[]{:S(2)}) %all-to-all-start) | async-done | bytes 196640 | tf_op jit(solution)/shard_map/all_to_all | solution.py:463
  28.0 0.0 copy-done.6
  28.0 0.0 copy-done.5
  28.0 0.0 copy-done
  28.0 0.0 copy-done.4
  28.0 0.0 copy-done.3
  28.0 2.6 %pairs.1 = (bf16[64,128]{1,0:T(8,128)(2,1)}, bf16[4,384]{1,0:T(4,128)(2,1)}, bf16[16,32,128]{2,1,0:T(8,128)(2,1)}) custom-call(bf16[768,128]{1,0:T(8,128)(2,1)S(1)} %bitcast.10, bf16[64,768]{1,0:T(8,128)(2,1)S(1)} %add_convert_fusion.adder, bf16[64,128]{1,0:T(8,128)(2,1)S(1)} %get-tuple-element.41.updated, f32[16,128]{1,0:T(8,128)S(1)} %get-tuple-element.42.slot_back, ...), custom_call_target="tpu_custom_call" | custom-call | tf_op jit(solution)/shard_map/pairs/pallas_call | solution.py:369
  (15 shorter events, 0.1 us)
Async XLA Ops:
  0.6 1.6 %collective-permute-start.1 = (bf16[64,128]{1,0:T(8,128)(2,1)}, bf16[64,128]{1,0:T(8,128)(2,1)S(1)}, u32[]{:S(2)}, u32[]{:S(2)}) collective-permute-start(bf16[64,128]{1,0:T(8,128)(2,1)} %own.1), channel_id=1, source_target_pairs={{0,1},{1,0},{2,3},{3,2},{4,5},{5,4},{6,7},{7,6},{8,9},{9,8},{10,11... | collective-permute-start | bytes 49160 | tf_op jit(solution)/shard_map/ppermute | solution.py:409
  1.1 3.8 %collective-permute-start = (bf16[64,128]{1,0:T(8,128)(2,1)}, bf16[64,128]{1,0:T(8,128)(2,1)S(1)}, u32[]{:S(2)}, u32[]{:S(2)}) collective-permute-start(bf16[64,128]{1,0:T(8,128)(2,1)} %own.1), channel_id=1, source_target_pairs={{1,2},{3,4},{5,6},{7,8},{9,10},{11,12},{13,14},{15,16},{17,18},{19... | collective-permute-start | bytes 49160 | tf_op jit(solution)/shard_map/ppermute | solution.py:408
  1.8 0.7 %copy-start.17 = (f32[128]{0:T(128)S(1)}, f32[128]{0:T(128)}, u32[]{:S(2)}) copy-start(f32[128]{0:T(128)} %param.32) | copy-start | bytes 1540
  1.8 0.7 %copy-start.14 = (s32[128]{0:T(128)S(1)}, s32[128]{0:T(128)}, u32[]{:S(2)}) copy-start(s32[128]{0:T(128)} %param.20) | copy-start | bytes 1540
  1.8 0.7 %copy-start.15 = (s32[2]{0:T(128)S(1)}, s32[2]{0:T(128)}, u32[]{:S(2)}) copy-start(s32[2]{0:T(128)} %param.19) | copy-start | bytes 28
  1.9 0.7 %copy-start.16 = (f32[128]{0:T(128)S(1)}, f32[128]{0:T(128)}, u32[]{:S(2)}) copy-start(f32[128]{0:T(128)} %param.21) | copy-start | bytes 1540
  1.9 0.8 %copy-start.2 = (bf16[128,128]{1,0:T(8,128)(2,1)S(1)}, bf16[128,128]{1,0:T(8,128)(2,1)}, u32[]{:S(2)}) copy-start(bf16[128,128]{1,0:T(8,128)(2,1)} %w_value.3) | copy-start | bytes 98308
  1.9 0.8 %copy-start.1 = (bf16[128,128]{1,0:T(8,128)(2,1)S(1)}, bf16[128,128]{1,0:T(8,128)(2,1)}, u32[]{:S(2)}) copy-start(bf16[128,128]{1,0:T(8,128)(2,1)} %w_key.3) | copy-start | bytes 98308
  2.0 3.0 %copy-start.7 = (bf16[128,384]{1,0:T(8,128)(2,1)S(1)}, bf16[128,384]{1,0:T(8,128)(2,1)}, u32[]{:S(2)}) copy-start(bf16[128,384]{1,0:T(8,128)(2,1)} %w_pool.1) | copy-start | bytes 294916
  2.7 0.8 %copy-start.10 = (bf16[128,128]{1,0:T(8,128)(2,1)S(1)}, bf16[128,128]{1,0:T(8,128)(2,1)}, u32[]{:S(2)}) copy-start(bf16[128,128]{1,0:T(8,128)(2,1)} %w_query.1) | copy-start | bytes 98308
  3.4 0.7 %copy-start.13 = (bf16[64,128]{1,0:T(8,128)(2,1)S(1)}, bf16[64,128]{1,0:T(8,128)(2,1)}, u32[]{:S(2)}) copy-start(bf16[64,128]{1,0:T(8,128)(2,1)} %own.1) | copy-start | bytes 49156
  4.1 0.9 %copy-start.9 = (bf16[128,128]{1,0:T(8,128)(2,1)S(1)}, bf16[128,128]{1,0:T(8,128)(2,1)}, u32[]{:S(2)}) copy-start(bf16[128,128]{1,0:T(8,128)(2,1)} %w_out.1) | copy-start | bytes 98308
  5.0 0.7 %copy-start.11 = (bf16[384,32]{0,1:T(8,128)(2,1)S(1)}, bf16[384,32]{0,1:T(8,128)(2,1)}, u32[]{:S(2)}) copy-start(bf16[384,32]{0,1:T(8,128)(2,1)} %param.29) | copy-start | bytes 73732
  5.7 0.9 %copy-start.8 = (bf16[384,128]{1,0:T(8,128)(2,1)S(1)}, bf16[384,128]{1,0:T(8,128)(2,1)}, u32[]{:S(2)}) copy-start(bf16[384,128]{1,0:T(8,128)(2,1)} %w_back.1) | copy-start | bytes 294916
  6.6 0.7 %copy-start.12 = (bf16[384,32]{0,1:T(8,128)(2,1)S(1)}, bf16[384,32]{0,1:T(8,128)(2,1)}, u32[]{:S(2)}) copy-start(bf16[384,32]{0,1:T(8,128)(2,1)} %param.30) | copy-start | bytes 73732
  9.7 18.3 %copy-start.6 = (bf16[512,128]{1,0:T(8,128)(2,1)S(1)}, bf16[512,128]{1,0:T(8,128)(2,1)}, u32[]{:S(2)}) copy-start(bf16[512,128]{1,0:T(8,128)(2,1)} %w_drop.1) | copy-start | bytes 393220
  9.8 18.1 %copy-start.5 = (bf16[128,512]{1,0:T(8,128)(2,1)S(1)}, bf16[128,512]{1,0:T(8,128)(2,1)}, u32[]{:S(2)}) copy-start(bf16[128,512]{1,0:T(8,128)(2,1)} %w_lift.1) | copy-start | bytes 393220
  10.3 17.7 %copy-start = (bf16[32,32,128]{2,1,0:T(8,128)(2,1)S(1)}, bf16[32,32,128]{2,1,0:T(8,128)(2,1)}, u32[]{:S(2)}) copy-start(bf16[32,32,128]{2,1,0:T(8,128)(2,1)} %param.31) | copy-start | bytes 786436
  10.3 17.7 %copy-start.4 = (bf16[128,512]{1,0:T(8,128)(2,1)S(1)}, bf16[128,512]{1,0:T(8,128)(2,1)}, u32[]{:S(2)}) copy-start(bf16[128,512]{1,0:T(8,128)(2,1)} %w_gate.1) | copy-start | bytes 393220
  10.3 17.6 %all-to-all-start = ((bf16[32,24,128]{2,1,0:T(8,128)(2,1)}), bf16[32,24,128]{2,1,0:T(8,128)(2,1)S(1)}, u32[]{:S(2)}, u32[]{:S(2)}) async-start(bf16[32,24,128]{2,1,0:T(8,128)(2,1)} %bitcast.6), calls=%async_computation | async-start | bytes 393216 | tf_op jit(solution)/shard_map/all_to_all | solution.py:463
  19.1 8.9 %copy-start.3 = (bf16[16,32,128]{2,1,0:T(8,128)(2,1)S(1)}, bf16[16,32,128]{2,1,0:T(8,128)(2,1)}, u32[]{:S(2)}) copy-start(bf16[16,32,128]{2,1,0:T(8,128)(2,1)} %pair_state.1) | copy-start | bytes 393220

commit v7 on v6

v7 whole, which is shorter than its diff:
```python
import math

import jax
import jax.numpy as jnp
from jax import lax
from jax.experimental import pallas as pl
from jax.experimental.pallas import tpu as pltpu
from jax.sharding import PartitionSpec as P

HEADS = 4
QB = 32
KW = 128
EPSILON = 1e-05
HALF = KW // 2
FEWEST = 8
LANES = 128
SLOTS = 16
BLOCK = 24
DESTS = 32
PAIR_ROWS = 8
MASKED = -1e30
SPARE = 12 << 20
MOST = 60 << 20
LOG2E = 1.4426950408889634
AXES = ("row", "col")
BF = jnp.bfloat16
F32 = jnp.float32


def layer_norm(values, gain):
    mean_value = jnp.mean(values, axis=-1, keepdims=True)
    centred = values - mean_value
    variance = jnp.mean(centred * centred, axis=-1, keepdims=True)
    return centred * lax.rsqrt(variance + EPSILON) * gain


def dot(a, b):
    return jnp.dot(a, b, preferred_element_type=F32)


def dot_t(a, b):
    return lax.dot_general(a, b, (((1,), (1,)), ((), ())), preferred_element_type=F32)


def iota(shape, axis):
    return lax.broadcasted_iota(jnp.int32, shape, axis)


def flag(mask):
    return jnp.where(mask, 1.0, 0.0).astype(BF)


def place():
    return lax.axis_index("row") * lax.axis_size("col") + lax.axis_index("col")


def repeat(count, step):
    if count <= 8:
        for at in range(count):
            step(at)
    else:

        def body(at, carry):
            step(at)
            return carry

        lax.fori_loop(0, count, body, 0)


def span(at, size):
    if isinstance(at, int):
        return pl.ds(at * size, size)
    return pl.ds(pl.multiple_of(at * size, size), size)


def ready_kernel(
    own_far,
    starts_far,
    counts_far,
    folded_far,
    atom_gain_far,
    pair_gain_far,
    w_query_far,
    w_key_far,
    w_value_far,
    w_out_far,
    w_pool_far,
    w_back_far,
    w_left_far,
    w_right_far,
    own_float,
    keyval,
    stacked,
    scores,
    top,
    far_bias,
    picks,
    row_scale,
    member,
    slot_scale,
    before,
    goes_on,
    last,
    adder,
    atom_gain,
    pair_gain,
    w_kv,
    w_out,
    w_pool,
    w_back,
    w_sides,
    own,
    key_starts,
    counts,
    counts_folded,
    w_query,
    ends,
    arrivals,
):
    rows, width = own.shape
    tokens = counts.shape[1]
    opm = w_left_far.shape[0]
    pairs = (
        (counts_far, counts),
        (folded_far, counts_folded),
        (own_far, own),
        (starts_far, key_starts),
        (atom_gain_far, atom_gain),
        (w_query_far, w_query),
        (w_key_far, w_kv.at[:, :width]),
        (w_value_far, w_kv.at[:, width:]),
        (pair_gain_far, pair_gain),
        (w_out_far, w_out),
        (w_pool_far, w_pool),
        (w_back_far, w_back),
        (w_left_far, w_sides.at[:opm]),
        (w_right_far, w_sides.at[opm : 2 * opm]),
    )
    copies = [pltpu.make_async_copy(a, b, arrivals.at[k]) for k, (a, b) in enumerate(pairs)]
    for copy in copies:
        copy.start()

    tiles = picks.shape[1] // rows
    devices = picks.shape[0] // BLOCK
    atoms = rows * devices
    own_tokens = tokens // devices
    token_rows = own_tokens * tiles
    lead = BLOCK - token_rows
    slots = rows // FEWEST + 1
    position = place()
    first = position * rows
    even = position % 2 == 0
    first_float = first.astype(F32)
    w_sides[2 * opm :, :] = jnp.zeros((LANES - 2 * opm, tiles * LANES), BF)

    for copy in copies[:2]:
        copy.wait()
    counts_wide = jnp.broadcast_to(counts[...].astype(F32), (tiles * rows, tokens)).astype(BF)
    counts_lane = counts_wide[:LANES]
    folded = counts_folded[...].astype(F32).astype(BF)
    upper = flag(iota((LANES, LANES), 0) <= iota((LANES, LANES), 1))
    lower = flag(iota((LANES, LANES), 1) <= iota((LANES, LANES), 0))
    within = dot(folded, upper)
    whole = dot(folded, jnp.ones((LANES, LANES), BF))
    base = jnp.zeros((1, 1), F32)
    passed = jnp.zeros((1, LANES), F32)
    for fold in range(folded.shape[0]):
        ended = within[fold : fold + 1] + passed <= first_float
        base = base + jnp.sum(jnp.where(ended, 1.0, 0.0), axis=1, keepdims=True)
        part = slice(fold * LANES, (fold + 1) * LANES)
        ends[part, :] = passed + dot_t(lower, counts_lane[:, part])
        passed = passed + whole[fold : fold + 1]

    token_lane = iota((SLOTS, tokens), 1).astype(F32)
    slot_token = iota((SLOTS, tokens), 0).astype(F32) + base
    slot_end = dot_t(flag(token_lane <= slot_token), counts_lane)
    slot_start = dot_t(flag(token_lane < slot_token), counts_lane)
    atom_lane = iota((SLOTS, rows), 1).astype(F32) + first_float
    member[...] = flag((atom_lane >= slot_start[:, :rows]) & (atom_lane < slot_end[:, :rows]))
    slot_scale[...] = 1.0 / jnp.maximum(slot_end - slot_start, 1.0)
    last_atom = first_float + (rows - 1)
    is_last = jnp.where((slot_start <= last_atom) & (slot_end > last_atom), 1.0, 0.0)
    last[...] = is_last
    goes_on[...] = is_last * jnp.where(slot_end > first_float + rows, 1.0, 0.0)
    is_first = iota((SLOTS, LANES), 0) == 0
    before[...] = jnp.where(is_first & (slot_start < first_float), 1.0, 0.0)

    def rows_step(at):
        def spread(lanes, axis):
            return iota((DESTS, BLOCK, lanes), axis).reshape(DESTS * BLOCK, lanes)

        here = span(at, DESTS * BLOCK)
        token_at = iota((DESTS * BLOCK, tokens), 1)
        turn = spread(tokens, 1) - lead
        row_token = (spread(tokens, 0) + at * DESTS) * own_tokens + turn % own_tokens
        row_end = dot_t(flag(token_at <= row_token), counts_wide)
        row_start = dot_t(flag(token_at < row_token), counts_wide)
        lanes = tiles * rows
        lane = iota((DESTS * BLOCK, lanes), 1)
        atom = (lane % rows + first).astype(F32)
        turn = spread(lanes, 1) - lead
        tile_fits = (turn >= 0) & (turn // own_tokens == lane // rows)
        picks[here, :] = flag(tile_fits & (atom >= row_start) & (atom < row_end))
        row_scale[here, :] = 1.0 / jnp.maximum(row_end - row_start, 1.0)[:, :LANES]

    repeat(devices // DESTS, rows_step)

    row_tokens = tokens // lax.axis_size("row")
    col_tokens = tokens // lax.axis_size("col")
    first_row = lax.axis_index("row") * row_tokens
    first_col = lax.axis_index("col") * col_tokens

    def adder_step(at):
        here = span(at, LANES)
        spot_lane = iota((1, LANES), 1) + at * LANES
        block = spot_lane // BLOCK
        spot = spot_lane % BLOCK
        edge = (block * rows).astype(F32)
        tally = jnp.zeros((1, LANES), F32)
        for fold in range(tokens // LANES):
            ended = jnp.where(ends[fold * LANES : (fold + 1) * LANES, :] <= edge, 1.0, 0.0)
            tally = tally + jnp.sum(ended, axis=0, keepdims=True)
        token = jnp.where(spot < slots, tally.astype(jnp.int32) + spot, -1)
        line = iota((SLOTS, LANES), 0)
        wanted = jnp.where(
            line == token_rows,
            (position - 1) * BLOCK + slots + 1,
            jnp.where(line == token_rows + 1, (position + 1) * BLOCK + slots, -1),
        )
        fixed = (spot_lane == wanted) | ((line < token_rows) & (spot == line + lead))
        lefts = token == iota((row_tokens, LANES), 0) + first_row
        rights = token == iota((col_tokens, LANES), 0) + first_col
        adder[:SLOTS, here] = flag(fixed)
        adder[SLOTS : SLOTS + row_tokens, here] = flag(lefts)
        adder[SLOTS + row_tokens :, here] = flag(rights)

    repeat(devices * BLOCK // LANES, adder_step)

    for copy in copies[2:8]:
        copy.wait()
    raw = own[...].astype(F32)
    own_float[...] = raw
    normed = layer_norm(raw, atom_gain[...]).astype(BF)
    near = dot(normed, w_kv[...]).astype(BF)
    keyval[...] = near
    query = dot(normed, w_query[...]).astype(BF)
    head_of = iota((1, width), 1) // (width // HEADS)
    heads = jnp.concatenate([query * flag(head_of == h) for h in range(HEADS)], axis=0)
    stacked[...] = heads
    near_index = first + iota((1, rows), 1)
    far_lane = iota((1, 2 * rows), 1)
    is_low = (far_lane < rows) != even
    far_index = first + far_lane % rows + jnp.where(is_low, -rows, rows)
    near_bias, bias = [], []
    for e in range(rows // QB):
        low = key_starts[0:1, e : e + 1]
        seen = (near_index >= low) & (near_index < low + KW)
        near_bias.append(jnp.broadcast_to(jnp.where(seen, 0.0, MASKED), (QB, rows)))
        seen = (far_index >= low) & (far_index < low + KW)
        seen = seen & (far_index >= 0) & (far_index < atoms)
        bias.append(jnp.broadcast_to(jnp.where(seen, 0.0, MASKED), (QB, 2 * rows)))
    far_bias[...] = jnp.concatenate(bias, axis=0)
    raw_scores = dot_t(heads, near[:, :width]) + jnp.concatenate(near_bias * HEADS, axis=0)
    scores[...] = raw_scores
    top[...] = jnp.max(raw_scores, axis=-1, keepdims=True)
    for copy in copies[8:]:
        copy.wait()


def atom_kernel(
    neighbour,
    sibling,
    own_float,
    keyval,
    stacked,
    scores,
    top,
    far_bias,
    picks,
    row_scale,
    member,
    slot_scale,
    before,
    goes_on,
    atom_gain,
    w_kv,
    w_out,
    w_pool,
    w_back,
    w_sides,
    payload,
    updated,
    slot_back,
):
    rows, width = own_float.shape
    tiles = w_pool.shape[1] // LANES
    devices = payload.shape[0] // BLOCK
    slots = rows // FEWEST + 1
    raw = jnp.concatenate([sibling[...], neighbour[...]], axis=0).astype(F32)
    normed = layer_norm(raw, atom_gain[...]).astype(BF)
    far = dot(normed, w_kv[...]).astype(BF)
    far_scores = dot_t(stacked[...], far[:, :width])
    far_scores = far_scores + jnp.concatenate([far_bias[...]] * HEADS, axis=0)
    most = jnp.maximum(top[...], jnp.max(far_scores, axis=-1, keepdims=True))
    scale = (width // HEADS) ** (-0.5) * LOG2E
    raised = jnp.concatenate(
        [
            jnp.exp2((far_scores - most) * scale).astype(BF),
            jnp.exp2((scores[...] - most) * scale).astype(BF),
        ],
        axis=1,
    )
    values = jnp.concatenate([far[:, width:], keyval[:, width:]], axis=0)
    mixed = dot(raised, jnp.concatenate([values, jnp.ones((3 * rows, width), BF)], axis=1))
    head_of = iota((1, width), 1) // (width // HEADS)
    head_mask = [(head_of == h).astype(F32) for h in range(HEADS)]
    total = sum(mixed[h * rows : (h + 1) * rows, :width] * head_mask[h] for h in range(HEADS))
    weight = sum(mixed[h * rows : (h + 1) * rows, width:] * head_mask[h] for h in range(HEADS))
    attended = (total / weight).astype(BF)
    fresh = (own_float[...] + dot(attended, w_out[...])).astype(BF)
    updated[...] = fresh
    feature = jnp.maximum(dot(fresh, w_pool[...]), 0.0).astype(BF)
    feature_tiles = jnp.concatenate(
        [feature[:, k * LANES : (k + 1) * LANES] for k in range(tiles)], axis=0
    )
    slot_single = (
        dot(member[...], feature) * jnp.concatenate([slot_scale[...]] * tiles, axis=1)
    ).astype(BF)
    sides = dot_t(slot_single, w_sides[...])
    backs = dot(slot_single, w_back[...])
    slot_back[...] = backs
    to_before = jnp.sum(backs * before[...], axis=0, keepdims=True)
    to_after = jnp.sum(backs * goes_on[...], axis=0, keepdims=True)
    spot = iota((SLOTS, LANES), 0)
    shared = jnp.where(
        spot < slots,
        sides,
        jnp.where(spot == slots, to_before, jnp.where(spot == slots + 1, to_after, 0.0)),
    )
    shared = jnp.concatenate([shared, jnp.zeros((BLOCK - SLOTS, LANES), F32)], axis=0)

    def send_step(at):
        here = span(at, DESTS * BLOCK)
        singles = dot(picks[here, :], feature_tiles) * row_scale[here, :]
        singles = singles.reshape(DESTS, BLOCK, LANES) + shared[None]
        payload[here, :] = singles.reshape(DESTS * BLOCK, LANES).astype(BF)

    repeat(devices // DESTS, send_step)


def pair_kernel(
    arrived,
    adder,
    updated,
    slot_back,
    slot_last,
    slot_member,
    pair_state,
    w_outer,
    pair_gain,
    w_gate,
    w_lift,
    w_drop,
    atom_out,
    token_single,
    pair_far,
    pair_out,
    leaving,
):
    row_tokens, col_tokens, pair_width = pair_state.shape
    own_tokens, channels = token_single.shape
    tiles = channels // LANES
    token_rows = own_tokens * tiles
    opm = math.isqrt(w_outer.shape[0])
    added = dot(adder[...], arrived[...])
    half_gate = w_gate[...] * jnp.asarray(0.5, BF)
    left = added[SLOTS : SLOTS + row_tokens, :opm].astype(BF)
    right = added[SLOTS + row_tokens :, opm : 2 * opm].astype(BF)
    product_lane = iota((opm, opm * opm), 1)
    unit = iota((opm, opm * opm), 0)
    left_wide = dot(left, flag(product_lane // opm == unit))
    right_wide = dot(right, flag(product_lane % opm == unit))

    def pair_rows(lefts, here):
        products = jnp.concatenate(
            [(lefts[i : i + 1, :] * right_wide).astype(BF) for i in range(PAIR_ROWS)], axis=0
        )
        flat = pair_state[pl.ds(here, PAIR_ROWS)].reshape(PAIR_ROWS * col_tokens, pair_width)
        summed = flat.astype(F32) + dot(products, w_outer[...])
        normed = layer_norm(summed, pair_gain[...]).astype(BF)
        gate = dot(normed, half_gate)
        lift = dot(normed, w_lift[...])
        hidden = (gate * lift * (1.0 + jnp.tanh(gate))).astype(BF)
        result = (summed + dot(hidden, w_drop[...])).astype(BF)
        pair_out[pl.ds(here, PAIR_ROWS)] = result.reshape(PAIR_ROWS, col_tokens, pair_width)

    token_single[...] = jnp.concatenate(
        [added[k * own_tokens : (k + 1) * own_tokens] for k in range(tiles)], axis=1
    ).astype(BF)
    spot = iota((SLOTS, LANES), 0)
    from_before = jnp.where(spot == 0, added[token_rows : token_rows + 1], 0.0)
    from_after = slot_last[...] * added[token_rows + 1 : token_rows + 2]
    back = (slot_back[...] + from_before + from_after).astype(BF)
    lifted = lax.dot_general(
        slot_member[...], back, (((0,), (0,)), ((), ())), preferred_element_type=F32
    )
    atom_out[...] = (updated[...].astype(F32) + lifted).astype(BF)

    copies = []
    for step in range(row_tokens // PAIR_ROWS):
        here = step * PAIR_ROWS
        pair_rows(left_wide[here : here + PAIR_ROWS], here)
        part = pl.ds(here, PAIR_ROWS)
        copies.append(
            pltpu.make_async_copy(pair_out.at[part], pair_far.at[part], leaving.at[step])
        )
        copies[-1].start()
    for copy in copies:
        copy.wait()


def call(kernel, name, operands, outputs, far=(), out_far=(), scratch=()):
    near_spec = pl.BlockSpec(memory_space=pltpu.VMEM)
    far_spec = pl.BlockSpec(memory_space=pltpu.HBM)
    held = sum(math.prod(a.shape) * a.dtype.itemsize for a in operands + outputs)
    return pl.pallas_call(
        kernel,
        out_shape=outputs,
        in_specs=[far_spec] * len(far) + [near_spec] * len(operands),
        out_specs=tuple(far_spec if k in out_far else near_spec for k in range(len(outputs))),
        scratch_shapes=scratch,
        compiler_params=pltpu.CompilerParams(vmem_limit_bytes=min(2 * held + SPARE, MOST)),
        name=name,
    )(*[pltpu.with_memory_space_constraint(a, pltpu.HBM) for a in far], *operands)


def per_device(
    atom_feats,
    key_starts,
    atom_counts,
    atom_gain,
    w_query,
    w_key,
    w_value,
    w_out,
    w_pool,
    w_back,
    pair_state,
    w_left,
    w_right,
    w_outer,
    pair_gain,
    w_gate,
    w_lift,
    w_drop,
):
    rows, width = atom_feats.shape
    devices = lax.axis_size(AXES)
    tokens = atom_counts.shape[0]
    channels = w_pool.shape[1]
    opm = w_left.shape[1]
    own_tokens = tokens // devices
    row_tokens, col_tokens, _ = pair_state.shape
    tiles = channels // LANES
    across = [(i, i + 1) for i in range(1, devices - 1, 2)]
    neighbour = lax.ppermute(atom_feats, AXES, across + [(j, i) for i, j in across])
    sibling = lax.ppermute(atom_feats, AXES, [(i, i ^ 1) for i in range(devices)])

    def held(*shape, dtype=F32):
        return jax.ShapeDtypeStruct(shape, dtype)

    counts_folded = atom_counts.reshape(-1, LANES)
    ready = call(
        ready_kernel,
        "ready",
        (),
        (
            held(rows, width),
            held(rows, 2 * width, dtype=BF),
            held(HEADS * rows, width, dtype=BF),
            held(HEADS * rows, rows),
            held(HEADS * rows, 1),
            held(rows, 2 * rows),
            held(devices * BLOCK, tiles * rows, dtype=BF),
            held(devices * BLOCK, LANES),
            held(SLOTS, rows, dtype=BF),
            held(SLOTS, LANES),
            held(SLOTS, LANES),
            held(SLOTS, LANES),
            held(SLOTS, LANES),
            held(SLOTS + row_tokens + col_tokens, devices * BLOCK, dtype=BF),
            held(1, width),
            held(1, LANES),
            held(width, 2 * width, dtype=BF),
            held(width, width, dtype=BF),
            held(width, channels, dtype=BF),
            held(channels, width, dtype=BF),
            held(LANES, channels, dtype=BF),
        ),
        far=(
            atom_feats,
            key_starts[None],
            atom_counts[None],
            counts_folded,
            atom_gain[None],
            pair_gain[None],
            w_query,
            w_key,
            w_value,
            w_out,
            w_pool,
            w_back,
            w_left.T,
            w_right.T,
        ),
        scratch=(
            pltpu.VMEM((rows, width), BF),
            pltpu.VMEM((1, key_starts.shape[0]), jnp.int32),
            pltpu.VMEM((1, tokens), jnp.int32),
            pltpu.VMEM(counts_folded.shape, jnp.int32),
            pltpu.VMEM((width, width), BF),
            pltpu.VMEM((tokens, LANES), F32),
            pltpu.SemaphoreType.DMA((14,)),
        ),
    )
    (
        own_float,
        keyval,
        stacked,
        scores,
        top,
        far_bias,
        picks,
        row_scale,
        member,
        slot_scale,
        before,
        goes_on,
        last,
        adder,
        atom_gain_kept,
        pair_gain_kept,
        *kept,
    ) = ready
    payload, updated, slot_back = call(
        atom_kernel,
        "atoms",
        (
            neighbour,
            sibling,
            own_float,
            keyval,
            stacked,
            scores,
            top,
            far_bias,
            picks,
            row_scale,
            member,
            slot_scale,
            before,
            goes_on,
            atom_gain_kept,
            *kept,
        ),
        (
            held(devices * BLOCK, LANES, dtype=BF),
            held(rows, width, dtype=BF),
            held(SLOTS, width),
        ),
    )
    arrived = lax.all_to_all(payload.reshape(devices, BLOCK, LANES), AXES, 0, 0)
    opm = w_left.shape[1]
    return call(
        pair_kernel,
        "pairs",
        (
            arrived.reshape(devices * BLOCK, LANES),
            adder,
            updated,
            slot_back,
            last,
            member,
            pair_state,
            w_outer.reshape(opm * opm, -1),
            pair_gain_kept,
            w_gate,
            w_lift,
            w_drop,
        ),
        (
            held(rows, width, dtype=BF),
            held(own_tokens, channels, dtype=BF),
            held(*pair_state.shape, dtype=BF),
        ),
        out_far=(2,),
        scratch=(
            pltpu.VMEM(pair_state.shape, BF),
            pltpu.SemaphoreType.DMA((row_tokens // PAIR_ROWS,)),
        ),
    )


def solution(mesh):
    in_specs = (
        P(("row", "col"), None),
        P(("row", "col")),
        P(),
        P(),
        P(),
        P(),
        P(),
        P(),
        P(),
        P(),
        P("row", "col", None),
        P(),
        P(),
        P(),
        P(),
        P(),
        P(),
        P(),
    )
    out_specs = (P(("row", "col"), None), P(("row", "col"), None), P("row", "col", None))
    return jax.shard_map(
        per_device, mesh=mesh, in_specs=in_specs, out_specs=out_specs, check_vma=False
    )
```

time: 31.2 us -> 27.2 us (0.87)
  blocking collectives: 0 us -> 14.4 us
  waiting for transfers between devices: 8.8 us -> 0.01 us
  starting transfers between devices: 9.92 us -> 5.03 us
  local copies, waits for them, and re-layouts: 4.53 us -> 0.03 us
  Pallas kernels: 5.62 us -> 6.71 us
  other arithmetic: 0.83 us -> 0 us
    all_to_all x0 -> x1, blocking collectives: none -> 14.4 us  [per_device(): arrived = lax.all_to_all(payload.reshape(devices, BLOCK, LANES), AXES, 0, 0)]
    all_to_all x1 -> x0, starting transfers between devices: 8.75 us -> none  [per_device(): arrived = lax.all_to_all(payload.reshape(devices, BLOCK, LANES), AXES, 0, 0)]
    all_to_all x1 -> x0, waiting for transfers between devices: 8.69 us -> none  [per_device(): arrived = lax.all_to_all(payload.reshape(devices, BLOCK, LANES), AXES, 0, 0)]
    unnamed x36 -> x10, local copies, waits for them, and re-layouts: 4.33 us -> 0.03 us
    ppermute x1, starting transfers between devices: 0.52 us -> 4.36 us  [per_device(): lax.ppermute(atom_feats, AXES, [(i, i ^ 1) for i in range(devices)])]
    pallas_call x3, Pallas kernels: 5.62 us -> 6.71 us  [call(): pl.pallas_call(kernel, out_shape=outputs, in_specs=[far_spec] * len(far)...]
  transfers between devices with their start and end apart: 3 -> 2, of which waited for: 2 -> 0; matrix products, arithmetic and copies ran while one was open for 1% -> 0% of each run, Pallas kernels for 3% -> 8%
where the time goes in v7:
time: 27.2 us; the launch traced here: 26.9 us
  blocking collectives  14.4 us (53%)
  Pallas kernels  6.71 us (25%)
  starting transfers between devices  5.03 us (18%)
  between operations  0.73 us (3%)
    all_to_all x1, blocking collectives, per_device(): arrived = lax.all_to_all(payload.reshape(devices, BLOCK, LANES), AXES, 0, 0)  14.4 us
    pallas_call x3, Pallas kernels, call(): pl.pallas_call(kernel, out_shape=outputs, in_specs=[far_spec] * len(far)...  6.71 us
    ppermute x1, starting transfers between devices, per_device(): lax.ppermute(atom_feats, AXES, [(i, i ^ 1) for i in range(devices)])  4.36 us
    ppermute x1, starting transfers between devices, per_device(): lax.ppermute(atom_feats, AXES, across + [(j, i) for i, j in across])  0.66 us
  transfers between devices with their start and end apart: 2, of which 0 were waited for; matrix products, arithmetic and copies ran while one was open for 0% of the time, Pallas kernels for 8%

profile of v7, /device:TPU:0, one launch (start us, length us, event | category | flops | bytes accessed | tf_op | source)
XLA Modules:
  0.0 26.9 jit_solution(8719156853322698502)
XLA Ops:
  0.6 0.7 %collective-permute-start = (bf16[64,128]{1,0:T(8,128)(2,1)}, bf16[64,128]{1,0:T(8,128)(2,1)S(1)}, u32[]{:S(2)}, u32[]{:S(2)}) collective-permute-start(bf16[64,128]{1,0:T(8,128)(2,1)} %own_far.1), channel_id=1, source_target_pairs={{1,2},{3,4},{5,6},{7,8},{9,10},{11,12},{13,14},{15,16},{17,18},{19... | collective-permute-start | bytes 49160 | tf_op jit(solution)/shard_map/ppermute | solution.py:466
  1.3 4.4 %collective-permute-start.1 = (bf16[64,128]{1,0:T(8,128)(2,1)}, bf16[64,128]{1,0:T(8,128)(2,1)S(1)}, u32[]{:S(2)}, u32[]{:S(2)}) collective-permute-start(bf16[64,128]{1,0:T(8,128)(2,1)} %own_far.1), channel_id=1, source_target_pairs={{0,1},{1,0},{2,3},{3,2},{4,5},{5,4},{6,7},{7,6},{8,9},{9,8},{10,11... | collective-permute-start | bytes 49160 | tf_op jit(solution)/shard_map/ppermute | solution.py:467
  5.7 2.0 %ready.1 = (f32[64,128]{1,0:T(8,128)S(1)}, bf16[64,256]{1,0:T(8,128)(2,1)S(1)}, bf16[256,128]{1,0:T(8,128)(2,1)S(1)}, f32[256,64]{1,0:T(8,128)S(1)}, f32[256,1]{...) custom-call(bf16[64,128]{1,0:T(8,128)(2,1)} %own_far.1, ...), custom_call_target="tpu_custom_call" | custom-call | tf_op jit(solution)/shard_map/ready/pallas_call | solution.py:426
  7.7 0.0 collective-permute-done.neighbour
  7.7 0.0 collective-permute-done.1.sibling
  7.7 0.0 copy-start.2
  7.8 0.0 copy-start.3
  7.8 0.0 copy-start.4
  7.8 1.5 %atoms.1 = (bf16[768,128]{1,0:T(8,128)(2,1)S(1)}, bf16[64,128]{1,0:T(8,128)(2,1)S(1)}, f32[16,128]{1,0:T(8,128)S(1)}) custom-call(bf16[64,128]{1,0:T(8,128)(2,1)S(1)} %collective-permute-done.neighbour, bf16[64,128]{1,0:T(8,128)(2,1)S(1)} %collective-permute-done.1.sibling, f32[64,128]{1,0:T(8,128)S(1)} %get-tuple-element.27.own_float, ...), custom_call_target="tpu_custom_call" | custom-call | tf_op jit(solution)/shard_map/atoms/pallas_call | solution.py:426
  9.3 0.0 copy-start
  9.3 0.0 copy-start.1
  9.3 14.4 %all_to_all.5 = bf16[32,24,128]{2,1,0:T(8,128)(2,1)S(1)} all-to-all(bf16[32,24,128]{2,1,0:T(8,128)(2,1)S(1)} %bitcast.11), channel_id=1, replica_groups=mesh['row'=8,'col'=4] {'row','col'}, dimensions={0} | all-to-all | bytes 393216 | tf_op jit(solution)/shard_map/all_to_all | solution.py:572
  23.6 0.0 copy-done.2
  23.7 0.0 copy-done.3
  23.7 0.0 copy-done.4
  23.7 0.0 copy-done
  23.7 0.0 copy-done.1
  23.7 3.2 %pairs.1 = (bf16[64,128]{1,0:T(8,128)(2,1)}, bf16[4,384]{1,0:T(4,128)(2,1)}, bf16[16,32,128]{2,1,0:T(8,128)(2,1)}) custom-call(bf16[768,128]{1,0:T(8,128)(2,1)S(1)} %bitcast.9, bf16[64,768]{1,0:T(8,128)(2,1)S(1)} %get-tuple-element.46.adder, bf16[64,128]{1,0:T(8,128)(2,1)S(1)} %get-tuple-element.47.updated, f32[16,128]{1,0:T(8,128)S(1)} %get-tuple-element.48.slot_back, ...), custom_call_target="tpu_custom_call" | custom-call | tf_op jit(solution)/shard_map/pairs/pallas_call | solution.py:426
Async XLA Ops:
  0.6 7.1 %collective-permute-start = (bf16[64,128]{1,0:T(8,128)(2,1)}, bf16[64,128]{1,0:T(8,128)(2,1)S(1)}, u32[]{:S(2)}, u32[]{:S(2)}) collective-permute-start(bf16[64,128]{1,0:T(8,128)(2,1)} %own_far.1), channel_id=1, source_target_pairs={{1,2},{3,4},{5,6},{7,8},{9,10},{11,12},{13,14},{15,16},{17,18},{19... | collective-permute-start | bytes 49160 | tf_op jit(solution)/shard_map/ppermute | solution.py:466
  1.3 6.4 %collective-permute-start.1 = (bf16[64,128]{1,0:T(8,128)(2,1)}, bf16[64,128]{1,0:T(8,128)(2,1)S(1)}, u32[]{:S(2)}, u32[]{:S(2)}) collective-permute-start(bf16[64,128]{1,0:T(8,128)(2,1)} %own_far.1), channel_id=1, source_target_pairs={{0,1},{1,0},{2,3},{3,2},{4,5},{5,4},{6,7},{7,6},{8,9},{9,8},{10,11... | collective-permute-start | bytes 49160 | tf_op jit(solution)/shard_map/ppermute | solution.py:467
  7.7 15.9 %copy-start.2 = (bf16[128,512]{1,0:T(8,128)(2,1)S(1)}, bf16[128,512]{1,0:T(8,128)(2,1)}, u32[]{:S(2)}) copy-start(bf16[128,512]{1,0:T(8,128)(2,1)} %w_gate.1) | copy-start | bytes 393220
  7.8 15.9 %copy-start.3 = (bf16[128,512]{1,0:T(8,128)(2,1)S(1)}, bf16[128,512]{1,0:T(8,128)(2,1)}, u32[]{:S(2)}) copy-start(bf16[128,512]{1,0:T(8,128)(2,1)} %w_lift.1) | copy-start | bytes 393220
  7.8 15.9 %copy-start.4 = (bf16[512,128]{1,0:T(8,128)(2,1)S(1)}, bf16[512,128]{1,0:T(8,128)(2,1)}, u32[]{:S(2)}) copy-start(bf16[512,128]{1,0:T(8,128)(2,1)} %w_drop.1) | copy-start | bytes 393220
  9.3 14.4 %copy-start = (bf16[32,32,128]{2,1,0:T(8,128)(2,1)S(1)}, bf16[32,32,128]{2,1,0:T(8,128)(2,1)}, u32[]{:S(2)}) copy-start(bf16[32,32,128]{2,1,0:T(8,128)(2,1)} %param.31) | copy-start | bytes 786436
  9.3 14.4 %copy-start.1 = (bf16[16,32,128]{2,1,0:T(8,128)(2,1)S(1)}, bf16[16,32,128]{2,1,0:T(8,128)(2,1)}, u32[]{:S(2)}) copy-start(bf16[16,32,128]{2,1,0:T(8,128)(2,1)} %pair_state.1) | copy-start | bytes 393220

commit v8 on v7

--- a/solution.py
+++ b/solution.py
@@ -17,7 +17,7 @@
 SLOTS = 16
 BLOCK = 24
 DESTS = 32
-PAIR_ROWS = 8
+PAIR_ROWS = 4
 MASKED = -1e30
 SPARE = 12 << 20
 MOST = 60 << 20
@@ -363,9 +363,7 @@
     w_drop,
     atom_out,
     token_single,
-    pair_far,
     pair_out,
-    leaving,
 ):
     row_tokens, col_tokens, pair_width = pair_state.shape
     own_tokens, channels = token_single.shape
@@ -394,6 +392,10 @@
         result = (summed + dot(hidden, w_drop[...])).astype(BF)
         pair_out[pl.ds(here, PAIR_ROWS)] = result.reshape(PAIR_ROWS, col_tokens, pair_width)
 
+    for step in range(row_tokens // PAIR_ROWS):
+        here = step * PAIR_ROWS
+        pair_rows(left_wide[here : here + PAIR_ROWS], here)
+
     token_single[...] = jnp.concatenate(
         [added[k * own_tokens : (k + 1) * own_tokens] for k in range(tiles)], axis=1
     ).astype(BF)
@@ -406,20 +408,8 @@
     )
     atom_out[...] = (updated[...].astype(F32) + lifted).astype(BF)
 
-    copies = []
-    for step in range(row_tokens // PAIR_ROWS):
-        here = step * PAIR_ROWS
-        pair_rows(left_wide[here : here + PAIR_ROWS], here)
-        part = pl.ds(here, PAIR_ROWS)
-        copies.append(
-            pltpu.make_async_copy(pair_out.at[part], pair_far.at[part], leaving.at[step])
-        )
-        copies[-1].start()
-    for copy in copies:
-        copy.wait()
-
-
-def call(kernel, name, operands, outputs, far=(), out_far=(), scratch=()):
+
+def call(kernel, name, operands, outputs, far=(), scratch=()):
     near_spec = pl.BlockSpec(memory_space=pltpu.VMEM)
     far_spec = pl.BlockSpec(memory_space=pltpu.HBM)
     held = sum(math.prod(a.shape) * a.dtype.itemsize for a in operands + outputs)
@@ -427,7 +417,7 @@
         kernel,
         out_shape=outputs,
         in_specs=[far_spec] * len(far) + [near_spec] * len(operands),
-        out_specs=tuple(far_spec if k in out_far else near_spec for k in range(len(outputs))),
+        out_specs=(near_spec,) * len(outputs),
         scratch_shapes=scratch,
         compiler_params=pltpu.CompilerParams(vmem_limit_bytes=min(2 * held + SPARE, MOST)),
         name=name,
@@ -593,11 +583,6 @@
             held(own_tokens, channels, dtype=BF),
             held(*pair_state.shape, dtype=BF),
         ),
-        out_far=(2,),
-        scratch=(
-            pltpu.VMEM(pair_state.shape, BF),
-            pltpu.SemaphoreType.DMA((row_tokens // PAIR_ROWS,)),
-        ),
     )
 
 

time: 27.2 us -> 27.4 us (level)
  no operation moved by 1% of the time
where the time goes in v8:
time: 27.4 us; the launch traced here: 27.1 us
  blocking collectives  14.4 us (53%)
  Pallas kernels  6.91 us (25%)
  starting transfers between devices  5.03 us (18%)
  between operations  0.73 us (3%)
    all_to_all x1, blocking collectives, per_device(): arrived = lax.all_to_all(payload.reshape(devices, BLOCK, LANES), AXES, 0, 0)  14.4 us
    pallas_call x3, Pallas kernels, call(): pl.pallas_call(kernel, out_shape=outputs, in_specs=[far_spec] * len(far)...  6.91 us
    ppermute x1, starting transfers between devices, per_device(): lax.ppermute(atom_feats, AXES, [(i, i ^ 1) for i in range(devices)])  4.36 us
    ppermute x1, starting transfers between devices, per_device(): lax.ppermute(atom_feats, AXES, across + [(j, i) for i, j in across])  0.66 us
  transfers between devices with their start and end apart: 2, of which 0 were waited for; matrix products, arithmetic and copies ran while one was open for 0% of the time, Pallas kernels for 8%

profile of v8, /device:TPU:0, one launch (start us, length us, event | category | flops | bytes accessed | tf_op | source)
XLA Modules:
  0.0 27.1 jit_solution(11821164133234574369)
XLA Ops:
  0.6 0.7 %collective-permute-start = (bf16[64,128]{1,0:T(8,128)(2,1)}, bf16[64,128]{1,0:T(8,128)(2,1)S(1)}, u32[]{:S(2)}, u32[]{:S(2)}) collective-permute-start(bf16[64,128]{1,0:T(8,128)(2,1)} %own_far.1), channel_id=1, source_target_pairs={{1,2},{3,4},{5,6},{7,8},{9,10},{11,12},{13,14},{15,16},{17,18},{19... | collective-permute-start | bytes 49160 | tf_op jit(solution)/shard_map/ppermute | solution.py:456
  1.3 4.4 %collective-permute-start.1 = (bf16[64,128]{1,0:T(8,128)(2,1)}, bf16[64,128]{1,0:T(8,128)(2,1)S(1)}, u32[]{:S(2)}, u32[]{:S(2)}) collective-permute-start(bf16[64,128]{1,0:T(8,128)(2,1)} %own_far.1), channel_id=1, source_target_pairs={{0,1},{1,0},{2,3},{3,2},{4,5},{5,4},{6,7},{7,6},{8,9},{9,8},{10,11... | collective-permute-start | bytes 49160 | tf_op jit(solution)/shard_map/ppermute | solution.py:457
  5.7 2.0 %ready.1 = (f32[64,128]{1,0:T(8,128)S(1)}, bf16[64,256]{1,0:T(8,128)(2,1)S(1)}, bf16[256,128]{1,0:T(8,128)(2,1)S(1)}, f32[256,64]{1,0:T(8,128)S(1)}, f32[256,1]{...) custom-call(bf16[64,128]{1,0:T(8,128)(2,1)} %own_far.1, ...), custom_call_target="tpu_custom_call" | custom-call | tf_op jit(solution)/shard_map/ready/pallas_call | solution.py:416
  7.7 0.0 collective-permute-done.neighbour
  7.7 0.0 collective-permute-done.1.sibling
  7.7 0.0 copy-start.2
  7.8 0.0 copy-start.3
  7.8 0.0 copy-start.4
  7.8 1.5 %atoms.1 = (bf16[768,128]{1,0:T(8,128)(2,1)S(1)}, bf16[64,128]{1,0:T(8,128)(2,1)S(1)}, f32[16,128]{1,0:T(8,128)S(1)}) custom-call(bf16[64,128]{1,0:T(8,128)(2,1)S(1)} %collective-permute-done.neighbour, bf16[64,128]{1,0:T(8,128)(2,1)S(1)} %collective-permute-done.1.sibling, f32[64,128]{1,0:T(8,128)S(1)} %get-tuple-element.27.own_float, ...), custom_call_target="tpu_custom_call" | custom-call | tf_op jit(solution)/shard_map/atoms/pallas_call | solution.py:416
  9.3 0.0 copy-start
  9.3 0.0 copy-start.1
  9.3 14.4 %all_to_all.5 = bf16[32,24,128]{2,1,0:T(8,128)(2,1)S(1)} all-to-all(bf16[32,24,128]{2,1,0:T(8,128)(2,1)S(1)} %bitcast.11), channel_id=1, replica_groups=mesh['row'=8,'col'=4] {'row','col'}, dimensions={0} | all-to-all | bytes 393216 | tf_op jit(solution)/shard_map/all_to_all | solution.py:562
  23.6 0.0 copy-done.2
  23.7 0.0 copy-done.3
  23.7 0.0 copy-done.4
  23.7 0.0 copy-done
  23.7 0.0 copy-done.1
  23.7 3.4 %pairs.1 = (bf16[64,128]{1,0:T(8,128)(2,1)}, bf16[4,384]{1,0:T(4,128)(2,1)}, bf16[16,32,128]{2,1,0:T(8,128)(2,1)}) custom-call(bf16[768,128]{1,0:T(8,128)(2,1)S(1)} %bitcast.9, bf16[64,768]{1,0:T(8,128)(2,1)S(1)} %get-tuple-element.46.adder, bf16[64,128]{1,0:T(8,128)(2,1)S(1)} %get-tuple-element.47.updated, f32[16,128]{1,0:T(8,128)S(1)} %get-tuple-element.48.slot_back, ...), custom_call_target="tpu_custom_call" | custom-call | tf_op jit(solution)/shard_map/pairs/pallas_call | solution.py:416
Async XLA Ops:
  0.6 7.1 %collective-permute-start = (bf16[64,128]{1,0:T(8,128)(2,1)}, bf16[64,128]{1,0:T(8,128)(2,1)S(1)}, u32[]{:S(2)}, u32[]{:S(2)}) collective-permute-start(bf16[64,128]{1,0:T(8,128)(2,1)} %own_far.1), channel_id=1, source_target_pairs={{1,2},{3,4},{5,6},{7,8},{9,10},{11,12},{13,14},{15,16},{17,18},{19... | collective-permute-start | bytes 49160 | tf_op jit(solution)/shard_map/ppermute | solution.py:456
  1.3 6.4 %collective-permute-start.1 = (bf16[64,128]{1,0:T(8,128)(2,1)}, bf16[64,128]{1,0:T(8,128)(2,1)S(1)}, u32[]{:S(2)}, u32[]{:S(2)}) collective-permute-start(bf16[64,128]{1,0:T(8,128)(2,1)} %own_far.1), channel_id=1, source_target_pairs={{0,1},{1,0},{2,3},{3,2},{4,5},{5,4},{6,7},{7,6},{8,9},{9,8},{10,11... | collective-permute-start | bytes 49160 | tf_op jit(solution)/shard_map/ppermute | solution.py:457
  7.7 15.9 %copy-start.2 = (bf16[128,512]{1,0:T(8,128)(2,1)S(1)}, bf16[128,512]{1,0:T(8,128)(2,1)}, u32[]{:S(2)}) copy-start(bf16[128,512]{1,0:T(8,128)(2,1)} %w_gate.1) | copy-start | bytes 393220
  7.8 15.9 %copy-start.3 = (bf16[128,512]{1,0:T(8,128)(2,1)S(1)}, bf16[128,512]{1,0:T(8,128)(2,1)}, u32[]{:S(2)}) copy-start(bf16[128,512]{1,0:T(8,128)(2,1)} %w_lift.1) | copy-start | bytes 393220
  7.8 15.9 %copy-start.4 = (bf16[512,128]{1,0:T(8,128)(2,1)S(1)}, bf16[512,128]{1,0:T(8,128)(2,1)}, u32[]{:S(2)}) copy-start(bf16[512,128]{1,0:T(8,128)(2,1)} %w_drop.1) | copy-start | bytes 393220
  9.3 14.4 %copy-start = (bf16[32,32,128]{2,1,0:T(8,128)(2,1)S(1)}, bf16[32,32,128]{2,1,0:T(8,128)(2,1)}, u32[]{:S(2)}) copy-start(bf16[32,32,128]{2,1,0:T(8,128)(2,1)} %param.31) | copy-start | bytes 786436
  9.3 14.4 %copy-start.1 = (bf16[16,32,128]{2,1,0:T(8,128)(2,1)S(1)}, bf16[16,32,128]{2,1,0:T(8,128)(2,1)}, u32[]{:S(2)}) copy-start(bf16[16,32,128]{2,1,0:T(8,128)(2,1)} %pair_state.1) | copy-start | bytes 393220

commit v9 on v8

--- a/solution.py
+++ b/solution.py
@@ -17,7 +17,7 @@
 SLOTS = 16
 BLOCK = 24
 DESTS = 32
-PAIR_ROWS = 4
+PAIR_ROWS = 16
 MASKED = -1e30
 SPARE = 12 << 20
 MOST = 60 << 20
@@ -88,6 +88,7 @@
     w_back_far,
     w_left_far,
     w_right_far,
+    w_outer_far,
     own_float,
     keyval,
     stacked,
@@ -109,6 +110,7 @@
     w_pool,
     w_back,
     w_sides,
+    w_outer,
     own,
     key_starts,
     counts,
@@ -135,6 +137,7 @@
         (w_back_far, w_back),
         (w_left_far, w_sides.at[:opm]),
         (w_right_far, w_sides.at[opm : 2 * opm]),
+        (w_outer_far, w_outer.at[:, : w_outer_far.shape[1]]),
     )
     copies = [pltpu.make_async_copy(a, b, arrivals.at[k]) for k, (a, b) in enumerate(pairs)]
     for copy in copies:
@@ -265,6 +268,9 @@
     top[...] = jnp.max(raw_scores, axis=-1, keepdims=True)
     for copy in copies[8:]:
         copy.wait()
+    pair_width = w_outer_far.shape[1]
+    average = jnp.full((pair_width, pair_width), 1.0 / pair_width, F32).astype(BF)
+    w_outer[:, pair_width:] = dot(w_outer[:, :pair_width], average).astype(BF)
 
 
 def atom_kernel(
@@ -379,13 +385,18 @@
     left_wide = dot(left, flag(product_lane // opm == unit))
     right_wide = dot(right, flag(product_lane % opm == unit))
 
+    average = jnp.full((pair_width, pair_width), 1.0 / pair_width, F32).astype(BF)
+
     def pair_rows(lefts, here):
         products = jnp.concatenate(
             [(lefts[i : i + 1, :] * right_wide).astype(BF) for i in range(PAIR_ROWS)], axis=0
         )
         flat = pair_state[pl.ds(here, PAIR_ROWS)].reshape(PAIR_ROWS * col_tokens, pair_width)
-        summed = flat.astype(F32) + dot(products, w_outer[...])
-        normed = layer_norm(summed, pair_gain[...]).astype(BF)
+        outer = dot(products, w_outer[...])
+        summed = flat.astype(F32) + outer[:, :pair_width]
+        centred = summed - (dot(flat, average) + outer[:, pair_width:])
+        variance = dot((centred * centred).astype(BF), average)
+        normed = (centred * lax.rsqrt(variance + EPSILON) * pair_gain[...]).astype(BF)
         gate = dot(normed, half_gate)
         lift = dot(normed, w_lift[...])
         hidden = (gate * lift * (1.0 + jnp.tanh(gate))).astype(BF)
@@ -452,6 +463,7 @@
     own_tokens = tokens // devices
     row_tokens, col_tokens, _ = pair_state.shape
     tiles = channels // LANES
+    opm = w_left.shape[1]
     across = [(i, i + 1) for i in range(1, devices - 1, 2)]
     neighbour = lax.ppermute(atom_feats, AXES, across + [(j, i) for i, j in across])
     sibling = lax.ppermute(atom_feats, AXES, [(i, i ^ 1) for i in range(devices)])
@@ -486,6 +498,7 @@
             held(width, channels, dtype=BF),
             held(channels, width, dtype=BF),
             held(LANES, channels, dtype=BF),
+            held(opm * opm, 2 * w_outer.shape[-1], dtype=BF),
         ),
         far=(
             atom_feats,
@@ -502,6 +515,7 @@
             w_back,
             w_left.T,
             w_right.T,
+            w_outer.reshape(opm * opm, -1),
         ),
         scratch=(
             pltpu.VMEM((rows, width), BF),
@@ -510,7 +524,7 @@
             pltpu.VMEM(counts_folded.shape, jnp.int32),
             pltpu.VMEM((width, width), BF),
             pltpu.VMEM((tokens, LANES), F32),
-            pltpu.SemaphoreType.DMA((14,)),
+            pltpu.SemaphoreType.DMA((15,)),
         ),
     )
     (
@@ -531,6 +545,7 @@
         atom_gain_kept,
         pair_gain_kept,
         *kept,
+        w_outer_kept,
     ) = ready
     payload, updated, slot_back = call(
         atom_kernel,
@@ -560,7 +575,6 @@
         ),
     )
     arrived = lax.all_to_all(payload.reshape(devices, BLOCK, LANES), AXES, 0, 0)
-    opm = w_left.shape[1]
     return call(
         pair_kernel,
         "pairs",
@@ -572,7 +586,7 @@
             last,
             member,
             pair_state,
-            w_outer.reshape(opm * opm, -1),
+            w_outer_kept,
             pair_gain_kept,
             w_gate,
             w_lift,

time: 27.4 us -> 26.5 us (0.967)
  Pallas kernels: 6.91 us -> 6.34 us
  blocking collectives: 14.4 us -> 14.1 us
    pallas_call x3, Pallas kernels: 6.91 us -> 6.34 us  [call(): pl.pallas_call(kernel, out_shape=outputs, in_specs=[far_spec] * len(far)...]
    all_to_all x1, blocking collectives: 14.4 us -> 14.1 us  [per_device(): arrived = lax.all_to_all(payload.reshape(devices, BLOCK, LANES), AXES, 0, 0)]
  transfers between devices with their start and end apart: 2 -> 2, of which waited for: 0 -> 0; matrix products, arithmetic and copies ran while one was open for 0% -> 0% of each run, Pallas kernels for 8% -> 9%
where the time goes in v9:
time: 26.5 us; the launch traced here: 26.2 us
  blocking collectives  14.1 us (53%)
  Pallas kernels  6.34 us (24%)
  starting transfers between devices  5.03 us (19%)
  between operations  0.72 us (3%)
    all_to_all x1, blocking collectives, per_device(): arrived = lax.all_to_all(payload.reshape(devices, BLOCK, LANES), AXES, 0, 0)  14.1 us
    pallas_call x3, Pallas kernels, call(): pl.pallas_call(kernel, out_shape=outputs, in_specs=[far_spec] * len(far)...  6.34 us
    ppermute x1, starting transfers between devices, per_device(): lax.ppermute(atom_feats, AXES, [(i, i ^ 1) for i in range(devices)])  4.36 us
    ppermute x1, starting transfers between devices, per_device(): lax.ppermute(atom_feats, AXES, across + [(j, i) for i, j in across])  0.66 us
  transfers between devices with their start and end apart: 2, of which 0 were waited for; matrix products, arithmetic and copies ran while one was open for 0% of the time, Pallas kernels for 9%

profile of v9, /device:TPU:0, one launch (start us, length us, event | category | flops | bytes accessed | tf_op | source)
XLA Modules:
  0.0 26.2 jit_solution(6304414249900331513)
XLA Ops:
  0.6 0.7 %collective-permute-start = (bf16[64,128]{1,0:T(8,128)(2,1)}, bf16[64,128]{1,0:T(8,128)(2,1)S(1)}, u32[]{:S(2)}, u32[]{:S(2)}) collective-permute-start(bf16[64,128]{1,0:T(8,128)(2,1)} %own_far.1), channel_id=1, source_target_pairs={{1,2},{3,4},{5,6},{7,8},{9,10},{11,12},{13,14},{15,16},{17,18},{19... | collective-permute-start | bytes 49160 | tf_op jit(solution)/shard_map/ppermute | solution.py:468
  1.3 4.4 %collective-permute-start.1 = (bf16[64,128]{1,0:T(8,128)(2,1)}, bf16[64,128]{1,0:T(8,128)(2,1)S(1)}, u32[]{:S(2)}, u32[]{:S(2)}) collective-permute-start(bf16[64,128]{1,0:T(8,128)(2,1)} %own_far.1), channel_id=1, source_target_pairs={{0,1},{1,0},{2,3},{3,2},{4,5},{5,4},{6,7},{7,6},{8,9},{9,8},{10,11... | collective-permute-start | bytes 49160 | tf_op jit(solution)/shard_map/ppermute | solution.py:469
  5.7 2.4 %ready.1 = (f32[64,128]{1,0:T(8,128)S(1)}, bf16[64,256]{1,0:T(8,128)(2,1)S(1)}, bf16[256,128]{1,0:T(8,128)(2,1)S(1)}, f32[256,64]{1,0:T(8,128)S(1)}, f32[256,1]{...) custom-call(bf16[64,128]{1,0:T(8,128)(2,1)} %own_far.1, ...), custom_call_target="tpu_custom_call" | custom-call | tf_op jit(solution)/shard_map/ready/pallas_call | solution.py:427
  8.0 0.0 collective-permute-done.neighbour
  8.0 0.0 collective-permute-done.1.sibling
  8.1 0.0 copy-start.3
  8.1 1.5 %atoms.1 = (bf16[768,128]{1,0:T(8,128)(2,1)S(1)}, bf16[64,128]{1,0:T(8,128)(2,1)S(1)}, f32[16,128]{1,0:T(8,128)S(1)}) custom-call(bf16[64,128]{1,0:T(8,128)(2,1)S(1)} %collective-permute-done.neighbour, bf16[64,128]{1,0:T(8,128)(2,1)S(1)} %collective-permute-done.1.sibling, f32[64,128]{1,0:T(8,128)S(1)} %get-tuple-element.28.own_float, ...), custom_call_target="tpu_custom_call" | custom-call | tf_op jit(solution)/shard_map/atoms/pallas_call | solution.py:427
  9.6 0.0 copy-start
  9.6 0.0 copy-start.1
  9.6 0.0 copy-start.2
  9.6 14.1 %all_to_all.5 = bf16[32,24,128]{2,1,0:T(8,128)(2,1)S(1)} all-to-all(bf16[32,24,128]{2,1,0:T(8,128)(2,1)S(1)} %bitcast.10), channel_id=1, replica_groups=mesh['row'=8,'col'=4] {'row','col'}, dimensions={0} | all-to-all | bytes 393216 | tf_op jit(solution)/shard_map/all_to_all | solution.py:577
  23.6 0.0 copy-done.3
  23.6 0.0 copy-done
  23.6 0.0 copy-done.1
  23.6 0.0 copy-done.2
  23.7 2.5 %pairs.1 = (bf16[64,128]{1,0:T(8,128)(2,1)}, bf16[4,384]{1,0:T(4,128)(2,1)}, bf16[16,32,128]{2,1,0:T(8,128)(2,1)}) custom-call(bf16[768,128]{1,0:T(8,128)(2,1)S(1)} %bitcast.9, bf16[64,768]{1,0:T(8,128)(2,1)S(1)} %get-tuple-element.47.adder, bf16[64,128]{1,0:T(8,128)(2,1)S(1)} %get-tuple-element.48.updated, f32[16,128]{1,0:T(8,128)S(1)} %get-tuple-element.49.slot_back, ...), custom_call_target="tpu_custom_call" | custom-call | tf_op jit(solution)/shard_map/pairs/pallas_call | solution.py:427
Async XLA Ops:
  0.6 7.4 %collective-permute-start = (bf16[64,128]{1,0:T(8,128)(2,1)}, bf16[64,128]{1,0:T(8,128)(2,1)S(1)}, u32[]{:S(2)}, u32[]{:S(2)}) collective-permute-start(bf16[64,128]{1,0:T(8,128)(2,1)} %own_far.1), channel_id=1, source_target_pairs={{1,2},{3,4},{5,6},{7,8},{9,10},{11,12},{13,14},{15,16},{17,18},{19... | collective-permute-start | bytes 49160 | tf_op jit(solution)/shard_map/ppermute | solution.py:468
  1.3 6.7 %collective-permute-start.1 = (bf16[64,128]{1,0:T(8,128)(2,1)}, bf16[64,128]{1,0:T(8,128)(2,1)S(1)}, u32[]{:S(2)}, u32[]{:S(2)}) collective-permute-start(bf16[64,128]{1,0:T(8,128)(2,1)} %own_far.1), channel_id=1, source_target_pairs={{0,1},{1,0},{2,3},{3,2},{4,5},{5,4},{6,7},{7,6},{8,9},{9,8},{10,11... | collective-permute-start | bytes 49160 | tf_op jit(solution)/shard_map/ppermute | solution.py:469
  8.1 15.6 %copy-start.3 = (bf16[512,128]{1,0:T(8,128)(2,1)S(1)}, bf16[512,128]{1,0:T(8,128)(2,1)}, u32[]{:S(2)}) copy-start(bf16[512,128]{1,0:T(8,128)(2,1)} %w_drop.1) | copy-start | bytes 393220
  9.6 14.1 %copy-start = (bf16[16,32,128]{2,1,0:T(8,128)(2,1)S(1)}, bf16[16,32,128]{2,1,0:T(8,128)(2,1)}, u32[]{:S(2)}) copy-start(bf16[16,32,128]{2,1,0:T(8,128)(2,1)} %pair_state.1) | copy-start | bytes 393220
  9.6 14.1 %copy-start.1 = (bf16[128,512]{1,0:T(8,128)(2,1)S(1)}, bf16[128,512]{1,0:T(8,128)(2,1)}, u32[]{:S(2)}) copy-start(bf16[128,512]{1,0:T(8,128)(2,1)} %w_gate.1) | copy-start | bytes 393220
  9.6 14.1 %copy-start.2 = (bf16[128,512]{1,0:T(8,128)(2,1)S(1)}, bf16[128,512]{1,0:T(8,128)(2,1)}, u32[]{:S(2)}) copy-start(bf16[128,512]{1,0:T(8,128)(2,1)} %w_lift.1) | copy-start | bytes 393220

commit v10 on v9

--- a/solution.py
+++ b/solution.py
@@ -52,6 +52,10 @@
 
 def place():
     return lax.axis_index("row") * lax.axis_size("col") + lax.axis_index("col")
+
+
+def member_at(block, devices):
+    return block ^ (devices // 2)
 
 
 def repeat(count, step):
@@ -195,7 +199,8 @@
         here = span(at, DESTS * BLOCK)
         token_at = iota((DESTS * BLOCK, tokens), 1)
         turn = spread(tokens, 1) - lead
-        row_token = (spread(tokens, 0) + at * DESTS) * own_tokens + turn % own_tokens
+        dest = member_at(spread(tokens, 0) + at * DESTS, devices)
+        row_token = dest * own_tokens + turn % own_tokens
         row_end = dot_t(flag(token_at <= row_token), counts_wide)
         row_start = dot_t(flag(token_at < row_token), counts_wide)
         lanes = tiles * rows
@@ -216,7 +221,7 @@
     def adder_step(at):
         here = span(at, LANES)
         spot_lane = iota((1, LANES), 1) + at * LANES
-        block = spot_lane // BLOCK
+        block = member_at(spot_lane // BLOCK, devices)
         spot = spot_lane % BLOCK
         edge = (block * rows).astype(F32)
         tally = jnp.zeros((1, LANES), F32)
@@ -230,7 +235,7 @@
             (position - 1) * BLOCK + slots + 1,
             jnp.where(line == token_rows + 1, (position + 1) * BLOCK + slots, -1),
         )
-        fixed = (spot_lane == wanted) | ((line < token_rows) & (spot == line + lead))
+        fixed = (block * BLOCK + spot == wanted) | ((line < token_rows) & (spot == line + lead))
         lefts = token == iota((row_tokens, LANES), 0) + first_row
         rights = token == iota((col_tokens, LANES), 0) + first_col
         adder[:SLOTS, here] = flag(fixed)
@@ -574,7 +579,10 @@
             held(SLOTS, width),
         ),
     )
-    arrived = lax.all_to_all(payload.reshape(devices, BLOCK, LANES), AXES, 0, 0)
+    order = [[member_at(k, devices) for k in range(devices)]]
+    arrived = lax.all_to_all(
+        payload.reshape(devices, BLOCK, LANES), AXES, 0, 0, axis_index_groups=order
+    )
     return call(
         pair_kernel,
         "pairs",

time: 26.5 us -> 26.5 us (level)
  no operation moved by 1% of the time
where the time goes in v10:
time: 26.5 us; the launch traced here: 26.2 us
  blocking collectives  14.1 us (53%)
  Pallas kernels  6.34 us (24%)
  starting transfers between devices  5.03 us (19%)
  between operations  0.72 us (3%)
    all_to_all x1, blocking collectives, per_device(): lax.all_to_all(payload.reshape(devices, BLOCK, LANES), AXES, 0, 0, axis_i...  14.1 us
    pallas_call x3, Pallas kernels, call(): pl.pallas_call(kernel, out_shape=outputs, in_specs=[far_spec] * len(far)...  6.34 us
    ppermute x1, starting transfers between devices, per_device(): lax.ppermute(atom_feats, AXES, [(i, i ^ 1) for i in range(devices)])  4.36 us
    ppermute x1, starting transfers between devices, per_device(): lax.ppermute(atom_feats, AXES, across + [(j, i) for i, j in across])  0.66 us
  transfers between devices with their start and end apart: 2, of which 0 were waited for; matrix products, arithmetic and copies ran while one was open for 0% of the time, Pallas kernels for 9%

profile of v10, /device:TPU:0, one launch (start us, length us, event | category | flops | bytes accessed | tf_op | source)
XLA Modules:
  0.0 26.2 jit_solution(14950545526380073713)
XLA Ops:
  0.6 0.7 %collective-permute-start = (bf16[64,128]{1,0:T(8,128)(2,1)}, bf16[64,128]{1,0:T(8,128)(2,1)S(1)}, u32[]{:S(2)}, u32[]{:S(2)}) collective-permute-start(bf16[64,128]{1,0:T(8,128)(2,1)} %own_far.1), channel_id=1, source_target_pairs={{1,2},{3,4},{5,6},{7,8},{9,10},{11,12},{13,14},{15,16},{17,18},{19... | collective-permute-start | bytes 49160 | tf_op jit(solution)/shard_map/ppermute | solution.py:473
  1.3 4.4 %collective-permute-start.1 = (bf16[64,128]{1,0:T(8,128)(2,1)}, bf16[64,128]{1,0:T(8,128)(2,1)S(1)}, u32[]{:S(2)}, u32[]{:S(2)}) collective-permute-start(bf16[64,128]{1,0:T(8,128)(2,1)} %own_far.1), channel_id=1, source_target_pairs={{0,1},{1,0},{2,3},{3,2},{4,5},{5,4},{6,7},{7,6},{8,9},{9,8},{10,11... | collective-permute-start | bytes 49160 | tf_op jit(solution)/shard_map/ppermute | solution.py:474
  5.7 2.4 %ready.1 = (f32[64,128]{1,0:T(8,128)S(1)}, bf16[64,256]{1,0:T(8,128)(2,1)S(1)}, bf16[256,128]{1,0:T(8,128)(2,1)S(1)}, f32[256,64]{1,0:T(8,128)S(1)}, f32[256,1]{...) custom-call(bf16[64,128]{1,0:T(8,128)(2,1)} %own_far.1, ...), custom_call_target="tpu_custom_call" | custom-call | tf_op jit(solution)/shard_map/ready/pallas_call | solution.py:432
  8.0 0.0 collective-permute-done.neighbour
  8.0 0.0 collective-permute-done.1.sibling
  8.1 0.0 copy-start.3
  8.1 1.5 %atoms.1 = (bf16[768,128]{1,0:T(8,128)(2,1)S(1)}, bf16[64,128]{1,0:T(8,128)(2,1)S(1)}, f32[16,128]{1,0:T(8,128)S(1)}) custom-call(bf16[64,128]{1,0:T(8,128)(2,1)S(1)} %collective-permute-done.neighbour, bf16[64,128]{1,0:T(8,128)(2,1)S(1)} %collective-permute-done.1.sibling, f32[64,128]{1,0:T(8,128)S(1)} %get-tuple-element.28.own_float, ...), custom_call_target="tpu_custom_call" | custom-call | tf_op jit(solution)/shard_map/atoms/pallas_call | solution.py:432
  9.6 0.0 copy-start
  9.6 0.0 copy-start.1
  9.6 0.0 copy-start.2
  9.6 14.1 %all_to_all.5 = bf16[32,24,128]{2,1,0:T(8,128)(2,1)S(1)} all-to-all(bf16[32,24,128]{2,1,0:T(8,128)(2,1)S(1)} %bitcast.10), channel_id=1, replica_groups={{16,17,18,19,20,21,22,23,24,25,26,27,28,29,30,31,0,1,2,3,4,5,6,7,8,9,10..., dimensions={0} | all-to-all | bytes 393216 | tf_op jit(solution)/shard_map/all_to_all | solution.py:583
  23.6 0.0 copy-done.3
  23.6 0.0 copy-done
  23.6 0.0 copy-done.1
  23.6 0.0 copy-done.2
  23.7 2.5 %pairs.1 = (bf16[64,128]{1,0:T(8,128)(2,1)}, bf16[4,384]{1,0:T(4,128)(2,1)}, bf16[16,32,128]{2,1,0:T(8,128)(2,1)}) custom-call(bf16[768,128]{1,0:T(8,128)(2,1)S(1)} %bitcast.9, bf16[64,768]{1,0:T(8,128)(2,1)S(1)} %get-tuple-element.47.adder, bf16[64,128]{1,0:T(8,128)(2,1)S(1)} %get-tuple-element.48.updated, f32[16,128]{1,0:T(8,128)S(1)} %get-tuple-element.49.slot_back, ...), custom_call_target="tpu_custom_call" | custom-call | tf_op jit(solution)/shard_map/pairs/pallas_call | solution.py:432
Async XLA Ops:
  0.6 7.4 %collective-permute-start = (bf16[64,128]{1,0:T(8,128)(2,1)}, bf16[64,128]{1,0:T(8,128)(2,1)S(1)}, u32[]{:S(2)}, u32[]{:S(2)}) collective-permute-start(bf16[64,128]{1,0:T(8,128)(2,1)} %own_far.1), channel_id=1, source_target_pairs={{1,2},{3,4},{5,6},{7,8},{9,10},{11,12},{13,14},{15,16},{17,18},{19... | collective-permute-start | bytes 49160 | tf_op jit(solution)/shard_map/ppermute | solution.py:473
  1.3 6.7 %collective-permute-start.1 = (bf16[64,128]{1,0:T(8,128)(2,1)}, bf16[64,128]{1,0:T(8,128)(2,1)S(1)}, u32[]{:S(2)}, u32[]{:S(2)}) collective-permute-start(bf16[64,128]{1,0:T(8,128)(2,1)} %own_far.1), channel_id=1, source_target_pairs={{0,1},{1,0},{2,3},{3,2},{4,5},{5,4},{6,7},{7,6},{8,9},{9,8},{10,11... | collective-permute-start | bytes 49160 | tf_op jit(solution)/shard_map/ppermute | solution.py:474
  8.1 15.6 %copy-start.3 = (bf16[512,128]{1,0:T(8,128)(2,1)S(1)}, bf16[512,128]{1,0:T(8,128)(2,1)}, u32[]{:S(2)}) copy-start(bf16[512,128]{1,0:T(8,128)(2,1)} %w_drop.1) | copy-start | bytes 393220
  9.6 14.1 %copy-start = (bf16[16,32,128]{2,1,0:T(8,128)(2,1)S(1)}, bf16[16,32,128]{2,1,0:T(8,128)(2,1)}, u32[]{:S(2)}) copy-start(bf16[16,32,128]{2,1,0:T(8,128)(2,1)} %pair_state.1) | copy-start | bytes 393220
  9.6 14.1 %copy-start.1 = (bf16[128,512]{1,0:T(8,128)(2,1)S(1)}, bf16[128,512]{1,0:T(8,128)(2,1)}, u32[]{:S(2)}) copy-start(bf16[128,512]{1,0:T(8,128)(2,1)} %w_gate.1) | copy-start | bytes 393220
  9.6 14.1 %copy-start.2 = (bf16[128,512]{1,0:T(8,128)(2,1)S(1)}, bf16[128,512]{1,0:T(8,128)(2,1)}, u32[]{:S(2)}) copy-start(bf16[128,512]{1,0:T(8,128)(2,1)} %w_lift.1) | copy-start | bytes 393220

commit v11 on v9

--- a/solution.py
+++ b/solution.py
@@ -15,7 +15,8 @@
 FEWEST = 8
 LANES = 128
 SLOTS = 16
-BLOCK = 24
+BLOCK = 16
+SLOT_ROW = 12
 DESTS = 32
 PAIR_ROWS = 16
 MASKED = -1e30
@@ -52,6 +53,19 @@
 
 def place():
     return lax.axis_index("row") * lax.axis_size("col") + lax.axis_index("col")
+
+
+def overlap(base, first_own, own_tokens, slots):
+    inner = jnp.minimum(first_own + own_tokens, base + slots) - jnp.maximum(first_own, base)
+    return jnp.maximum(inner, 0)
+
+
+def edge_row(base, first_own, own_tokens, slots):
+    last_own = first_own + own_tokens - 1
+    last_held = (last_own >= base) & (last_own < base + slots)
+    free = jnp.where(last_held, 0, own_tokens - 1)
+    whole = overlap(base, first_own, own_tokens, slots) == own_tokens
+    return jnp.where(whole, BLOCK - 1, free)
 
 
 def repeat(count, step):
@@ -97,6 +111,7 @@
     far_bias,
     picks,
     row_scale,
+    selects,
     member,
     slot_scale,
     before,
@@ -137,6 +152,8 @@
         (w_back_far, w_back),
         (w_left_far, w_sides.at[:opm]),
         (w_right_far, w_sides.at[opm : 2 * opm]),
+        (w_left_far, w_sides.at[2 * LANES - 2 * opm : 2 * LANES - opm]),
+        (w_right_far, w_sides.at[2 * LANES - opm :]),
         (w_outer_far, w_outer.at[:, : w_outer_far.shape[1]]),
     )
     copies = [pltpu.make_async_copy(a, b, arrivals.at[k]) for k, (a, b) in enumerate(pairs)]
@@ -148,13 +165,14 @@
     atoms = rows * devices
     own_tokens = tokens // devices
     token_rows = own_tokens * tiles
-    lead = BLOCK - token_rows
     slots = rows // FEWEST + 1
     position = place()
     first = position * rows
     even = position % 2 == 0
     first_float = first.astype(F32)
-    w_sides[2 * opm :, :] = jnp.zeros((LANES - 2 * opm, tiles * LANES), BF)
+    w_sides[2 * opm : 2 * LANES - 2 * opm, :] = jnp.zeros(
+        (2 * LANES - 4 * opm, tiles * LANES), BF
+    )
 
     for copy in copies[:2]:
         copy.wait()
@@ -174,6 +192,7 @@
         ends[part, :] = passed + dot_t(lower, counts_lane[:, part])
         passed = passed + whole[fold : fold + 1]
 
+    base_token = base.astype(jnp.int32)
     token_lane = iota((SLOTS, tokens), 1).astype(F32)
     slot_token = iota((SLOTS, tokens), 0).astype(F32) + base
     slot_end = dot_t(flag(token_lane <= slot_token), counts_lane)
@@ -194,17 +213,34 @@
 
         here = span(at, DESTS * BLOCK)
         token_at = iota((DESTS * BLOCK, tokens), 1)
-        turn = spread(tokens, 1) - lead
-        row_token = (spread(tokens, 0) + at * DESTS) * own_tokens + turn % own_tokens
+        turn = spread(tokens, 1) % own_tokens
+        row_token = (spread(tokens, 0) + at * DESTS) * own_tokens + turn
         row_end = dot_t(flag(token_at <= row_token), counts_wide)
         row_start = dot_t(flag(token_at < row_token), counts_wide)
         lanes = tiles * rows
         lane = iota((DESTS * BLOCK, lanes), 1)
         atom = (lane % rows + first).astype(F32)
-        turn = spread(lanes, 1) - lead
-        tile_fits = (turn >= 0) & (turn // own_tokens == lane // rows)
+        tile_fits = spread(lanes, 1) // own_tokens == lane // rows
         picks[here, :] = flag(tile_fits & (atom >= row_start) & (atom < row_end))
         row_scale[here, :] = 1.0 / jnp.maximum(row_end - row_start, 1.0)[:, :LANES]
+        lanes = 3 * SLOTS
+        dest = spread(lanes, 0) + at * DESTS
+        spot = spread(lanes, 1)
+        kind = iota((DESTS * BLOCK, lanes), 1) // SLOTS
+        slot = iota((DESTS * BLOCK, lanes), 1) % SLOTS
+        first_own = dest * own_tokens
+        shared_tokens = overlap(base_token, first_own, own_tokens, slots)
+        token = base_token + slot
+        index = jnp.where(token < first_own, slot, slot - shared_tokens)
+        mine = (token >= first_own) & (token < first_own + own_tokens)
+        room = 2 * (BLOCK - SLOT_ROW)
+        target = jnp.where(index < room, SLOT_ROW + index // 2, jnp.where(kind == 0, 0, -1))
+        target = jnp.where(index % 2 == kind, target, -1)
+        is_slot = (kind < 2) & (slot < slots) & jnp.logical_not(mine) & (spot == target)
+        on_edge = spot == edge_row(base_token, first_own, own_tokens, slots)
+        beside = jnp.where(slot == 0, position - 1, position + 1)
+        is_edge = (kind == 2) & (slot < 2) & on_edge & (dest == beside)
+        selects[here, :] = flag(is_slot | is_edge)
 
     repeat(devices // DESTS, rows_step)
 
@@ -223,19 +259,38 @@
         for fold in range(tokens // LANES):
             ended = jnp.where(ends[fold * LANES : (fold + 1) * LANES, :] <= edge, 1.0, 0.0)
             tally = tally + jnp.sum(ended, axis=0, keepdims=True)
-        token = jnp.where(spot < slots, tally.astype(jnp.int32) + spot, -1)
+        start = tally.astype(jnp.int32)
+        first_own = position * own_tokens
+        shared_tokens = overlap(start, first_own, own_tokens, slots)
+
+        def token_of(index):
+            slot = jnp.where(start + index < first_own, index, index + shared_tokens)
+            return jnp.where((index >= 0) & (slot < slots), start + slot, -1)
+
+        in_slots = spot >= SLOT_ROW
+        room = 2 * (BLOCK - SLOT_ROW)
+        ninth = jnp.where((spot == 0) & (shared_tokens == 0), start + room, -1)
+        low_token = jnp.where(in_slots, token_of(2 * (spot - SLOT_ROW)), ninth)
+        high_token = jnp.where(in_slots, token_of(2 * (spot - SLOT_ROW) + 1), -1)
+        own_token = first_own + spot % own_tokens
+        held = (spot < token_rows) & (own_token >= start) & (own_token < start + slots)
+        own_token = jnp.where(held, own_token, -1)
         line = iota((SLOTS, LANES), 0)
-        wanted = jnp.where(
-            line == token_rows,
-            (position - 1) * BLOCK + slots + 1,
-            jnp.where(line == token_rows + 1, (position + 1) * BLOCK + slots, -1),
-        )
-        fixed = (spot_lane == wanted) | ((line < token_rows) & (spot == line + lead))
-        lefts = token == iota((row_tokens, LANES), 0) + first_row
-        rights = token == iota((col_tokens, LANES), 0) + first_col
-        adder[:SLOTS, here] = flag(fixed)
-        adder[SLOTS : SLOTS + row_tokens, here] = flag(lefts)
-        adder[SLOTS + row_tokens :, here] = flag(rights)
+        side = jnp.where(line == token_rows, position - 1, position + 1)
+        on_edge = spot == edge_row(start, first_own, own_tokens, slots)
+        is_edge = (line >= token_rows) & (line < token_rows + 2) & on_edge & (block == side)
+        lines = [(line < token_rows) & (spot == line) & held | is_edge]
+        row_line = iota((row_tokens, LANES), 0) + first_row
+        col_line = iota((col_tokens, LANES), 0) + first_col
+        for wanted in (row_line, col_line):
+            lines += [low_token == wanted, high_token == wanted]
+        for tile in range(tiles):
+            tile_token = jnp.where(spot // own_tokens == tile, own_token, -1)
+            lines += [tile_token == row_line, tile_token == col_line]
+        top = 0
+        for part in lines:
+            adder[top : top + part.shape[0], here] = flag(part)
+            top += part.shape[0]
 
     repeat(devices * BLOCK // LANES, adder_step)
 
@@ -284,6 +339,7 @@
     far_bias,
     picks,
     row_scale,
+    selects,
     member,
     slot_scale,
     before,
@@ -301,7 +357,6 @@
     rows, width = own_float.shape
     tiles = w_pool.shape[1] // LANES
     devices = payload.shape[0] // BLOCK
-    slots = rows // FEWEST + 1
     raw = jnp.concatenate([sibling[...], neighbour[...]], axis=0).astype(F32)
     normed = layer_norm(raw, atom_gain[...]).astype(BF)
     far = dot(normed, w_kv[...]).astype(BF)
@@ -332,24 +387,19 @@
     slot_single = (
         dot(member[...], feature) * jnp.concatenate([slot_scale[...]] * tiles, axis=1)
     ).astype(BF)
-    sides = dot_t(slot_single, w_sides[...])
+    sides = dot_t(slot_single, w_sides[...]).astype(BF)
     backs = dot(slot_single, w_back[...])
     slot_back[...] = backs
     to_before = jnp.sum(backs * before[...], axis=0, keepdims=True)
     to_after = jnp.sum(backs * goes_on[...], axis=0, keepdims=True)
     spot = iota((SLOTS, LANES), 0)
-    shared = jnp.where(
-        spot < slots,
-        sides,
-        jnp.where(spot == slots, to_before, jnp.where(spot == slots + 1, to_after, 0.0)),
-    )
-    shared = jnp.concatenate([shared, jnp.zeros((BLOCK - SLOTS, LANES), F32)], axis=0)
+    edges = jnp.where(spot == 0, to_before, jnp.where(spot == 1, to_after, 0.0)).astype(BF)
+    shared = jnp.concatenate([sides[:, :LANES], sides[:, LANES:], edges], axis=0)
 
     def send_step(at):
         here = span(at, DESTS * BLOCK)
         singles = dot(picks[here, :], feature_tiles) * row_scale[here, :]
-        singles = singles.reshape(DESTS, BLOCK, LANES) + shared[None]
-        payload[here, :] = singles.reshape(DESTS * BLOCK, LANES).astype(BF)
+        payload[here, :] = (singles + dot(selects[here, :], shared)).astype(BF)
 
     repeat(devices // DESTS, send_step)
 
@@ -367,6 +417,7 @@
     w_gate,
     w_lift,
     w_drop,
+    w_sides,
     atom_out,
     token_single,
     pair_out,
@@ -378,8 +429,18 @@
     opm = math.isqrt(w_outer.shape[0])
     added = dot(adder[...], arrived[...])
     half_gate = w_gate[...] * jnp.asarray(0.5, BF)
-    left = added[SLOTS : SLOTS + row_tokens, :opm].astype(BF)
-    right = added[SLOTS + row_tokens :, opm : 2 * opm].astype(BF)
+    parts, top = [], 0
+    for height in (SLOTS,) + (row_tokens,) * 2 + (col_tokens,) * 2 + (row_tokens, col_tokens) * tiles:
+        parts.append(added[top : top + height])
+        top += height
+    sums, left_low, left_high, right_low, right_high, *own = parts
+    own_left = jnp.concatenate(own[0::2], axis=1).astype(BF)
+    own_right = jnp.concatenate(own[1::2], axis=1).astype(BF)
+    own_sides = dot_t(jnp.concatenate([own_left, own_right], axis=0), w_sides[:LANES])
+    left = left_low[:, :opm] + left_high[:, 2 * opm : 3 * opm] + own_sides[:row_tokens, :opm]
+    right = right_low[:, opm : 2 * opm] + right_high[:, 3 * opm : 4 * opm]
+    right = right + own_sides[row_tokens:, opm : 2 * opm]
+    left, right = left.astype(BF), right.astype(BF)
     product_lane = iota((opm, opm * opm), 1)
     unit = iota((opm, opm * opm), 0)
     left_wide = dot(left, flag(product_lane // opm == unit))
@@ -408,11 +469,11 @@
         pair_rows(left_wide[here : here + PAIR_ROWS], here)
 
     token_single[...] = jnp.concatenate(
-        [added[k * own_tokens : (k + 1) * own_tokens] for k in range(tiles)], axis=1
+        [sums[k * own_tokens : (k + 1) * own_tokens] for k in range(tiles)], axis=1
     ).astype(BF)
     spot = iota((SLOTS, LANES), 0)
-    from_before = jnp.where(spot == 0, added[token_rows : token_rows + 1], 0.0)
-    from_after = slot_last[...] * added[token_rows + 1 : token_rows + 2]
+    from_before = jnp.where(spot == 0, sums[token_rows : token_rows + 1], 0.0)
+    from_after = slot_last[...] * sums[token_rows + 1 : token_rows + 2]
     back = (slot_back[...] + from_before + from_after).astype(BF)
     lifted = lax.dot_general(
         slot_member[...], back, (((0,), (0,)), ((), ())), preferred_element_type=F32
@@ -485,19 +546,22 @@
             held(rows, 2 * rows),
             held(devices * BLOCK, tiles * rows, dtype=BF),
             held(devices * BLOCK, LANES),
+            held(devices * BLOCK, 3 * SLOTS, dtype=BF),
             held(SLOTS, rows, dtype=BF),
             held(SLOTS, LANES),
             held(SLOTS, LANES),
             held(SLOTS, LANES),
             held(SLOTS, LANES),
-            held(SLOTS + row_tokens + col_tokens, devices * BLOCK, dtype=BF),
+            held(
+                SLOTS + (2 + tiles) * (row_tokens + col_tokens), devices * BLOCK, dtype=BF
+            ),
             held(1, width),
             held(1, LANES),
             held(width, 2 * width, dtype=BF),
             held(width, width, dtype=BF),
             held(width, channels, dtype=BF),
             held(channels, width, dtype=BF),
-            held(LANES, channels, dtype=BF),
+            held(2 * LANES, channels, dtype=BF),
             held(opm * opm, 2 * w_outer.shape[-1], dtype=BF),
         ),
         far=(
@@ -524,7 +588,7 @@
             pltpu.VMEM(counts_folded.shape, jnp.int32),
             pltpu.VMEM((width, width), BF),
             pltpu.VMEM((tokens, LANES), F32),
-            pltpu.SemaphoreType.DMA((15,)),
+            pltpu.SemaphoreType.DMA((17,)),
         ),
     )
     (
@@ -536,6 +600,7 @@
         far_bias,
         picks,
         row_scale,
+        selects,
         member,
         slot_scale,
         before,
@@ -561,6 +626,7 @@
             far_bias,
             picks,
             row_scale,
+            selects,
             member,
             slot_scale,
             before,
@@ -591,6 +657,7 @@
             w_gate,
             w_lift,
             w_drop,
+            kept[-1],
         ),
         (
             held(rows, width, dtype=BF),

time: 26.5 us -> 25.9 us (0.977)
  blocking collectives: 14.1 us -> 13 us
  Pallas kernels: 6.34 us -> 7.02 us
    all_to_all x1, blocking collectives: 14.1 us -> 13 us  [per_device(): arrived = lax.all_to_all(payload.reshape(devices, BLOCK, LANES), AXES, 0, 0)]
    pallas_call x3, Pallas kernels: 6.34 us -> 7.02 us  [call(): pl.pallas_call(kernel, out_shape=outputs, in_specs=[far_spec] * len(far)...]
  transfers between devices with their start and end apart: 2 -> 2, of which waited for: 0 -> 0; matrix products, arithmetic and copies ran while one was open for 0% -> 0% of each run, Pallas kernels for 9% -> 11%
where the time goes in v11:
time: 25.9 us; the launch traced here: 25.8 us
  blocking collectives  13 us (50%)
  Pallas kernels  7.02 us (27%)
  starting transfers between devices  5.03 us (19%)
  between operations  0.72 us (3%)
    all_to_all x1, blocking collectives, per_device(): arrived = lax.all_to_all(payload.reshape(devices, BLOCK, LANES), AXES, 0, 0)  13 us
    pallas_call x3, Pallas kernels, call(): pl.pallas_call(kernel, out_shape=outputs, in_specs=[far_spec] * len(far)...  7.02 us
    ppermute x1, starting transfers between devices, per_device(): lax.ppermute(atom_feats, AXES, [(i, i ^ 1) for i in range(devices)])  4.36 us
    ppermute x1, starting transfers between devices, per_device(): lax.ppermute(atom_feats, AXES, across + [(j, i) for i, j in across])  0.66 us
  transfers between devices with their start and end apart: 2, of which 0 were waited for; matrix products, arithmetic and copies ran while one was open for 0% of the time, Pallas kernels for 11%

profile of v11, /device:TPU:0, one launch (start us, length us, event | category | flops | bytes accessed | tf_op | source)
XLA Modules:
  0.0 25.8 jit_solution(3831327021749320734)
XLA Ops:
  0.6 0.7 %collective-permute-start = (bf16[64,128]{1,0:T(8,128)(2,1)}, bf16[64,128]{1,0:T(8,128)(2,1)S(1)}, u32[]{:S(2)}, u32[]{:S(2)}) collective-permute-start(bf16[64,128]{1,0:T(8,128)(2,1)} %own_far.1), channel_id=1, source_target_pairs={{1,2},{3,4},{5,6},{7,8},{9,10},{11,12},{13,14},{15,16},{17,18},{19... | collective-permute-start | bytes 49160 | tf_op jit(solution)/shard_map/ppermute | solution.py:529
  1.3 4.4 %collective-permute-start.1 = (bf16[64,128]{1,0:T(8,128)(2,1)}, bf16[64,128]{1,0:T(8,128)(2,1)S(1)}, u32[]{:S(2)}, u32[]{:S(2)}) collective-permute-start(bf16[64,128]{1,0:T(8,128)(2,1)} %own_far.1), channel_id=1, source_target_pairs={{0,1},{1,0},{2,3},{3,2},{4,5},{5,4},{6,7},{7,6},{8,9},{9,8},{10,11... | collective-permute-start | bytes 49160 | tf_op jit(solution)/shard_map/ppermute | solution.py:530
  5.7 2.8 %ready.1 = (f32[64,128]{1,0:T(8,128)S(1)}, bf16[64,256]{1,0:T(8,128)(2,1)S(1)}, bf16[256,128]{1,0:T(8,128)(2,1)S(1)}, f32[256,64]{1,0:T(8,128)S(1)}, f32[256,1]{...) custom-call(bf16[64,128]{1,0:T(8,128)(2,1)} %own_far.1, ...), custom_call_target="tpu_custom_call" | custom-call | tf_op jit(solution)/shard_map/ready/pallas_call | solution.py:488
  8.5 0.0 collective-permute-done.neighbour
  8.5 0.0 collective-permute-done.1.sibling
  8.5 0.0 copy-start.2
  8.5 0.0 copy-start.3
  8.5 1.6 %atoms.1 = (bf16[512,128]{1,0:T(8,128)(2,1)S(1)}, bf16[64,128]{1,0:T(8,128)(2,1)S(1)}, f32[16,128]{1,0:T(8,128)S(1)}) custom-call(bf16[64,128]{1,0:T(8,128)(2,1)S(1)} %collective-permute-done.neighbour, bf16[64,128]{1,0:T(8,128)(2,1)S(1)} %collective-permute-done.1.sibling, f32[64,128]{1,0:T(8,128)S(1)} %get-tuple-element.29.own_float, ...), custom_call_target="tpu_custom_call" | custom-call | tf_op jit(solution)/shard_map/atoms/pallas_call | solution.py:488
  10.1 0.0 copy-start
  10.1 0.0 copy-start.1
  10.1 13.0 %all_to_all.5 = bf16[32,16,128]{2,1,0:T(8,128)(2,1)S(1)} all-to-all(bf16[32,16,128]{2,1,0:T(8,128)(2,1)S(1)} %bitcast.10), channel_id=1, replica_groups=mesh['row'=8,'col'=4] {'row','col'}, dimensions={0} | all-to-all | bytes 262144 | tf_op jit(solution)/shard_map/all_to_all | solution.py:643
  23.1 0.0 copy-done.2
  23.1 0.0 copy-done.3
  23.1 0.0 copy-done
  23.1 0.0 copy-done.1
  23.1 2.7 %pairs.1 = (bf16[64,128]{1,0:T(8,128)(2,1)}, bf16[4,384]{1,0:T(4,128)(2,1)}, bf16[16,32,128]{2,1,0:T(8,128)(2,1)}) custom-call(bf16[512,128]{1,0:T(8,128)(2,1)S(1)} %bitcast.9, bf16[256,512]{1,0:T(8,128)(2,1)S(1)} %get-tuple-element.49.adder, bf16[64,128]{1,0:T(8,128)(2,1)S(1)} %get-tuple-element.50.updated, f32[16,128]{1,0:T(8,128)S(1)} %get-tuple-element.51.slot_back, ...), custom_call_target="tpu_custom_call" | custom-call | tf_op jit(solution)/shard_map/pairs/pallas_call | solution.py:488
Async XLA Ops:
  0.6 7.8 %collective-permute-start = (bf16[64,128]{1,0:T(8,128)(2,1)}, bf16[64,128]{1,0:T(8,128)(2,1)S(1)}, u32[]{:S(2)}, u32[]{:S(2)}) collective-permute-start(bf16[64,128]{1,0:T(8,128)(2,1)} %own_far.1), channel_id=1, source_target_pairs={{1,2},{3,4},{5,6},{7,8},{9,10},{11,12},{13,14},{15,16},{17,18},{19... | collective-permute-start | bytes 49160 | tf_op jit(solution)/shard_map/ppermute | solution.py:529
  1.3 7.2 %collective-permute-start.1 = (bf16[64,128]{1,0:T(8,128)(2,1)}, bf16[64,128]{1,0:T(8,128)(2,1)S(1)}, u32[]{:S(2)}, u32[]{:S(2)}) collective-permute-start(bf16[64,128]{1,0:T(8,128)(2,1)} %own_far.1), channel_id=1, source_target_pairs={{0,1},{1,0},{2,3},{3,2},{4,5},{5,4},{6,7},{7,6},{8,9},{9,8},{10,11... | collective-permute-start | bytes 49160 | tf_op jit(solution)/shard_map/ppermute | solution.py:530
  8.5 14.6 %copy-start.2 = (bf16[128,512]{1,0:T(8,128)(2,1)S(1)}, bf16[128,512]{1,0:T(8,128)(2,1)}, u32[]{:S(2)}) copy-start(bf16[128,512]{1,0:T(8,128)(2,1)} %w_lift.1) | copy-start | bytes 393220
  8.5 14.6 %copy-start.3 = (bf16[512,128]{1,0:T(8,128)(2,1)S(1)}, bf16[512,128]{1,0:T(8,128)(2,1)}, u32[]{:S(2)}) copy-start(bf16[512,128]{1,0:T(8,128)(2,1)} %w_drop.1) | copy-start | bytes 393220
  10.1 13.0 %copy-start = (bf16[16,32,128]{2,1,0:T(8,128)(2,1)S(1)}, bf16[16,32,128]{2,1,0:T(8,128)(2,1)}, u32[]{:S(2)}) copy-start(bf16[16,32,128]{2,1,0:T(8,128)(2,1)} %pair_state.1) | copy-start | bytes 393220
  10.1 13.0 %copy-start.1 = (bf16[128,512]{1,0:T(8,128)(2,1)S(1)}, bf16[128,512]{1,0:T(8,128)(2,1)}, u32[]{:S(2)}) copy-start(bf16[128,512]{1,0:T(8,128)(2,1)} %w_gate.1) | copy-start | bytes 393220

commit v12 on v11

--- a/solution.py
+++ b/solution.py
@@ -28,13 +28,6 @@
 F32 = jnp.float32
 
 
-def layer_norm(values, gain):
-    mean_value = jnp.mean(values, axis=-1, keepdims=True)
-    centred = values - mean_value
-    variance = jnp.mean(centred * centred, axis=-1, keepdims=True)
-    return centred * lax.rsqrt(variance + EPSILON) * gain
-
-
 def dot(a, b):
     return jnp.dot(a, b, preferred_element_type=F32)
 
@@ -45,6 +38,14 @@
 
 def iota(shape, axis):
     return lax.broadcasted_iota(jnp.int32, shape, axis)
+
+
+def centred_rows(values, gain):
+    width = values.shape[1]
+    average = jnp.full((width, width), 1.0 / width, F32).astype(BF)
+    centred = values.astype(F32) - dot(values, average)
+    variance = dot((centred * centred).astype(BF), average)
+    return (centred * gain).astype(BF), lax.rsqrt(variance + EPSILON)
 
 
 def flag(mask):
@@ -174,7 +175,7 @@
         (2 * LANES - 4 * opm, tiles * LANES), BF
     )
 
-    for copy in copies[:2]:
+    for copy in copies[:8]:
         copy.wait()
     counts_wide = jnp.broadcast_to(counts[...].astype(F32), (tiles * rows, tokens)).astype(BF)
     counts_lane = counts_wide[:LANES]
@@ -294,14 +295,11 @@
 
     repeat(devices * BLOCK // LANES, adder_step)
 
-    for copy in copies[2:8]:
-        copy.wait()
-    raw = own[...].astype(F32)
-    own_float[...] = raw
-    normed = layer_norm(raw, atom_gain[...]).astype(BF)
-    near = dot(normed, w_kv[...]).astype(BF)
+    own_float[...] = own[...].astype(F32)
+    normed, scaling = centred_rows(own[...], atom_gain[...])
+    near = (dot(normed, w_kv[...]) * jnp.concatenate([scaling] * 2, axis=1)).astype(BF)
     keyval[...] = near
-    query = dot(normed, w_query[...]).astype(BF)
+    query = (dot(normed, w_query[...]) * scaling).astype(BF)
     head_of = iota((1, width), 1) // (width // HEADS)
     heads = jnp.concatenate([query * flag(head_of == h) for h in range(HEADS)], axis=0)
     stacked[...] = heads
@@ -357,9 +355,9 @@
     rows, width = own_float.shape
     tiles = w_pool.shape[1] // LANES
     devices = payload.shape[0] // BLOCK
-    raw = jnp.concatenate([sibling[...], neighbour[...]], axis=0).astype(F32)
-    normed = layer_norm(raw, atom_gain[...]).astype(BF)
-    far = dot(normed, w_kv[...]).astype(BF)
+    raw = jnp.concatenate([sibling[...], neighbour[...]], axis=0)
+    normed, scaling = centred_rows(raw, atom_gain[...])
+    far = (dot(normed, w_kv[...]) * jnp.concatenate([scaling] * 2, axis=1)).astype(BF)
     far_scores = dot_t(stacked[...], far[:, :width])
     far_scores = far_scores + jnp.concatenate([far_bias[...]] * HEADS, axis=0)
     most = jnp.maximum(top[...], jnp.max(far_scores, axis=-1, keepdims=True))
@@ -444,22 +442,28 @@
     product_lane = iota((opm, opm * opm), 1)
     unit = iota((opm, opm * opm), 0)
     left_wide = dot(left, flag(product_lane // opm == unit))
-    right_wide = dot(right, flag(product_lane % opm == unit))
+    rights = dot(right, flag(product_lane % opm == unit)).astype(BF)
 
     average = jnp.full((pair_width, pair_width), 1.0 / pair_width, F32).astype(BF)
 
     def pair_rows(lefts, here):
-        products = jnp.concatenate(
-            [(lefts[i : i + 1, :] * right_wide).astype(BF) for i in range(PAIR_ROWS)], axis=0
-        )
+        products = []
+        for i in range(PAIR_ROWS):
+            spread = jnp.broadcast_to(lefts[i : i + 1, :], (SLOTS, lefts.shape[1])).astype(BF)
+            products += [
+                spread * rights[at : at + SLOTS] for at in range(0, col_tokens, SLOTS)
+            ]
+        products = jnp.concatenate(products, axis=0)
         flat = pair_state[pl.ds(here, PAIR_ROWS)].reshape(PAIR_ROWS * col_tokens, pair_width)
         outer = dot(products, w_outer[...])
         summed = flat.astype(F32) + outer[:, :pair_width]
         centred = summed - (dot(flat, average) + outer[:, pair_width:])
         variance = dot((centred * centred).astype(BF), average)
-        normed = (centred * lax.rsqrt(variance + EPSILON) * pair_gain[...]).astype(BF)
-        gate = dot(normed, half_gate)
-        lift = dot(normed, w_lift[...])
+        scaling = lax.rsqrt(variance + EPSILON)
+        normed = (centred * pair_gain[...]).astype(BF)
+        wide = jnp.concatenate([scaling] * (w_lift.shape[1] // pair_width), axis=1)
+        gate = dot(normed, half_gate) * wide
+        lift = dot(normed, w_lift[...]) * wide
         hidden = (gate * lift * (1.0 + jnp.tanh(gate))).astype(BF)
         result = (summed + dot(hidden, w_drop[...])).astype(BF)
         pair_out[pl.ds(here, PAIR_ROWS)] = result.reshape(PAIR_ROWS, col_tokens, pair_width)

time: 25.9 us -> 25.8 us (level)
  transfers between devices with their start and end apart: 2 -> 2, of which waited for: 0 -> 0; matrix products, arithmetic and copies ran while one was open for 0% -> 0% of each run, Pallas kernels for 11% -> 10%
where the time goes in v12:
time: 25.8 us; the launch traced here: 25.6 us
  blocking collectives  13.1 us (51%)
  Pallas kernels  6.77 us (26%)
  starting transfers between devices  5.03 us (19%)
  between operations  0.72 us (3%)
    all_to_all x1, blocking collectives, per_device(): arrived = lax.all_to_all(payload.reshape(devices, BLOCK, LANES), AXES, 0, 0)  13.1 us
    pallas_call x3, Pallas kernels, call(): pl.pallas_call(kernel, out_shape=outputs, in_specs=[far_spec] * len(far)...  6.77 us
    ppermute x1, starting transfers between devices, per_device(): lax.ppermute(atom_feats, AXES, [(i, i ^ 1) for i in range(devices)])  4.36 us
    ppermute x1, starting transfers between devices, per_device(): lax.ppermute(atom_feats, AXES, across + [(j, i) for i, j in across])  0.66 us
  transfers between devices with their start and end apart: 2, of which 0 were waited for; matrix products, arithmetic and copies ran while one was open for 0% of the time, Pallas kernels for 10%

profile of v12, /device:TPU:0, one launch (start us, length us, event | category | flops | bytes accessed | tf_op | source)
XLA Modules:
  0.0 25.6 jit_solution(17953279019271872565)
XLA Ops:
  0.6 0.7 %collective-permute-start = (bf16[64,128]{1,0:T(8,128)(2,1)}, bf16[64,128]{1,0:T(8,128)(2,1)S(1)}, u32[]{:S(2)}, u32[]{:S(2)}) collective-permute-start(bf16[64,128]{1,0:T(8,128)(2,1)} %own_far.1), channel_id=1, source_target_pairs={{1,2},{3,4},{5,6},{7,8},{9,10},{11,12},{13,14},{15,16},{17,18},{19... | collective-permute-start | bytes 49160 | tf_op jit(solution)/shard_map/ppermute | solution.py:533
  1.3 4.4 %collective-permute-start.1 = (bf16[64,128]{1,0:T(8,128)(2,1)}, bf16[64,128]{1,0:T(8,128)(2,1)S(1)}, u32[]{:S(2)}, u32[]{:S(2)}) collective-permute-start(bf16[64,128]{1,0:T(8,128)(2,1)} %own_far.1), channel_id=1, source_target_pairs={{0,1},{1,0},{2,3},{3,2},{4,5},{5,4},{6,7},{7,6},{8,9},{9,8},{10,11... | collective-permute-start | bytes 49160 | tf_op jit(solution)/shard_map/ppermute | solution.py:534
  5.7 2.7 %ready.1 = (f32[64,128]{1,0:T(8,128)S(1)}, bf16[64,256]{1,0:T(8,128)(2,1)S(1)}, bf16[256,128]{1,0:T(8,128)(2,1)S(1)}, f32[256,64]{1,0:T(8,128)S(1)}, f32[256,1]{...) custom-call(bf16[64,128]{1,0:T(8,128)(2,1)} %own_far.1, ...), custom_call_target="tpu_custom_call" | custom-call | tf_op jit(solution)/shard_map/ready/pallas_call | solution.py:492
  8.3 0.0 collective-permute-done.neighbour
  8.3 0.0 collective-permute-done.1.sibling
  8.4 0.0 copy-start.2
  8.4 0.0 copy-start.3
  8.4 1.5 %atoms.1 = (bf16[512,128]{1,0:T(8,128)(2,1)S(1)}, bf16[64,128]{1,0:T(8,128)(2,1)S(1)}, f32[16,128]{1,0:T(8,128)S(1)}) custom-call(bf16[64,128]{1,0:T(8,128)(2,1)S(1)} %collective-permute-done.neighbour, bf16[64,128]{1,0:T(8,128)(2,1)S(1)} %collective-permute-done.1.sibling, f32[64,128]{1,0:T(8,128)S(1)} %get-tuple-element.29.own_float, ...), custom_call_target="tpu_custom_call" | custom-call | tf_op jit(solution)/shard_map/atoms/pallas_call | solution.py:492
  9.9 0.0 copy-start
  9.9 0.0 copy-start.1
  9.9 13.1 %all_to_all.5 = bf16[32,16,128]{2,1,0:T(8,128)(2,1)S(1)} all-to-all(bf16[32,16,128]{2,1,0:T(8,128)(2,1)S(1)} %bitcast.10), channel_id=1, replica_groups=mesh['row'=8,'col'=4] {'row','col'}, dimensions={0} | all-to-all | bytes 262144 | tf_op jit(solution)/shard_map/all_to_all | solution.py:647
  23.0 0.0 copy-done.2
  23.0 0.0 copy-done.3
  23.0 0.0 copy-done
  23.0 0.0 copy-done.1
  23.0 2.6 %pairs.1 = (bf16[64,128]{1,0:T(8,128)(2,1)}, bf16[4,384]{1,0:T(4,128)(2,1)}, bf16[16,32,128]{2,1,0:T(8,128)(2,1)}) custom-call(bf16[512,128]{1,0:T(8,128)(2,1)S(1)} %bitcast.9, bf16[256,512]{1,0:T(8,128)(2,1)S(1)} %get-tuple-element.49.adder, bf16[64,128]{1,0:T(8,128)(2,1)S(1)} %get-tuple-element.50.updated, f32[16,128]{1,0:T(8,128)S(1)} %get-tuple-element.51.slot_back, ...), custom_call_target="tpu_custom_call" | custom-call | tf_op jit(solution)/shard_map/pairs/pallas_call | solution.py:492
Async XLA Ops:
  0.6 7.7 %collective-permute-start = (bf16[64,128]{1,0:T(8,128)(2,1)}, bf16[64,128]{1,0:T(8,128)(2,1)S(1)}, u32[]{:S(2)}, u32[]{:S(2)}) collective-permute-start(bf16[64,128]{1,0:T(8,128)(2,1)} %own_far.1), channel_id=1, source_target_pairs={{1,2},{3,4},{5,6},{7,8},{9,10},{11,12},{13,14},{15,16},{17,18},{19... | collective-permute-start | bytes 49160 | tf_op jit(solution)/shard_map/ppermute | solution.py:533
  1.3 7.0 %collective-permute-start.1 = (bf16[64,128]{1,0:T(8,128)(2,1)}, bf16[64,128]{1,0:T(8,128)(2,1)S(1)}, u32[]{:S(2)}, u32[]{:S(2)}) collective-permute-start(bf16[64,128]{1,0:T(8,128)(2,1)} %own_far.1), channel_id=1, source_target_pairs={{0,1},{1,0},{2,3},{3,2},{4,5},{5,4},{6,7},{7,6},{8,9},{9,8},{10,11... | collective-permute-start | bytes 49160 | tf_op jit(solution)/shard_map/ppermute | solution.py:534
  8.4 14.6 %copy-start.2 = (bf16[128,512]{1,0:T(8,128)(2,1)S(1)}, bf16[128,512]{1,0:T(8,128)(2,1)}, u32[]{:S(2)}) copy-start(bf16[128,512]{1,0:T(8,128)(2,1)} %w_lift.1) | copy-start | bytes 393220
  8.4 14.6 %copy-start.3 = (bf16[512,128]{1,0:T(8,128)(2,1)S(1)}, bf16[512,128]{1,0:T(8,128)(2,1)}, u32[]{:S(2)}) copy-start(bf16[512,128]{1,0:T(8,128)(2,1)} %w_drop.1) | copy-start | bytes 393220
  9.9 13.1 %copy-start = (bf16[16,32,128]{2,1,0:T(8,128)(2,1)S(1)}, bf16[16,32,128]{2,1,0:T(8,128)(2,1)}, u32[]{:S(2)}) copy-start(bf16[16,32,128]{2,1,0:T(8,128)(2,1)} %pair_state.1) | copy-start | bytes 393220
  9.9 13.1 %copy-start.1 = (bf16[128,512]{1,0:T(8,128)(2,1)S(1)}, bf16[128,512]{1,0:T(8,128)(2,1)}, u32[]{:S(2)}) copy-start(bf16[128,512]{1,0:T(8,128)(2,1)} %w_gate.1) | copy-start | bytes 393220

commit v13 on v12

--- a/solution.py
+++ b/solution.py
@@ -19,6 +19,7 @@
 SLOT_ROW = 12
 DESTS = 32
 PAIR_ROWS = 16
+GROUP = 8
 MASKED = -1e30
 SPARE = 12 << 20
 MOST = 60 << 20
@@ -439,38 +440,65 @@
     right = right_low[:, opm : 2 * opm] + right_high[:, 3 * opm : 4 * opm]
     right = right + own_sides[row_tokens:, opm : 2 * opm]
     left, right = left.astype(BF), right.astype(BF)
-    product_lane = iota((opm, opm * opm), 1)
-    unit = iota((opm, opm * opm), 0)
-    left_wide = dot(left, flag(product_lane // opm == unit))
-    rights = dot(right, flag(product_lane % opm == unit)).astype(BF)
-
-    average = jnp.full((pair_width, pair_width), 1.0 / pair_width, F32).astype(BF)
-
-    def pair_rows(lefts, here):
-        products = []
-        for i in range(PAIR_ROWS):
-            spread = jnp.broadcast_to(lefts[i : i + 1, :], (SLOTS, lefts.shape[1])).astype(BF)
-            products += [
-                spread * rights[at : at + SLOTS] for at in range(0, col_tokens, SLOTS)
-            ]
-        products = jnp.concatenate(products, axis=0)
+    depth = GROUP * opm
+    unit = flag(iota((opm, depth), 1) % opm == iota((opm, depth), 0))
+    corner = jnp.where(iota((GROUP, depth), 1) // opm == iota((GROUP, depth), 0), 1.0, 0.0)
+
+    def spread(rows_of, first, count):
+        return jnp.concatenate(
+            [
+                jnp.broadcast_to(rows_of[k : k + 1, :], (GROUP, depth)) * corner
+                for k in range(first, first + count)
+            ],
+            axis=0,
+        ).astype(BF)
+
+    left_wide = dot(left, unit)
+    right_blocks = spread(dot(right, unit), 0, col_tokens)
+    stages = opm // GROUP
+    table = [
+        dot(right_blocks, w_outer[g * depth : (g + 1) * depth, :]) for g in range(stages)
+    ]
+    tables = [
+        jnp.concatenate(
+            [
+                table[g][j * GROUP : (j + 1) * GROUP]
+                for j in range(h * GROUP, (h + 1) * GROUP)
+                for g in range(stages)
+            ],
+            axis=0,
+        ).astype(BF)
+        for h in range(col_tokens // GROUP)
+    ]
+
+    def pair_rows(here):
+        left_blocks = spread(left_wide, here, PAIR_ROWS)
+        terms = [dot(left_blocks, part) for part in tables]
+        outer = jnp.concatenate(
+            [
+                term[i * GROUP : (i + 1) * GROUP]
+                for i in range(PAIR_ROWS)
+                for term in terms
+            ],
+            axis=0,
+        )
         flat = pair_state[pl.ds(here, PAIR_ROWS)].reshape(PAIR_ROWS * col_tokens, pair_width)
-        outer = dot(products, w_outer[...])
-        summed = flat.astype(F32) + outer[:, :pair_width]
-        centred = summed - (dot(flat, average) + outer[:, pair_width:])
-        variance = dot((centred * centred).astype(BF), average)
+        flat = flat.astype(F32)
+        summed = flat + outer[:, :pair_width]
+        pair_mean = jnp.mean(flat, axis=-1, keepdims=True)
+        centred = summed - (pair_mean + outer[:, pair_width:])
+        variance = jnp.mean(centred * centred, axis=-1, keepdims=True)
         scaling = lax.rsqrt(variance + EPSILON)
         normed = (centred * pair_gain[...]).astype(BF)
-        wide = jnp.concatenate([scaling] * (w_lift.shape[1] // pair_width), axis=1)
-        gate = dot(normed, half_gate) * wide
-        lift = dot(normed, w_lift[...]) * wide
+        gate = dot(normed, half_gate) * scaling
+        lift = dot(normed, w_lift[...]) * scaling
         hidden = (gate * lift * (1.0 + jnp.tanh(gate))).astype(BF)
         result = (summed + dot(hidden, w_drop[...])).astype(BF)
         pair_out[pl.ds(here, PAIR_ROWS)] = result.reshape(PAIR_ROWS, col_tokens, pair_width)
 
     for step in range(row_tokens // PAIR_ROWS):
         here = step * PAIR_ROWS
-        pair_rows(left_wide[here : here + PAIR_ROWS], here)
+        pair_rows(here)
 
     token_single[...] = jnp.concatenate(
         [sums[k * own_tokens : (k + 1) * own_tokens] for k in range(tiles)], axis=1

time: 25.8 us -> 25.4 us (0.984)
  Pallas kernels: 6.77 us -> 6.39 us
    pallas_call x3, Pallas kernels: 6.77 us -> 6.39 us  [call(): pl.pallas_call(kernel, out_shape=outputs, in_specs=[far_spec] * len(far)...]
  transfers between devices with their start and end apart: 2 -> 2, of which waited for: 0 -> 0; matrix products, arithmetic and copies ran while one was open for 0% -> 0% of each run, Pallas kernels for 10% -> 11%
where the time goes in v13:
time: 25.4 us; the launch traced here: 25.2 us
  blocking collectives  13.1 us (52%)
  Pallas kernels  6.39 us (25%)
  starting transfers between devices  5.03 us (20%)
  between operations  0.72 us (3%)
    all_to_all x1, blocking collectives, per_device(): arrived = lax.all_to_all(payload.reshape(devices, BLOCK, LANES), AXES, 0, 0)  13.1 us
    pallas_call x3, Pallas kernels, call(): pl.pallas_call(kernel, out_shape=outputs, in_specs=[far_spec] * len(far)...  6.39 us
    ppermute x1, starting transfers between devices, per_device(): lax.ppermute(atom_feats, AXES, [(i, i ^ 1) for i in range(devices)])  4.36 us
    ppermute x1, starting transfers between devices, per_device(): lax.ppermute(atom_feats, AXES, across + [(j, i) for i, j in across])  0.66 us
  transfers between devices with their start and end apart: 2, of which 0 were waited for; matrix products, arithmetic and copies ran while one was open for 0% of the time, Pallas kernels for 11%

profile of v13, /device:TPU:0, one launch (start us, length us, event | category | flops | bytes accessed | tf_op | source)
XLA Modules:
  0.0 25.2 jit_solution(4911215909943431953)
XLA Ops:
  0.6 0.7 %collective-permute-start = (bf16[64,128]{1,0:T(8,128)(2,1)}, bf16[64,128]{1,0:T(8,128)(2,1)S(1)}, u32[]{:S(2)}, u32[]{:S(2)}) collective-permute-start(bf16[64,128]{1,0:T(8,128)(2,1)} %own_far.1), channel_id=1, source_target_pairs={{1,2},{3,4},{5,6},{7,8},{9,10},{11,12},{13,14},{15,16},{17,18},{19... | collective-permute-start | bytes 49160 | tf_op jit(solution)/shard_map/ppermute | solution.py:561
  1.3 4.4 %collective-permute-start.1 = (bf16[64,128]{1,0:T(8,128)(2,1)}, bf16[64,128]{1,0:T(8,128)(2,1)S(1)}, u32[]{:S(2)}, u32[]{:S(2)}) collective-permute-start(bf16[64,128]{1,0:T(8,128)(2,1)} %own_far.1), channel_id=1, source_target_pairs={{0,1},{1,0},{2,3},{3,2},{4,5},{5,4},{6,7},{7,6},{8,9},{9,8},{10,11... | collective-permute-start | bytes 49160 | tf_op jit(solution)/shard_map/ppermute | solution.py:562
  5.7 2.7 %ready.1 = (f32[64,128]{1,0:T(8,128)S(1)}, bf16[64,256]{1,0:T(8,128)(2,1)S(1)}, bf16[256,128]{1,0:T(8,128)(2,1)S(1)}, f32[256,64]{1,0:T(8,128)S(1)}, f32[256,1]{...) custom-call(bf16[64,128]{1,0:T(8,128)(2,1)} %own_far.1, ...), custom_call_target="tpu_custom_call" | custom-call | tf_op jit(solution)/shard_map/ready/pallas_call | solution.py:520
  8.3 0.0 collective-permute-done.neighbour
  8.3 0.0 collective-permute-done.1.sibling
  8.4 0.0 copy-start.2
  8.4 0.0 copy-start.3
  8.4 1.5 %atoms.1 = (bf16[512,128]{1,0:T(8,128)(2,1)S(1)}, bf16[64,128]{1,0:T(8,128)(2,1)S(1)}, f32[16,128]{1,0:T(8,128)S(1)}) custom-call(bf16[64,128]{1,0:T(8,128)(2,1)S(1)} %collective-permute-done.neighbour, bf16[64,128]{1,0:T(8,128)(2,1)S(1)} %collective-permute-done.1.sibling, f32[64,128]{1,0:T(8,128)S(1)} %get-tuple-element.29.own_float, ...), custom_call_target="tpu_custom_call" | custom-call | tf_op jit(solution)/shard_map/atoms/pallas_call | solution.py:520
  9.9 0.0 copy-start
  9.9 0.0 copy-start.1
  9.9 13.1 %all_to_all.5 = bf16[32,16,128]{2,1,0:T(8,128)(2,1)S(1)} all-to-all(bf16[32,16,128]{2,1,0:T(8,128)(2,1)S(1)} %bitcast.10), channel_id=1, replica_groups=mesh['row'=8,'col'=4] {'row','col'}, dimensions={0} | all-to-all | bytes 262144 | tf_op jit(solution)/shard_map/all_to_all | solution.py:675
  23.0 0.0 copy-done.2
  23.0 0.0 copy-done.3
  23.0 0.0 copy-done
  23.0 0.0 copy-done.1
  23.0 2.2 %pairs.1 = (bf16[64,128]{1,0:T(8,128)(2,1)}, bf16[4,384]{1,0:T(4,128)(2,1)}, bf16[16,32,128]{2,1,0:T(8,128)(2,1)}) custom-call(bf16[512,128]{1,0:T(8,128)(2,1)S(1)} %bitcast.9, bf16[256,512]{1,0:T(8,128)(2,1)S(1)} %get-tuple-element.49.adder, bf16[64,128]{1,0:T(8,128)(2,1)S(1)} %get-tuple-element.50.updated, f32[16,128]{1,0:T(8,128)S(1)} %get-tuple-element.51.slot_back, ...), custom_call_target="tpu_custom_call" | custom-call | tf_op jit(solution)/shard_map/pairs/pallas_call | solution.py:520
Async XLA Ops:
  0.6 7.7 %collective-permute-start = (bf16[64,128]{1,0:T(8,128)(2,1)}, bf16[64,128]{1,0:T(8,128)(2,1)S(1)}, u32[]{:S(2)}, u32[]{:S(2)}) collective-permute-start(bf16[64,128]{1,0:T(8,128)(2,1)} %own_far.1), channel_id=1, source_target_pairs={{1,2},{3,4},{5,6},{7,8},{9,10},{11,12},{13,14},{15,16},{17,18},{19... | collective-permute-start | bytes 49160 | tf_op jit(solution)/shard_map/ppermute | solution.py:561
  1.3 7.0 %collective-permute-start.1 = (bf16[64,128]{1,0:T(8,128)(2,1)}, bf16[64,128]{1,0:T(8,128)(2,1)S(1)}, u32[]{:S(2)}, u32[]{:S(2)}) collective-permute-start(bf16[64,128]{1,0:T(8,128)(2,1)} %own_far.1), channel_id=1, source_target_pairs={{0,1},{1,0},{2,3},{3,2},{4,5},{5,4},{6,7},{7,6},{8,9},{9,8},{10,11... | collective-permute-start | bytes 49160 | tf_op jit(solution)/shard_map/ppermute | solution.py:562
  8.4 14.6 %copy-start.2 = (bf16[128,512]{1,0:T(8,128)(2,1)S(1)}, bf16[128,512]{1,0:T(8,128)(2,1)}, u32[]{:S(2)}) copy-start(bf16[128,512]{1,0:T(8,128)(2,1)} %w_lift.1) | copy-start | bytes 393220
  8.4 14.6 %copy-start.3 = (bf16[512,128]{1,0:T(8,128)(2,1)S(1)}, bf16[512,128]{1,0:T(8,128)(2,1)}, u32[]{:S(2)}) copy-start(bf16[512,128]{1,0:T(8,128)(2,1)} %w_drop.1) | copy-start | bytes 393220
  9.9 13.1 %copy-start = (bf16[16,32,128]{2,1,0:T(8,128)(2,1)S(1)}, bf16[16,32,128]{2,1,0:T(8,128)(2,1)}, u32[]{:S(2)}) copy-start(bf16[16,32,128]{2,1,0:T(8,128)(2,1)} %pair_state.1) | copy-start | bytes 393220
  9.9 13.1 %copy-start.1 = (bf16[128,512]{1,0:T(8,128)(2,1)S(1)}, bf16[128,512]{1,0:T(8,128)(2,1)}, u32[]{:S(2)}) copy-start(bf16[128,512]{1,0:T(8,128)(2,1)} %w_gate.1) | copy-start | bytes 393220

commit v14 on v13

--- a/solution.py
+++ b/solution.py
@@ -106,8 +106,8 @@
     w_right_far,
     w_outer_far,
     own_float,
-    keyval,
-    stacked,
+    own_mixed,
+    probes,
     scores,
     top,
     far_bias,
@@ -122,8 +122,7 @@
     adder,
     atom_gain,
     pair_gain,
-    w_kv,
-    w_out,
+    w_mixed,
     w_pool,
     w_back,
     w_sides,
@@ -133,6 +132,9 @@
     counts,
     counts_folded,
     w_query,
+    w_key,
+    w_value,
+    w_out,
     ends,
     arrivals,
 ):
@@ -146,10 +148,10 @@
         (starts_far, key_starts),
         (atom_gain_far, atom_gain),
         (w_query_far, w_query),
-        (w_key_far, w_kv.at[:, :width]),
-        (w_value_far, w_kv.at[:, width:]),
+        (w_key_far, w_key),
+        (w_value_far, w_value),
+        (w_out_far, w_out),
         (pair_gain_far, pair_gain),
-        (w_out_far, w_out),
         (w_pool_far, w_pool),
         (w_back_far, w_back),
         (w_left_far, w_sides.at[:opm]),
@@ -176,7 +178,7 @@
         (2 * LANES - 4 * opm, tiles * LANES), BF
     )
 
-    for copy in copies[:8]:
+    for copy in copies[:9]:
         copy.wait()
     counts_wide = jnp.broadcast_to(counts[...].astype(F32), (tiles * rows, tokens)).astype(BF)
     counts_lane = counts_wide[:LANES]
@@ -214,13 +216,13 @@
             return iota((DESTS, BLOCK, lanes), axis).reshape(DESTS * BLOCK, lanes)
 
         here = span(at, DESTS * BLOCK)
-        token_at = iota((DESTS * BLOCK, tokens), 1)
+        token_at = iota((1, tokens), 1)
         turn = spread(tokens, 1) % own_tokens
         row_token = (spread(tokens, 0) + at * DESTS) * own_tokens + turn
         row_end = dot_t(flag(token_at <= row_token), counts_wide)
         row_start = dot_t(flag(token_at < row_token), counts_wide)
         lanes = tiles * rows
-        lane = iota((DESTS * BLOCK, lanes), 1)
+        lane = iota((1, lanes), 1)
         atom = (lane % rows + first).astype(F32)
         tile_fits = spread(lanes, 1) // own_tokens == lane // rows
         picks[here, :] = flag(tile_fits & (atom >= row_start) & (atom < row_end))
@@ -228,8 +230,8 @@
         lanes = 3 * SLOTS
         dest = spread(lanes, 0) + at * DESTS
         spot = spread(lanes, 1)
-        kind = iota((DESTS * BLOCK, lanes), 1) // SLOTS
-        slot = iota((DESTS * BLOCK, lanes), 1) % SLOTS
+        kind = iota((1, lanes), 1) // SLOTS
+        slot = iota((1, lanes), 1) % SLOTS
         first_own = dest * own_tokens
         shared_tokens = overlap(base_token, first_own, own_tokens, slots)
         token = base_token + slot
@@ -298,12 +300,19 @@
 
     own_float[...] = own[...].astype(F32)
     normed, scaling = centred_rows(own[...], atom_gain[...])
-    near = (dot(normed, w_kv[...]) * jnp.concatenate([scaling] * 2, axis=1)).astype(BF)
-    keyval[...] = near
+    near = (dot(normed, w_key[...]) * scaling).astype(BF)
     query = (dot(normed, w_query[...]) * scaling).astype(BF)
     head_of = iota((1, width), 1) // (width // HEADS)
-    heads = jnp.concatenate([query * flag(head_of == h) for h in range(HEADS)], axis=0)
-    stacked[...] = heads
+    head_mask = [flag(head_of == h) for h in range(HEADS)]
+    heads = jnp.concatenate([query * m for m in head_mask], axis=0)
+    probes[...] = dot_t(heads, w_key[...]).astype(BF)
+    w_mix = jnp.concatenate(
+        [dot(w_value[...] * m, w_out[...]).astype(BF) for m in head_mask], axis=1
+    )
+    w_mixed[...] = w_mix
+    own_mixed[...] = (
+        dot(normed, w_mix) * jnp.concatenate([scaling] * HEADS, axis=1)
+    ).astype(BF)
     near_index = first + iota((1, rows), 1)
     far_lane = iota((1, 2 * rows), 1)
     is_low = (far_lane < rows) != even
@@ -317,10 +326,10 @@
         seen = seen & (far_index >= 0) & (far_index < atoms)
         bias.append(jnp.broadcast_to(jnp.where(seen, 0.0, MASKED), (QB, 2 * rows)))
     far_bias[...] = jnp.concatenate(bias, axis=0)
-    raw_scores = dot_t(heads, near[:, :width]) + jnp.concatenate(near_bias * HEADS, axis=0)
+    raw_scores = dot_t(heads, near) + jnp.concatenate(near_bias * HEADS, axis=0)
     scores[...] = raw_scores
     top[...] = jnp.max(raw_scores, axis=-1, keepdims=True)
-    for copy in copies[8:]:
+    for copy in copies[9:]:
         copy.wait()
     pair_width = w_outer_far.shape[1]
     average = jnp.full((pair_width, pair_width), 1.0 / pair_width, F32).astype(BF)
@@ -331,8 +340,8 @@
     neighbour,
     sibling,
     own_float,
-    keyval,
-    stacked,
+    own_mixed,
+    probes,
     scores,
     top,
     far_bias,
@@ -344,8 +353,7 @@
     before,
     goes_on,
     atom_gain,
-    w_kv,
-    w_out,
+    w_mixed,
     w_pool,
     w_back,
     w_sides,
@@ -357,9 +365,16 @@
     tiles = w_pool.shape[1] // LANES
     devices = payload.shape[0] // BLOCK
     raw = jnp.concatenate([sibling[...], neighbour[...]], axis=0)
-    normed, scaling = centred_rows(raw, atom_gain[...])
-    far = (dot(normed, w_kv[...]) * jnp.concatenate([scaling] * 2, axis=1)).astype(BF)
-    far_scores = dot_t(stacked[...], far[:, :width])
+    average = jnp.full((width, width), 1.0 / width, F32).astype(BF)
+    centred = raw.astype(F32) - dot(raw, average)
+    squares = (centred * centred).astype(BF)
+    normed = (centred * atom_gain[...]).astype(BF)
+    scaling = lax.rsqrt(dot(squares, average) + EPSILON)
+    scaling_row = lax.rsqrt(dot_t(average[:SLOTS], squares) + EPSILON)[0:1]
+    far_mixed = (
+        dot(normed, w_mixed[...]) * jnp.concatenate([scaling] * HEADS, axis=1)
+    ).astype(BF)
+    far_scores = dot_t(probes[...], normed) * scaling_row
     far_scores = far_scores + jnp.concatenate([far_bias[...]] * HEADS, axis=0)
     most = jnp.maximum(top[...], jnp.max(far_scores, axis=-1, keepdims=True))
     scale = (width // HEADS) ** (-0.5) * LOG2E
@@ -370,14 +385,14 @@
         ],
         axis=1,
     )
-    values = jnp.concatenate([far[:, width:], keyval[:, width:]], axis=0)
-    mixed = dot(raised, jnp.concatenate([values, jnp.ones((3 * rows, width), BF)], axis=1))
-    head_of = iota((1, width), 1) // (width // HEADS)
-    head_mask = [(head_of == h).astype(F32) for h in range(HEADS)]
-    total = sum(mixed[h * rows : (h + 1) * rows, :width] * head_mask[h] for h in range(HEADS))
-    weight = sum(mixed[h * rows : (h + 1) * rows, width:] * head_mask[h] for h in range(HEADS))
-    attended = (total / weight).astype(BF)
-    fresh = (own_float[...] + dot(attended, w_out[...])).astype(BF)
+    ones = jnp.ones((3 * rows, width), BF)
+    change = own_float[...]
+    for h in range(HEADS):
+        part = slice(h * width, (h + 1) * width)
+        values = jnp.concatenate([far_mixed[:, part], own_mixed[:, part]], axis=0)
+        mixed = dot(raised[h * rows : (h + 1) * rows], jnp.concatenate([values, ones], axis=1))
+        change = change + mixed[:, :width] / mixed[:, width:]
+    fresh = change.astype(BF)
     updated[...] = fresh
     feature = jnp.maximum(dot(fresh, w_pool[...]), 0.0).astype(BF)
     feature_tiles = jnp.concatenate(
@@ -571,7 +586,7 @@
         (),
         (
             held(rows, width),
-            held(rows, 2 * width, dtype=BF),
+            held(rows, HEADS * width, dtype=BF),
             held(HEADS * rows, width, dtype=BF),
             held(HEADS * rows, rows),
             held(HEADS * rows, 1),
@@ -589,8 +604,7 @@
             ),
             held(1, width),
             held(1, LANES),
-            held(width, 2 * width, dtype=BF),
-            held(width, width, dtype=BF),
+            held(width, HEADS * width, dtype=BF),
             held(width, channels, dtype=BF),
             held(channels, width, dtype=BF),
             held(2 * LANES, channels, dtype=BF),
@@ -619,14 +633,17 @@
             pltpu.VMEM((1, tokens), jnp.int32),
             pltpu.VMEM(counts_folded.shape, jnp.int32),
             pltpu.VMEM((width, width), BF),
+            pltpu.VMEM((width, width), BF),
+            pltpu.VMEM((width, width), BF),
+            pltpu.VMEM((width, width), BF),
             pltpu.VMEM((tokens, LANES), F32),
             pltpu.SemaphoreType.DMA((17,)),
         ),
     )
     (
         own_float,
-        keyval,
-        stacked,
+        own_mixed,
+        probes,
         scores,
         top,
         far_bias,
@@ -651,8 +668,8 @@
             neighbour,
             sibling,
             own_float,
-            keyval,
-            stacked,
+            own_mixed,
+            probes,
             scores,
             top,
             far_bias,

time: 25.4 us -> 25.2 us (level)
  transfers between devices with their start and end apart: 2 -> 2, of which waited for: 0 -> 0; matrix products, arithmetic and copies ran while one was open for 0% -> 0% of each run, Pallas kernels for 11% -> 12%
where the time goes in v14:
time: 25.2 us; the launch traced here: 25 us
  blocking collectives  13 us (52%)
  Pallas kernels  6.31 us (25%)
  starting transfers between devices  5.03 us (20%)
  between operations  0.72 us (3%)
    all_to_all x1, blocking collectives, per_device(): arrived = lax.all_to_all(payload.reshape(devices, BLOCK, LANES), AXES, 0, 0)  13 us
    pallas_call x3, Pallas kernels, call(): pl.pallas_call(kernel, out_shape=outputs, in_specs=[far_spec] * len(far)...  6.31 us
    ppermute x1, starting transfers between devices, per_device(): lax.ppermute(atom_feats, AXES, [(i, i ^ 1) for i in range(devices)])  4.36 us
    ppermute x1, starting transfers between devices, per_device(): lax.ppermute(atom_feats, AXES, across + [(j, i) for i, j in across])  0.66 us
  transfers between devices with their start and end apart: 2, of which 0 were waited for; matrix products, arithmetic and copies ran while one was open for 0% of the time, Pallas kernels for 12%

profile of v14, /device:TPU:0, one launch (start us, length us, event | category | flops | bytes accessed | tf_op | source)
XLA Modules:
  0.0 25.0 jit_solution(43239054139508157)
XLA Ops:
  0.6 0.7 %collective-permute-start = (bf16[64,128]{1,0:T(8,128)(2,1)}, bf16[64,128]{1,0:T(8,128)(2,1)S(1)}, u32[]{:S(2)}, u32[]{:S(2)}) collective-permute-start(bf16[64,128]{1,0:T(8,128)(2,1)} %own_far.1), channel_id=1, source_target_pairs={{1,2},{3,4},{5,6},{7,8},{9,10},{11,12},{13,14},{15,16},{17,18},{19... | collective-permute-start | bytes 49160 | tf_op jit(solution)/shard_map/ppermute | solution.py:576
  1.3 4.4 %collective-permute-start.1 = (bf16[64,128]{1,0:T(8,128)(2,1)}, bf16[64,128]{1,0:T(8,128)(2,1)S(1)}, u32[]{:S(2)}, u32[]{:S(2)}) collective-permute-start(bf16[64,128]{1,0:T(8,128)(2,1)} %own_far.1), channel_id=1, source_target_pairs={{0,1},{1,0},{2,3},{3,2},{4,5},{5,4},{6,7},{7,6},{8,9},{9,8},{10,11... | collective-permute-start | bytes 49160 | tf_op jit(solution)/shard_map/ppermute | solution.py:577
  5.7 2.9 %ready.1 = (f32[64,128]{1,0:T(8,128)S(1)}, bf16[64,512]{1,0:T(8,128)(2,1)S(1)}, bf16[256,128]{1,0:T(8,128)(2,1)S(1)}, f32[256,64]{1,0:T(8,128)S(1)}, f32[256,1]{...) custom-call(bf16[64,128]{1,0:T(8,128)(2,1)} %own_far.1, ...), custom_call_target="tpu_custom_call" | custom-call | tf_op jit(solution)/shard_map/ready/pallas_call | solution.py:535
  8.6 0.0 collective-permute-done.neighbour
  8.6 0.0 collective-permute-done.1.sibling
  8.6 0.0 copy-start.2
  8.6 0.0 copy-start.3
  8.6 1.2 %atoms.1 = (bf16[512,128]{1,0:T(8,128)(2,1)S(1)}, bf16[64,128]{1,0:T(8,128)(2,1)S(1)}, f32[16,128]{1,0:T(8,128)S(1)}) custom-call(bf16[64,128]{1,0:T(8,128)(2,1)S(1)} %collective-permute-done.neighbour, bf16[64,128]{1,0:T(8,128)(2,1)S(1)} %collective-permute-done.1.sibling, f32[64,128]{1,0:T(8,128)S(1)} %get-tuple-element.28.own_float, ...), custom_call_target="tpu_custom_call" | custom-call | tf_op jit(solution)/shard_map/atoms/pallas_call | solution.py:535
  9.8 0.0 copy-start
  9.8 0.0 copy-start.1
  9.9 13.0 %all_to_all.5 = bf16[32,16,128]{2,1,0:T(8,128)(2,1)S(1)} all-to-all(bf16[32,16,128]{2,1,0:T(8,128)(2,1)S(1)} %bitcast.10), channel_id=1, replica_groups=mesh['row'=8,'col'=4] {'row','col'}, dimensions={0} | all-to-all | bytes 262144 | tf_op jit(solution)/shard_map/all_to_all | solution.py:692
  22.8 0.0 copy-done.2
  22.8 0.0 copy-done.3
  22.8 0.0 copy-done
  22.8 0.0 copy-done.1
  22.8 2.2 %pairs.1 = (bf16[64,128]{1,0:T(8,128)(2,1)}, bf16[4,384]{1,0:T(4,128)(2,1)}, bf16[16,32,128]{2,1,0:T(8,128)(2,1)}) custom-call(bf16[512,128]{1,0:T(8,128)(2,1)S(1)} %bitcast.9, bf16[256,512]{1,0:T(8,128)(2,1)S(1)} %get-tuple-element.47.adder, bf16[64,128]{1,0:T(8,128)(2,1)S(1)} %get-tuple-element.48.updated, f32[16,128]{1,0:T(8,128)S(1)} %get-tuple-element.49.slot_back, ...), custom_call_target="tpu_custom_call" | custom-call | tf_op jit(solution)/shard_map/pairs/pallas_call | solution.py:535
Async XLA Ops:
  0.6 7.9 %collective-permute-start = (bf16[64,128]{1,0:T(8,128)(2,1)}, bf16[64,128]{1,0:T(8,128)(2,1)S(1)}, u32[]{:S(2)}, u32[]{:S(2)}) collective-permute-start(bf16[64,128]{1,0:T(8,128)(2,1)} %own_far.1), channel_id=1, source_target_pairs={{1,2},{3,4},{5,6},{7,8},{9,10},{11,12},{13,14},{15,16},{17,18},{19... | collective-permute-start | bytes 49160 | tf_op jit(solution)/shard_map/ppermute | solution.py:576
  1.3 7.3 %collective-permute-start.1 = (bf16[64,128]{1,0:T(8,128)(2,1)}, bf16[64,128]{1,0:T(8,128)(2,1)S(1)}, u32[]{:S(2)}, u32[]{:S(2)}) collective-permute-start(bf16[64,128]{1,0:T(8,128)(2,1)} %own_far.1), channel_id=1, source_target_pairs={{0,1},{1,0},{2,3},{3,2},{4,5},{5,4},{6,7},{7,6},{8,9},{9,8},{10,11... | collective-permute-start | bytes 49160 | tf_op jit(solution)/shard_map/ppermute | solution.py:577
  8.6 14.2 %copy-start.2 = (bf16[128,512]{1,0:T(8,128)(2,1)S(1)}, bf16[128,512]{1,0:T(8,128)(2,1)}, u32[]{:S(2)}) copy-start(bf16[128,512]{1,0:T(8,128)(2,1)} %w_lift.1) | copy-start | bytes 393220
  8.6 14.2 %copy-start.3 = (bf16[512,128]{1,0:T(8,128)(2,1)S(1)}, bf16[512,128]{1,0:T(8,128)(2,1)}, u32[]{:S(2)}) copy-start(bf16[512,128]{1,0:T(8,128)(2,1)} %w_drop.1) | copy-start | bytes 393220
  9.8 13.0 %copy-start = (bf16[16,32,128]{2,1,0:T(8,128)(2,1)S(1)}, bf16[16,32,128]{2,1,0:T(8,128)(2,1)}, u32[]{:S(2)}) copy-start(bf16[16,32,128]{2,1,0:T(8,128)(2,1)} %pair_state.1) | copy-start | bytes 393220
  9.8 13.0 %copy-start.1 = (bf16[128,512]{1,0:T(8,128)(2,1)S(1)}, bf16[128,512]{1,0:T(8,128)(2,1)}, u32[]{:S(2)}) copy-start(bf16[128,512]{1,0:T(8,128)(2,1)} %w_gate.1) | copy-start | bytes 393220

commit v15 on v14

--- a/solution.py
+++ b/solution.py
@@ -111,15 +111,14 @@
     scores,
     top,
     far_bias,
-    picks,
-    row_scale,
-    selects,
+    route,
     member,
     slot_scale,
     before,
     goes_on,
     last,
     adder,
+    own_scale,
     atom_gain,
     pair_gain,
     w_mixed,
@@ -135,6 +134,7 @@
     w_key,
     w_value,
     w_out,
+    begins,
     ends,
     arrivals,
 ):
@@ -164,8 +164,8 @@
     for copy in copies:
         copy.start()
 
-    tiles = picks.shape[1] // rows
-    devices = picks.shape[0] // BLOCK
+    tiles = w_pool.shape[1] // LANES
+    devices = route.shape[0] // BLOCK
     atoms = rows * devices
     own_tokens = tokens // devices
     token_rows = own_tokens * tiles
@@ -180,11 +180,11 @@
 
     for copy in copies[:9]:
         copy.wait()
-    counts_wide = jnp.broadcast_to(counts[...].astype(F32), (tiles * rows, tokens)).astype(BF)
-    counts_lane = counts_wide[:LANES]
+    counts_lane = jnp.broadcast_to(counts[...].astype(F32), (LANES, tokens)).astype(BF)
     folded = counts_folded[...].astype(F32).astype(BF)
     upper = flag(iota((LANES, LANES), 0) <= iota((LANES, LANES), 1))
     lower = flag(iota((LANES, LANES), 1) <= iota((LANES, LANES), 0))
+    below = flag(iota((LANES, LANES), 1) < iota((LANES, LANES), 0))
     within = dot(folded, upper)
     whole = dot(folded, jnp.ones((LANES, LANES), BF))
     base = jnp.zeros((1, 1), F32)
@@ -194,6 +194,7 @@
         base = base + jnp.sum(jnp.where(ended, 1.0, 0.0), axis=1, keepdims=True)
         part = slice(fold * LANES, (fold + 1) * LANES)
         ends[part, :] = passed + dot_t(lower, counts_lane[:, part])
+        begins[part, :] = passed + dot_t(below, counts_lane[:, part])
         passed = passed + whole[fold : fold + 1]
 
     base_token = base.astype(jnp.int32)
@@ -211,40 +212,44 @@
     is_first = iota((SLOTS, LANES), 0) == 0
     before[...] = jnp.where(is_first & (slot_start < first_float), 1.0, 0.0)
 
+    lanes = 2 * LANES
+    lane = iota((1, lanes), 1)
+    atom = (lane % rows + first).astype(F32)
+    inside = (atom >= jnp.concatenate([begins[...]] * 2, axis=1)) & (lane < tiles * rows)
+    inside = flag(inside & (atom < jnp.concatenate([ends[...]] * 2, axis=1)))
+    tile_fits = iota((BLOCK, lanes), 0) // own_tokens == iota((BLOCK, lanes), 1) // rows
+    tile_fits = jnp.where(tile_fits, 1.0, 0.0)
+    column = iota((1, LANES), 1) - (tiles * rows - LANES)
+    kind, slot = column // SLOTS, column % SLOTS
+    token = base_token + slot
+
     def rows_step(at):
-        def spread(lanes, axis):
-            return iota((DESTS, BLOCK, lanes), axis).reshape(DESTS * BLOCK, lanes)
-
         here = span(at, DESTS * BLOCK)
-        token_at = iota((1, tokens), 1)
-        turn = spread(tokens, 1) % own_tokens
-        row_token = (spread(tokens, 0) + at * DESTS) * own_tokens + turn
-        row_end = dot_t(flag(token_at <= row_token), counts_wide)
-        row_start = dot_t(flag(token_at < row_token), counts_wide)
-        lanes = tiles * rows
-        lane = iota((1, lanes), 1)
-        atom = (lane % rows + first).astype(F32)
-        tile_fits = spread(lanes, 1) // own_tokens == lane // rows
-        picks[here, :] = flag(tile_fits & (atom >= row_start) & (atom < row_end))
-        row_scale[here, :] = 1.0 / jnp.maximum(row_end - row_start, 1.0)[:, :LANES]
-        lanes = 3 * SLOTS
-        dest = spread(lanes, 0) + at * DESTS
-        spot = spread(lanes, 1)
-        kind = iota((1, lanes), 1) // SLOTS
-        slot = iota((1, lanes), 1) % SLOTS
+        dest = iota((DESTS, BLOCK, tokens), 0).reshape(DESTS * BLOCK, tokens) + at * DESTS
+        turn = iota((DESTS, BLOCK, tokens), 1).reshape(DESTS * BLOCK, tokens) % own_tokens
+        picks = dot(flag(iota((1, tokens), 1) == dest * own_tokens + turn), inside)
+        picks = picks.reshape(DESTS, BLOCK, lanes) * tile_fits[None]
+        picks = picks.reshape(DESTS * BLOCK, lanes)
+        dest = iota((DESTS, LANES), 0) + at * DESTS
         first_own = dest * own_tokens
         shared_tokens = overlap(base_token, first_own, own_tokens, slots)
-        token = base_token + slot
         index = jnp.where(token < first_own, slot, slot - shared_tokens)
         mine = (token >= first_own) & (token < first_own + own_tokens)
         room = 2 * (BLOCK - SLOT_ROW)
         target = jnp.where(index < room, SLOT_ROW + index // 2, jnp.where(kind == 0, 0, -1))
-        target = jnp.where(index % 2 == kind, target, -1)
-        is_slot = (kind < 2) & (slot < slots) & jnp.logical_not(mine) & (spot == target)
-        on_edge = spot == edge_row(base_token, first_own, own_tokens, slots)
+        fits = (index % 2 == kind) & (slot < slots) & jnp.logical_not(mine) & (column >= 0)
+        target = jnp.where(fits & (kind < 2), target, -1)
         beside = jnp.where(slot == 0, position - 1, position + 1)
-        is_edge = (kind == 2) & (slot < 2) & on_edge & (dest == beside)
-        selects[here, :] = flag(is_slot | is_edge)
+        is_edge = (kind == 2) & (slot < 2) & (dest == beside)
+        row = edge_row(base_token, first_own, own_tokens, slots)
+        target = jnp.where(is_edge, row, target)
+        spot = iota((BLOCK, LANES), 0)
+        selects = [
+            jnp.where(jnp.broadcast_to(target[d : d + 1], (BLOCK, LANES)) == spot, 1.0, 0.0)
+            for d in range(DESTS)
+        ]
+        high = picks[:, LANES:] + jnp.concatenate(selects, axis=0)
+        route[here, :] = jnp.concatenate([picks[:, :LANES], high], axis=1).astype(BF)
 
     repeat(devices // DESTS, rows_step)
 
@@ -252,6 +257,17 @@
     col_tokens = tokens // lax.axis_size("col")
     first_row = lax.axis_index("row") * row_tokens
     first_col = lax.axis_index("col") * col_tokens
+
+    def row_counts(height, first_token, cycle):
+        token_row = iota((height, tokens), 0) % cycle + first_token
+        return dot_t(flag(iota((1, tokens), 1) == token_row), counts_lane)
+
+    owned = [
+        row_counts(SLOTS, position * own_tokens, own_tokens),
+        row_counts(row_tokens, first_row, row_tokens),
+        row_counts(col_tokens, first_col, col_tokens),
+    ]
+    own_scale[...] = 1.0 / jnp.concatenate(owned, axis=0)
 
     def adder_step(at):
         here = span(at, LANES)
@@ -345,9 +361,7 @@
     scores,
     top,
     far_bias,
-    picks,
-    row_scale,
-    selects,
+    route,
     member,
     slot_scale,
     before,
@@ -408,12 +422,14 @@
     to_after = jnp.sum(backs * goes_on[...], axis=0, keepdims=True)
     spot = iota((SLOTS, LANES), 0)
     edges = jnp.where(spot == 0, to_before, jnp.where(spot == 1, to_after, 0.0)).astype(BF)
-    shared = jnp.concatenate([sides[:, :LANES], sides[:, LANES:], edges], axis=0)
+    spare = jnp.zeros((2 * LANES - tiles * rows - 3 * SLOTS, LANES), BF)
+    source = jnp.concatenate(
+        [feature_tiles, sides[:, :LANES], sides[:, LANES:], edges, spare], axis=0
+    )
 
     def send_step(at):
         here = span(at, DESTS * BLOCK)
-        singles = dot(picks[here, :], feature_tiles) * row_scale[here, :]
-        payload[here, :] = (singles + dot(selects[here, :], shared)).astype(BF)
+        payload[here, :] = dot(route[here, :], source).astype(BF)
 
     repeat(devices // DESTS, send_step)
 
@@ -432,6 +448,7 @@
     w_lift,
     w_drop,
     w_sides,
+    own_scale,
     atom_out,
     token_single,
     pair_out,
@@ -448,8 +465,11 @@
         parts.append(added[top : top + height])
         top += height
     sums, left_low, left_high, right_low, right_high, *own = parts
-    own_left = jnp.concatenate(own[0::2], axis=1).astype(BF)
-    own_right = jnp.concatenate(own[1::2], axis=1).astype(BF)
+    owned = own_scale[...]
+    row_scale = owned[SLOTS : SLOTS + row_tokens]
+    col_scale = owned[SLOTS + row_tokens :]
+    own_left = jnp.concatenate([part * row_scale for part in own[0::2]], axis=1).astype(BF)
+    own_right = jnp.concatenate([part * col_scale for part in own[1::2]], axis=1).astype(BF)
     own_sides = dot_t(jnp.concatenate([own_left, own_right], axis=0), w_sides[:LANES])
     left = left_low[:, :opm] + left_high[:, 2 * opm : 3 * opm] + own_sides[:row_tokens, :opm]
     right = right_low[:, opm : 2 * opm] + right_high[:, 3 * opm : 4 * opm]
@@ -515,8 +535,9 @@
         here = step * PAIR_ROWS
         pair_rows(here)
 
+    singles = sums * owned[:SLOTS]
     token_single[...] = jnp.concatenate(
-        [sums[k * own_tokens : (k + 1) * own_tokens] for k in range(tiles)], axis=1
+        [singles[k * own_tokens : (k + 1) * own_tokens] for k in range(tiles)], axis=1
     ).astype(BF)
     spot = iota((SLOTS, LANES), 0)
     from_before = jnp.where(spot == 0, sums[token_rows : token_rows + 1], 0.0)
@@ -591,9 +612,7 @@
             held(HEADS * rows, rows),
             held(HEADS * rows, 1),
             held(rows, 2 * rows),
-            held(devices * BLOCK, tiles * rows, dtype=BF),
-            held(devices * BLOCK, LANES),
-            held(devices * BLOCK, 3 * SLOTS, dtype=BF),
+            held(devices * BLOCK, 2 * LANES, dtype=BF),
             held(SLOTS, rows, dtype=BF),
             held(SLOTS, LANES),
             held(SLOTS, LANES),
@@ -602,6 +621,7 @@
             held(
                 SLOTS + (2 + tiles) * (row_tokens + col_tokens), devices * BLOCK, dtype=BF
             ),
+            held(SLOTS + row_tokens + col_tokens, LANES),
             held(1, width),
             held(1, LANES),
             held(width, HEADS * width, dtype=BF),
@@ -637,6 +657,7 @@
             pltpu.VMEM((width, width), BF),
             pltpu.VMEM((width, width), BF),
             pltpu.VMEM((tokens, LANES), F32),
+            pltpu.VMEM((tokens, LANES), F32),
             pltpu.SemaphoreType.DMA((17,)),
         ),
     )
@@ -647,15 +668,14 @@
         scores,
         top,
         far_bias,
-        picks,
-        row_scale,
-        selects,
+        route,
         member,
         slot_scale,
         before,
         goes_on,
         last,
         adder,
+        own_scale,
         atom_gain_kept,
         pair_gain_kept,
         *kept,
@@ -673,9 +693,7 @@
             scores,
             top,
             far_bias,
-            picks,
-            row_scale,
-            selects,
+            route,
             member,
             slot_scale,
             before,
@@ -707,6 +725,7 @@
             w_lift,
             w_drop,
             kept[-1],
+            own_scale,
         ),
         (
             held(rows, width, dtype=BF),

time: 25.2 us -> 25.2 us (level)
  Pallas kernels: 6.31 us -> 5.8 us
  blocking collectives: 13 us -> 13.4 us
    pallas_call x3, Pallas kernels: 6.31 us -> 5.8 us  [call(): pl.pallas_call(kernel, out_shape=outputs, in_specs=[far_spec] * len(far)...]
    all_to_all x1, blocking collectives: 13 us -> 13.4 us  [per_device(): arrived = lax.all_to_all(payload.reshape(devices, BLOCK, LANES), AXES, 0, 0)]
  transfers between devices with their start and end apart: 2 -> 2, of which waited for: 0 -> 0; matrix products, arithmetic and copies ran while one was open for 0% -> 0% of each run, Pallas kernels for 12% -> 9%
where the time goes in v15:
time: 25.2 us; the launch traced here: 25 us
  blocking collectives  13.4 us (53%)
  Pallas kernels  5.8 us (23%)
  starting transfers between devices  5.03 us (20%)
  between operations  0.72 us (3%)
    all_to_all x1, blocking collectives, per_device(): arrived = lax.all_to_all(payload.reshape(devices, BLOCK, LANES), AXES, 0, 0)  13.4 us
    pallas_call x3, Pallas kernels, call(): pl.pallas_call(kernel, out_shape=outputs, in_specs=[far_spec] * len(far)...  5.8 us
    ppermute x1, starting transfers between devices, per_device(): lax.ppermute(atom_feats, AXES, [(i, i ^ 1) for i in range(devices)])  4.36 us
    ppermute x1, starting transfers between devices, per_device(): lax.ppermute(atom_feats, AXES, across + [(j, i) for i, j in across])  0.66 us
  transfers between devices with their start and end apart: 2, of which 0 were waited for; matrix products, arithmetic and copies ran while one was open for 0% of the time, Pallas kernels for 9%

profile of v15, /device:TPU:0, one launch (start us, length us, event | category | flops | bytes accessed | tf_op | source)
XLA Modules:
  0.0 25.0 jit_solution(8719524347813679408)
XLA Ops:
  0.6 0.7 %collective-permute-start = (bf16[64,128]{1,0:T(8,128)(2,1)}, bf16[64,128]{1,0:T(8,128)(2,1)S(1)}, u32[]{:S(2)}, u32[]{:S(2)}) collective-permute-start(bf16[64,128]{1,0:T(8,128)(2,1)} %own_far.1), channel_id=1, source_target_pairs={{1,2},{3,4},{5,6},{7,8},{9,10},{11,12},{13,14},{15,16},{17,18},{19... | collective-permute-start | bytes 49160 | tf_op jit(solution)/shard_map/ppermute | solution.py:597
  1.3 4.4 %collective-permute-start.1 = (bf16[64,128]{1,0:T(8,128)(2,1)}, bf16[64,128]{1,0:T(8,128)(2,1)S(1)}, u32[]{:S(2)}, u32[]{:S(2)}) collective-permute-start(bf16[64,128]{1,0:T(8,128)(2,1)} %own_far.1), channel_id=1, source_target_pairs={{0,1},{1,0},{2,3},{3,2},{4,5},{5,4},{6,7},{7,6},{8,9},{9,8},{10,11... | collective-permute-start | bytes 49160 | tf_op jit(solution)/shard_map/ppermute | solution.py:598
  5.7 2.3 %ready.1 = (f32[64,128]{1,0:T(8,128)S(1)}, bf16[64,512]{1,0:T(8,128)(2,1)S(1)}, bf16[256,128]{1,0:T(8,128)(2,1)S(1)}, f32[256,64]{1,0:T(8,128)S(1)}, f32[256,1]{...) custom-call(bf16[64,128]{1,0:T(8,128)(2,1)} %own_far.1, ...), custom_call_target="tpu_custom_call" | custom-call | tf_op jit(solution)/shard_map/ready/pallas_call | solution.py:556
  8.0 0.0 collective-permute-done.neighbour
  8.0 0.0 collective-permute-done.1.sibling
  8.0 0.0 copy-start.2
  8.0 0.0 copy-start.3
  8.0 1.3 %atoms.1 = (bf16[512,128]{1,0:T(8,128)(2,1)S(1)}, bf16[64,128]{1,0:T(8,128)(2,1)S(1)}, f32[16,128]{1,0:T(8,128)S(1)}) custom-call(bf16[64,128]{1,0:T(8,128)(2,1)S(1)} %collective-permute-done.neighbour, bf16[64,128]{1,0:T(8,128)(2,1)S(1)} %collective-permute-done.1.sibling, f32[64,128]{1,0:T(8,128)S(1)} %get-tuple-element.27.own_float, ...), custom_call_target="tpu_custom_call" | custom-call | tf_op jit(solution)/shard_map/atoms/pallas_call | solution.py:556
  9.3 0.0 copy-start
  9.3 0.0 copy-start.1
  9.3 13.4 %all_to_all.5 = bf16[32,16,128]{2,1,0:T(8,128)(2,1)S(1)} all-to-all(bf16[32,16,128]{2,1,0:T(8,128)(2,1)S(1)} %bitcast.10), channel_id=1, replica_groups=mesh['row'=8,'col'=4] {'row','col'}, dimensions={0} | all-to-all | bytes 262144 | tf_op jit(solution)/shard_map/all_to_all | solution.py:710
  22.8 0.0 copy-done.2
  22.8 0.0 copy-done.3
  22.8 0.0 copy-done
  22.8 0.0 copy-done.1
  22.8 2.2 %pairs.1 = (bf16[64,128]{1,0:T(8,128)(2,1)}, bf16[4,384]{1,0:T(4,128)(2,1)}, bf16[16,32,128]{2,1,0:T(8,128)(2,1)}) custom-call(bf16[512,128]{1,0:T(8,128)(2,1)S(1)} %bitcast.9, bf16[256,512]{1,0:T(8,128)(2,1)S(1)} %get-tuple-element.44.adder, bf16[64,128]{1,0:T(8,128)(2,1)S(1)} %get-tuple-element.45.updated, f32[16,128]{1,0:T(8,128)S(1)} %get-tuple-element.46.slot_back, ...), custom_call_target="tpu_custom_call" | custom-call | tf_op jit(solution)/shard_map/pairs/pallas_call | solution.py:556
Async XLA Ops:
  0.6 7.4 %collective-permute-start = (bf16[64,128]{1,0:T(8,128)(2,1)}, bf16[64,128]{1,0:T(8,128)(2,1)S(1)}, u32[]{:S(2)}, u32[]{:S(2)}) collective-permute-start(bf16[64,128]{1,0:T(8,128)(2,1)} %own_far.1), channel_id=1, source_target_pairs={{1,2},{3,4},{5,6},{7,8},{9,10},{11,12},{13,14},{15,16},{17,18},{19... | collective-permute-start | bytes 49160 | tf_op jit(solution)/shard_map/ppermute | solution.py:597
  1.3 6.7 %collective-permute-start.1 = (bf16[64,128]{1,0:T(8,128)(2,1)}, bf16[64,128]{1,0:T(8,128)(2,1)S(1)}, u32[]{:S(2)}, u32[]{:S(2)}) collective-permute-start(bf16[64,128]{1,0:T(8,128)(2,1)} %own_far.1), channel_id=1, source_target_pairs={{0,1},{1,0},{2,3},{3,2},{4,5},{5,4},{6,7},{7,6},{8,9},{9,8},{10,11... | collective-permute-start | bytes 49160 | tf_op jit(solution)/shard_map/ppermute | solution.py:598
  8.0 14.8 %copy-start.2 = (bf16[128,512]{1,0:T(8,128)(2,1)S(1)}, bf16[128,512]{1,0:T(8,128)(2,1)}, u32[]{:S(2)}) copy-start(bf16[128,512]{1,0:T(8,128)(2,1)} %w_lift.1) | copy-start | bytes 393220
  8.0 14.7 %copy-start.3 = (bf16[512,128]{1,0:T(8,128)(2,1)S(1)}, bf16[512,128]{1,0:T(8,128)(2,1)}, u32[]{:S(2)}) copy-start(bf16[512,128]{1,0:T(8,128)(2,1)} %w_drop.1) | copy-start | bytes 393220
  9.3 13.5 %copy-start = (bf16[16,32,128]{2,1,0:T(8,128)(2,1)S(1)}, bf16[16,32,128]{2,1,0:T(8,128)(2,1)}, u32[]{:S(2)}) copy-start(bf16[16,32,128]{2,1,0:T(8,128)(2,1)} %pair_state.1) | copy-start | bytes 393220
  9.3 13.5 %copy-start.1 = (bf16[128,512]{1,0:T(8,128)(2,1)S(1)}, bf16[128,512]{1,0:T(8,128)(2,1)}, u32[]{:S(2)}) copy-start(bf16[128,512]{1,0:T(8,128)(2,1)} %w_gate.1) | copy-start | bytes 393220

commit v16 on v15

--- a/solution.py
+++ b/solution.py
@@ -474,9 +474,7 @@
     left = left_low[:, :opm] + left_high[:, 2 * opm : 3 * opm] + own_sides[:row_tokens, :opm]
     right = right_low[:, opm : 2 * opm] + right_high[:, 3 * opm : 4 * opm]
     right = right + own_sides[row_tokens:, opm : 2 * opm]
-    left, right = left.astype(BF), right.astype(BF)
     depth = GROUP * opm
-    unit = flag(iota((opm, depth), 1) % opm == iota((opm, depth), 0))
     corner = jnp.where(iota((GROUP, depth), 1) // opm == iota((GROUP, depth), 0), 1.0, 0.0)
 
     def spread(rows_of, first, count):
@@ -488,8 +486,8 @@
             axis=0,
         ).astype(BF)
 
-    left_wide = dot(left, unit)
-    right_blocks = spread(dot(right, unit), 0, col_tokens)
+    left_wide = jnp.concatenate([left] * GROUP, axis=1)
+    right_blocks = spread(jnp.concatenate([right] * GROUP, axis=1), 0, col_tokens)
     stages = opm // GROUP
     table = [
         dot(right_blocks, w_outer[g * depth : (g + 1) * depth, :]) for g in range(stages)
@@ -526,9 +524,9 @@
         scaling = lax.rsqrt(variance + EPSILON)
         normed = (centred * pair_gain[...]).astype(BF)
         gate = dot(normed, half_gate) * scaling
-        lift = dot(normed, w_lift[...]) * scaling
+        lift = dot(normed, w_lift[...])
         hidden = (gate * lift * (1.0 + jnp.tanh(gate))).astype(BF)
-        result = (summed + dot(hidden, w_drop[...])).astype(BF)
+        result = (summed + dot(hidden, w_drop[...]) * scaling).astype(BF)
         pair_out[pl.ds(here, PAIR_ROWS)] = result.reshape(PAIR_ROWS, col_tokens, pair_width)
 
     for step in range(row_tokens // PAIR_ROWS):

time: 25.2 us -> 25.1 us (level)
  no operation moved by 1% of the time
where the time goes in v16:
time: 25.1 us; the launch traced here: 24.9 us
  blocking collectives  13.4 us (53%)
  Pallas kernels  5.72 us (23%)
  starting transfers between devices  5.03 us (20%)
  between operations  0.72 us (3%)
    all_to_all x1, blocking collectives, per_device(): arrived = lax.all_to_all(payload.reshape(devices, BLOCK, LANES), AXES, 0, 0)  13.4 us
    pallas_call x3, Pallas kernels, call(): pl.pallas_call(kernel, out_shape=outputs, in_specs=[far_spec] * len(far)...  5.72 us
    ppermute x1, starting transfers between devices, per_device(): lax.ppermute(atom_feats, AXES, [(i, i ^ 1) for i in range(devices)])  4.36 us
    ppermute x1, starting transfers between devices, per_device(): lax.ppermute(atom_feats, AXES, across + [(j, i) for i, j in across])  0.66 us
  transfers between devices with their start and end apart: 2, of which 0 were waited for; matrix products, arithmetic and copies ran while one was open for 0% of the time, Pallas kernels for 9%

profile of v16, /device:TPU:0, one launch (start us, length us, event | category | flops | bytes accessed | tf_op | source)
XLA Modules:
  0.0 24.9 jit_solution(2472878849236091777)
XLA Ops:
  0.6 0.7 %collective-permute-start = (bf16[64,128]{1,0:T(8,128)(2,1)}, bf16[64,128]{1,0:T(8,128)(2,1)S(1)}, u32[]{:S(2)}, u32[]{:S(2)}) collective-permute-start(bf16[64,128]{1,0:T(8,128)(2,1)} %own_far.1), channel_id=1, source_target_pairs={{1,2},{3,4},{5,6},{7,8},{9,10},{11,12},{13,14},{15,16},{17,18},{19... | collective-permute-start | bytes 49160 | tf_op jit(solution)/shard_map/ppermute | solution.py:595
  1.3 4.4 %collective-permute-start.1 = (bf16[64,128]{1,0:T(8,128)(2,1)}, bf16[64,128]{1,0:T(8,128)(2,1)S(1)}, u32[]{:S(2)}, u32[]{:S(2)}) collective-permute-start(bf16[64,128]{1,0:T(8,128)(2,1)} %own_far.1), channel_id=1, source_target_pairs={{0,1},{1,0},{2,3},{3,2},{4,5},{5,4},{6,7},{7,6},{8,9},{9,8},{10,11... | collective-permute-start | bytes 49160 | tf_op jit(solution)/shard_map/ppermute | solution.py:596
  5.7 2.3 %ready.1 = (f32[64,128]{1,0:T(8,128)S(1)}, bf16[64,512]{1,0:T(8,128)(2,1)S(1)}, bf16[256,128]{1,0:T(8,128)(2,1)S(1)}, f32[256,64]{1,0:T(8,128)S(1)}, f32[256,1]{...) custom-call(bf16[64,128]{1,0:T(8,128)(2,1)} %own_far.1, ...), custom_call_target="tpu_custom_call" | custom-call | tf_op jit(solution)/shard_map/ready/pallas_call | solution.py:554
  8.0 0.0 collective-permute-done.neighbour
  8.0 0.0 collective-permute-done.1.sibling
  8.0 0.0 copy-start.2
  8.0 0.0 copy-start.3
  8.0 1.3 %atoms.1 = (bf16[512,128]{1,0:T(8,128)(2,1)S(1)}, bf16[64,128]{1,0:T(8,128)(2,1)S(1)}, f32[16,128]{1,0:T(8,128)S(1)}) custom-call(bf16[64,128]{1,0:T(8,128)(2,1)S(1)} %collective-permute-done.neighbour, bf16[64,128]{1,0:T(8,128)(2,1)S(1)} %collective-permute-done.1.sibling, f32[64,128]{1,0:T(8,128)S(1)} %get-tuple-element.27.own_float, ...), custom_call_target="tpu_custom_call" | custom-call | tf_op jit(solution)/shard_map/atoms/pallas_call | solution.py:554
  9.3 0.0 copy-start
  9.3 0.0 copy-start.1
  9.3 13.4 %all_to_all.5 = bf16[32,16,128]{2,1,0:T(8,128)(2,1)S(1)} all-to-all(bf16[32,16,128]{2,1,0:T(8,128)(2,1)S(1)} %bitcast.10), channel_id=1, replica_groups=mesh['row'=8,'col'=4] {'row','col'}, dimensions={0} | all-to-all | bytes 262144 | tf_op jit(solution)/shard_map/all_to_all | solution.py:708
  22.8 0.0 copy-done.2
  22.8 0.0 copy-done.3
  22.8 0.0 copy-done
  22.8 0.0 copy-done.1
  22.8 2.2 %pairs.1 = (bf16[64,128]{1,0:T(8,128)(2,1)}, bf16[4,384]{1,0:T(4,128)(2,1)}, bf16[16,32,128]{2,1,0:T(8,128)(2,1)}) custom-call(bf16[512,128]{1,0:T(8,128)(2,1)S(1)} %bitcast.9, bf16[256,512]{1,0:T(8,128)(2,1)S(1)} %get-tuple-element.44.adder, bf16[64,128]{1,0:T(8,128)(2,1)S(1)} %get-tuple-element.45.updated, f32[16,128]{1,0:T(8,128)S(1)} %get-tuple-element.46.slot_back, ...), custom_call_target="tpu_custom_call" | custom-call | tf_op jit(solution)/shard_map/pairs/pallas_call | solution.py:554
Async XLA Ops:
  0.6 7.4 %collective-permute-start = (bf16[64,128]{1,0:T(8,128)(2,1)}, bf16[64,128]{1,0:T(8,128)(2,1)S(1)}, u32[]{:S(2)}, u32[]{:S(2)}) collective-permute-start(bf16[64,128]{1,0:T(8,128)(2,1)} %own_far.1), channel_id=1, source_target_pairs={{1,2},{3,4},{5,6},{7,8},{9,10},{11,12},{13,14},{15,16},{17,18},{19... | collective-permute-start | bytes 49160 | tf_op jit(solution)/shard_map/ppermute | solution.py:595
  1.3 6.7 %collective-permute-start.1 = (bf16[64,128]{1,0:T(8,128)(2,1)}, bf16[64,128]{1,0:T(8,128)(2,1)S(1)}, u32[]{:S(2)}, u32[]{:S(2)}) collective-permute-start(bf16[64,128]{1,0:T(8,128)(2,1)} %own_far.1), channel_id=1, source_target_pairs={{0,1},{1,0},{2,3},{3,2},{4,5},{5,4},{6,7},{7,6},{8,9},{9,8},{10,11... | collective-permute-start | bytes 49160 | tf_op jit(solution)/shard_map/ppermute | solution.py:596
  8.0 14.8 %copy-start.2 = (bf16[128,512]{1,0:T(8,128)(2,1)S(1)}, bf16[128,512]{1,0:T(8,128)(2,1)}, u32[]{:S(2)}) copy-start(bf16[128,512]{1,0:T(8,128)(2,1)} %w_lift.1) | copy-start | bytes 393220
  8.0 14.7 %copy-start.3 = (bf16[512,128]{1,0:T(8,128)(2,1)S(1)}, bf16[512,128]{1,0:T(8,128)(2,1)}, u32[]{:S(2)}) copy-start(bf16[512,128]{1,0:T(8,128)(2,1)} %w_drop.1) | copy-start | bytes 393220
  9.3 13.5 %copy-start = (bf16[16,32,128]{2,1,0:T(8,128)(2,1)S(1)}, bf16[16,32,128]{2,1,0:T(8,128)(2,1)}, u32[]{:S(2)}) copy-start(bf16[16,32,128]{2,1,0:T(8,128)(2,1)} %pair_state.1) | copy-start | bytes 393220
  9.3 13.5 %copy-start.1 = (bf16[128,512]{1,0:T(8,128)(2,1)S(1)}, bf16[128,512]{1,0:T(8,128)(2,1)}, u32[]{:S(2)}) copy-start(bf16[128,512]{1,0:T(8,128)(2,1)} %w_gate.1) | copy-start | bytes 393220

commit v17 on v16

--- a/solution.py
+++ b/solution.py
@@ -112,10 +112,9 @@
     top,
     far_bias,
     route,
+    slot_route,
     member,
     slot_scale,
-    before,
-    goes_on,
     last,
     adder,
     own_scale,
@@ -208,9 +207,8 @@
     last_atom = first_float + (rows - 1)
     is_last = jnp.where((slot_start <= last_atom) & (slot_end > last_atom), 1.0, 0.0)
     last[...] = is_last
-    goes_on[...] = is_last * jnp.where(slot_end > first_float + rows, 1.0, 0.0)
-    is_first = iota((SLOTS, LANES), 0) == 0
-    before[...] = jnp.where(is_first & (slot_start < first_float), 1.0, 0.0)
+    goes_on = is_last * jnp.where(slot_end > first_float + rows, 1.0, 0.0)
+    carried = jnp.where(slot_start[0:1] < first_float, 1.0, 0.0)
 
     lanes = 2 * LANES
     lane = iota((1, lanes), 1)
@@ -219,7 +217,29 @@
     inside = flag(inside & (atom < jnp.concatenate([ends[...]] * 2, axis=1)))
     tile_fits = iota((BLOCK, lanes), 0) // own_tokens == iota((BLOCK, lanes), 1) // rows
     tile_fits = jnp.where(tile_fits, 1.0, 0.0)
-    column = iota((1, LANES), 1) - (tiles * rows - LANES)
+    twice = jnp.concatenate([slot_start, slot_start], axis=1)
+    held_atoms = atom >= twice
+    twice = jnp.concatenate([slot_end, slot_end], axis=1)
+    held_atoms = jnp.where(held_atoms & (atom < twice), 1.0, 0.0)
+    third = lane // rows
+    edge_atoms = jnp.concatenate(
+        [
+            held_atoms[0:1] * jnp.concatenate([carried] * 2, axis=1),
+            jnp.sum(held_atoms * jnp.concatenate([goes_on] * 2, axis=1), axis=0, keepdims=True),
+            jnp.zeros((SLOTS - 2, lanes), F32),
+        ],
+        axis=0,
+    )
+    slot_atoms = jnp.concatenate(
+        [
+            jnp.where(third == 0, held_atoms, 0.0),
+            jnp.where(third == 1, held_atoms, 0.0),
+            jnp.where(third == 2, edge_atoms, 0.0),
+            jnp.zeros((LANES - 3 * SLOTS, lanes), F32),
+        ],
+        axis=0,
+    ).astype(BF)
+    column = iota((1, LANES), 1)
     kind, slot = column // SLOTS, column % SLOTS
     token = base_token + slot
 
@@ -229,7 +249,7 @@
         turn = iota((DESTS, BLOCK, tokens), 1).reshape(DESTS * BLOCK, tokens) % own_tokens
         picks = dot(flag(iota((1, tokens), 1) == dest * own_tokens + turn), inside)
         picks = picks.reshape(DESTS, BLOCK, lanes) * tile_fits[None]
-        picks = picks.reshape(DESTS * BLOCK, lanes)
+        route[here, :] = picks.reshape(DESTS * BLOCK, lanes).astype(BF)
         dest = iota((DESTS, LANES), 0) + at * DESTS
         first_own = dest * own_tokens
         shared_tokens = overlap(base_token, first_own, own_tokens, slots)
@@ -237,7 +257,7 @@
         mine = (token >= first_own) & (token < first_own + own_tokens)
         room = 2 * (BLOCK - SLOT_ROW)
         target = jnp.where(index < room, SLOT_ROW + index // 2, jnp.where(kind == 0, 0, -1))
-        fits = (index % 2 == kind) & (slot < slots) & jnp.logical_not(mine) & (column >= 0)
+        fits = (index % 2 == kind) & (slot < slots) & jnp.logical_not(mine)
         target = jnp.where(fits & (kind < 2), target, -1)
         beside = jnp.where(slot == 0, position - 1, position + 1)
         is_edge = (kind == 2) & (slot < 2) & (dest == beside)
@@ -248,8 +268,8 @@
             jnp.where(jnp.broadcast_to(target[d : d + 1], (BLOCK, LANES)) == spot, 1.0, 0.0)
             for d in range(DESTS)
         ]
-        high = picks[:, LANES:] + jnp.concatenate(selects, axis=0)
-        route[here, :] = jnp.concatenate([picks[:, :LANES], high], axis=1).astype(BF)
+        selects = jnp.concatenate(selects, axis=0).astype(BF)
+        slot_route[here, :] = dot(selects, slot_atoms).astype(BF)
 
     repeat(devices // DESTS, rows_step)
 
@@ -362,10 +382,9 @@
     top,
     far_bias,
     route,
+    slot_route,
     member,
     slot_scale,
-    before,
-    goes_on,
     atom_gain,
     w_mixed,
     w_pool,
@@ -412,26 +431,19 @@
     feature_tiles = jnp.concatenate(
         [feature[:, k * LANES : (k + 1) * LANES] for k in range(tiles)], axis=0
     )
-    slot_single = (
-        dot(member[...], feature) * jnp.concatenate([slot_scale[...]] * tiles, axis=1)
-    ).astype(BF)
-    sides = dot_t(slot_single, w_sides[...]).astype(BF)
-    backs = dot(slot_single, w_back[...])
-    slot_back[...] = backs
-    to_before = jnp.sum(backs * before[...], axis=0, keepdims=True)
-    to_after = jnp.sum(backs * goes_on[...], axis=0, keepdims=True)
-    spot = iota((SLOTS, LANES), 0)
-    edges = jnp.where(spot == 0, to_before, jnp.where(spot == 1, to_after, 0.0)).astype(BF)
-    spare = jnp.zeros((2 * LANES - tiles * rows - 3 * SLOTS, LANES), BF)
-    source = jnp.concatenate(
-        [feature_tiles, sides[:, :LANES], sides[:, LANES:], edges, spare], axis=0
-    )
+    sides = dot_t(feature, w_sides[...]).astype(BF)
+    backs = dot(feature, w_back[...]).astype(BF)
+    spare = jnp.zeros((2 * LANES - 3 * rows, LANES), BF)
+    source = jnp.concatenate([feature_tiles, spare], axis=0)
+    slot_source = jnp.concatenate([sides[:, :LANES], sides[:, LANES:], backs, spare], axis=0)
 
     def send_step(at):
         here = span(at, DESTS * BLOCK)
-        payload[here, :] = dot(route[here, :], source).astype(BF)
+        singles = dot(route[here, :], source)
+        payload[here, :] = (singles + dot(slot_route[here, :], slot_source)).astype(BF)
 
     repeat(devices // DESTS, send_step)
+    slot_back[...] = dot(member[...], backs) * slot_scale[...]
 
 
 def pair_kernel(
@@ -440,6 +452,7 @@
     updated,
     slot_back,
     slot_last,
+    slot_scale,
     slot_member,
     pair_state,
     w_outer,
@@ -471,9 +484,10 @@
     own_left = jnp.concatenate([part * row_scale for part in own[0::2]], axis=1).astype(BF)
     own_right = jnp.concatenate([part * col_scale for part in own[1::2]], axis=1).astype(BF)
     own_sides = dot_t(jnp.concatenate([own_left, own_right], axis=0), w_sides[:LANES])
-    left = left_low[:, :opm] + left_high[:, 2 * opm : 3 * opm] + own_sides[:row_tokens, :opm]
+    left = left_low[:, :opm] + left_high[:, 2 * opm : 3 * opm]
+    left = left * row_scale[:, :opm] + own_sides[:row_tokens, :opm]
     right = right_low[:, opm : 2 * opm] + right_high[:, 3 * opm : 4 * opm]
-    right = right + own_sides[row_tokens:, opm : 2 * opm]
+    right = right * col_scale[:, :opm] + own_sides[row_tokens:, opm : 2 * opm]
     depth = GROUP * opm
     corner = jnp.where(iota((GROUP, depth), 1) // opm == iota((GROUP, depth), 0), 1.0, 0.0)
 
@@ -540,7 +554,7 @@
     spot = iota((SLOTS, LANES), 0)
     from_before = jnp.where(spot == 0, sums[token_rows : token_rows + 1], 0.0)
     from_after = slot_last[...] * sums[token_rows + 1 : token_rows + 2]
-    back = (slot_back[...] + from_before + from_after).astype(BF)
+    back = (slot_back[...] + (from_before + from_after) * slot_scale[...]).astype(BF)
     lifted = lax.dot_general(
         slot_member[...], back, (((0,), (0,)), ((), ())), preferred_element_type=F32
     )
@@ -611,9 +625,8 @@
             held(HEADS * rows, 1),
             held(rows, 2 * rows),
             held(devices * BLOCK, 2 * LANES, dtype=BF),
+            held(devices * BLOCK, 2 * LANES, dtype=BF),
             held(SLOTS, rows, dtype=BF),
-            held(SLOTS, LANES),
-            held(SLOTS, LANES),
             held(SLOTS, LANES),
             held(SLOTS, LANES),
             held(
@@ -667,10 +680,9 @@
         top,
         far_bias,
         route,
+        slot_route,
         member,
         slot_scale,
-        before,
-        goes_on,
         last,
         adder,
         own_scale,
@@ -692,10 +704,9 @@
             top,
             far_bias,
             route,
+            slot_route,
             member,
             slot_scale,
-            before,
-            goes_on,
             atom_gain_kept,
             *kept,
         ),
@@ -715,6 +726,7 @@
             updated,
             slot_back,
             last,
+            slot_scale,
             member,
             pair_state,
             w_outer_kept,

time: 25.1 us -> 25.1 us (level)
  no operation moved by 1% of the time
where the time goes in v17:
time: 25.1 us; the launch traced here: 24.9 us
  blocking collectives  13.4 us (53%)
  Pallas kernels  5.78 us (23%)
  starting transfers between devices  5.03 us (20%)
  between operations  0.71 us (3%)
    all_to_all x1, blocking collectives, per_device(): arrived = lax.all_to_all(payload.reshape(devices, BLOCK, LANES), AXES, 0, 0)  13.4 us
    pallas_call x3, Pallas kernels, call(): pl.pallas_call(kernel, out_shape=outputs, in_specs=[far_spec] * len(far)...  5.78 us
    ppermute x1, starting transfers between devices, per_device(): lax.ppermute(atom_feats, AXES, [(i, i ^ 1) for i in range(devices)])  4.36 us
    ppermute x1, starting transfers between devices, per_device(): lax.ppermute(atom_feats, AXES, across + [(j, i) for i, j in across])  0.66 us
  transfers between devices with their start and end apart: 2, of which 0 were waited for; matrix products, arithmetic and copies ran while one was open for 0% of the time, Pallas kernels for 9%

profile of v17, /device:TPU:0, one launch (start us, length us, event | category | flops | bytes accessed | tf_op | source)
XLA Modules:
  0.0 24.9 jit_solution(13868935578629256888)
XLA Ops:
  0.6 0.7 %collective-permute-start = (bf16[64,128]{1,0:T(8,128)(2,1)}, bf16[64,128]{1,0:T(8,128)(2,1)S(1)}, u32[]{:S(2)}, u32[]{:S(2)}) collective-permute-start(bf16[64,128]{1,0:T(8,128)(2,1)} %own_far.1), channel_id=1, source_target_pairs={{1,2},{3,4},{5,6},{7,8},{9,10},{11,12},{13,14},{15,16},{17,18},{19... | collective-permute-start | bytes 49160 | tf_op jit(solution)/shard_map/ppermute | solution.py:609
  1.3 4.4 %collective-permute-start.1 = (bf16[64,128]{1,0:T(8,128)(2,1)}, bf16[64,128]{1,0:T(8,128)(2,1)S(1)}, u32[]{:S(2)}, u32[]{:S(2)}) collective-permute-start(bf16[64,128]{1,0:T(8,128)(2,1)} %own_far.1), channel_id=1, source_target_pairs={{0,1},{1,0},{2,3},{3,2},{4,5},{5,4},{6,7},{7,6},{8,9},{9,8},{10,11... | collective-permute-start | bytes 49160 | tf_op jit(solution)/shard_map/ppermute | solution.py:610
  5.7 2.4 %ready.1 = (f32[64,128]{1,0:T(8,128)S(1)}, bf16[64,512]{1,0:T(8,128)(2,1)S(1)}, bf16[256,128]{1,0:T(8,128)(2,1)S(1)}, f32[256,64]{1,0:T(8,128)S(1)}, f32[256,1]{...) custom-call(bf16[64,128]{1,0:T(8,128)(2,1)} %own_far.1, ...), custom_call_target="tpu_custom_call" | custom-call | tf_op jit(solution)/shard_map/ready/pallas_call | solution.py:568
  8.0 0.0 collective-permute-done.neighbour
  8.0 0.0 collective-permute-done.1.sibling
  8.1 0.0 copy-start.2
  8.1 0.0 copy-start.3
  8.1 1.3 %atoms.1 = (bf16[512,128]{1,0:T(8,128)(2,1)S(1)}, bf16[64,128]{1,0:T(8,128)(2,1)S(1)}, f32[16,128]{1,0:T(8,128)S(1)}) custom-call(bf16[64,128]{1,0:T(8,128)(2,1)S(1)} %collective-permute-done.neighbour, bf16[64,128]{1,0:T(8,128)(2,1)S(1)} %collective-permute-done.1.sibling, f32[64,128]{1,0:T(8,128)S(1)} %get-tuple-element.26.own_float, ...), custom_call_target="tpu_custom_call" | custom-call | tf_op jit(solution)/shard_map/atoms/pallas_call | solution.py:568
  9.4 0.0 copy-start
  9.4 0.0 copy-start.1
  9.4 13.4 %all_to_all.5 = bf16[32,16,128]{2,1,0:T(8,128)(2,1)S(1)} all-to-all(bf16[32,16,128]{2,1,0:T(8,128)(2,1)S(1)} %bitcast.10), channel_id=1, replica_groups=mesh['row'=8,'col'=4] {'row','col'}, dimensions={0} | all-to-all | bytes 262144 | tf_op jit(solution)/shard_map/all_to_all | solution.py:719
  22.8 0.0 copy-done.2
  22.8 0.0 copy-done.3
  22.8 0.0 copy-done
  22.8 0.0 copy-done.1
  22.8 2.1 %pairs.1 = (bf16[64,128]{1,0:T(8,128)(2,1)}, bf16[4,384]{1,0:T(4,128)(2,1)}, bf16[16,32,128]{2,1,0:T(8,128)(2,1)}) custom-call(bf16[512,128]{1,0:T(8,128)(2,1)S(1)} %bitcast.9, bf16[256,512]{1,0:T(8,128)(2,1)S(1)} %get-tuple-element.42.adder, bf16[64,128]{1,0:T(8,128)(2,1)S(1)} %get-tuple-element.43.updated, f32[16,128]{1,0:T(8,128)S(1)} %get-tuple-element.44.slot_back, ...), custom_call_target="tpu_custom_call" | custom-call | tf_op jit(solution)/shard_map/pairs/pallas_call | solution.py:568
Async XLA Ops:
  0.6 7.4 %collective-permute-start = (bf16[64,128]{1,0:T(8,128)(2,1)}, bf16[64,128]{1,0:T(8,128)(2,1)S(1)}, u32[]{:S(2)}, u32[]{:S(2)}) collective-permute-start(bf16[64,128]{1,0:T(8,128)(2,1)} %own_far.1), channel_id=1, source_target_pairs={{1,2},{3,4},{5,6},{7,8},{9,10},{11,12},{13,14},{15,16},{17,18},{19... | collective-permute-start | bytes 49160 | tf_op jit(solution)/shard_map/ppermute | solution.py:609
  1.3 6.7 %collective-permute-start.1 = (bf16[64,128]{1,0:T(8,128)(2,1)}, bf16[64,128]{1,0:T(8,128)(2,1)S(1)}, u32[]{:S(2)}, u32[]{:S(2)}) collective-permute-start(bf16[64,128]{1,0:T(8,128)(2,1)} %own_far.1), channel_id=1, source_target_pairs={{0,1},{1,0},{2,3},{3,2},{4,5},{5,4},{6,7},{7,6},{8,9},{9,8},{10,11... | collective-permute-start | bytes 49160 | tf_op jit(solution)/shard_map/ppermute | solution.py:610
  8.1 14.7 %copy-start.2 = (bf16[128,512]{1,0:T(8,128)(2,1)S(1)}, bf16[128,512]{1,0:T(8,128)(2,1)}, u32[]{:S(2)}) copy-start(bf16[128,512]{1,0:T(8,128)(2,1)} %w_lift.1) | copy-start | bytes 393220
  8.1 14.7 %copy-start.3 = (bf16[512,128]{1,0:T(8,128)(2,1)S(1)}, bf16[512,128]{1,0:T(8,128)(2,1)}, u32[]{:S(2)}) copy-start(bf16[512,128]{1,0:T(8,128)(2,1)} %w_drop.1) | copy-start | bytes 393220
  9.4 13.4 %copy-start = (bf16[16,32,128]{2,1,0:T(8,128)(2,1)S(1)}, bf16[16,32,128]{2,1,0:T(8,128)(2,1)}, u32[]{:S(2)}) copy-start(bf16[16,32,128]{2,1,0:T(8,128)(2,1)} %pair_state.1) | copy-start | bytes 393220
  9.4 13.4 %copy-start.1 = (bf16[128,512]{1,0:T(8,128)(2,1)S(1)}, bf16[128,512]{1,0:T(8,128)(2,1)}, u32[]{:S(2)}) copy-start(bf16[128,512]{1,0:T(8,128)(2,1)} %w_gate.1) | copy-start | bytes 393220

commit v18 on v16

--- a/solution.py
+++ b/solution.py
@@ -106,9 +106,8 @@
     w_right_far,
     w_outer_far,
     own_float,
-    own_mixed,
     probes,
-    scores,
+    own_part,
     top,
     far_bias,
     route,
@@ -326,7 +325,7 @@
         [dot(w_value[...] * m, w_out[...]).astype(BF) for m in head_mask], axis=1
     )
     w_mixed[...] = w_mix
-    own_mixed[...] = (
+    own_mixed = (
         dot(normed, w_mix) * jnp.concatenate([scaling] * HEADS, axis=1)
     ).astype(BF)
     near_index = first + iota((1, rows), 1)
@@ -343,8 +342,14 @@
         bias.append(jnp.broadcast_to(jnp.where(seen, 0.0, MASKED), (QB, 2 * rows)))
     far_bias[...] = jnp.concatenate(bias, axis=0)
     raw_scores = dot_t(heads, near) + jnp.concatenate(near_bias * HEADS, axis=0)
-    scores[...] = raw_scores
-    top[...] = jnp.max(raw_scores, axis=-1, keepdims=True)
+    most = jnp.max(raw_scores, axis=-1, keepdims=True)
+    top[...] = most
+    raised = jnp.exp2((raw_scores - most) * ((width // HEADS) ** (-0.5) * LOG2E)).astype(BF)
+    ones = jnp.ones((rows, width), BF)
+    for h in range(HEADS):
+        part = slice(h * rows, (h + 1) * rows)
+        values = jnp.concatenate([own_mixed[:, h * width : (h + 1) * width], ones], axis=1)
+        own_part[part, :] = dot(raised[part], values)
     for copy in copies[9:]:
         copy.wait()
     pair_width = w_outer_far.shape[1]
@@ -356,9 +361,8 @@
     neighbour,
     sibling,
     own_float,
-    own_mixed,
     probes,
-    scores,
+    own_part,
     top,
     far_bias,
     route,
@@ -392,19 +396,14 @@
     far_scores = far_scores + jnp.concatenate([far_bias[...]] * HEADS, axis=0)
     most = jnp.maximum(top[...], jnp.max(far_scores, axis=-1, keepdims=True))
     scale = (width // HEADS) ** (-0.5) * LOG2E
-    raised = jnp.concatenate(
-        [
-            jnp.exp2((far_scores - most) * scale).astype(BF),
-            jnp.exp2((scores[...] - most) * scale).astype(BF),
-        ],
-        axis=1,
-    )
-    ones = jnp.ones((3 * rows, width), BF)
+    raised = jnp.exp2((far_scores - most) * scale).astype(BF)
+    shrink = jnp.exp2((top[...] - most) * scale)
+    ones = jnp.ones((2 * rows, width), BF)
     change = own_float[...]
     for h in range(HEADS):
-        part = slice(h * width, (h + 1) * width)
-        values = jnp.concatenate([far_mixed[:, part], own_mixed[:, part]], axis=0)
-        mixed = dot(raised[h * rows : (h + 1) * rows], jnp.concatenate([values, ones], axis=1))
+        part = slice(h * rows, (h + 1) * rows)
+        values = jnp.concatenate([far_mixed[:, h * width : (h + 1) * width], ones], axis=1)
+        mixed = dot(raised[part], values) + own_part[part, :] * shrink[part]
         change = change + mixed[:, :width] / mixed[:, width:]
     fresh = change.astype(BF)
     updated[...] = fresh
@@ -605,9 +604,8 @@
         (),
         (
             held(rows, width),
-            held(rows, HEADS * width, dtype=BF),
             held(HEADS * rows, width, dtype=BF),
-            held(HEADS * rows, rows),
+            held(HEADS * rows, 2 * width),
             held(HEADS * rows, 1),
             held(rows, 2 * rows),
             held(devices * BLOCK, 2 * LANES, dtype=BF),
@@ -661,9 +659,8 @@
     )
     (
         own_float,
-        own_mixed,
         probes,
-        scores,
+        own_part,
         top,
         far_bias,
         route,
@@ -686,9 +683,8 @@
             neighbour,
             sibling,
             own_float,
-            own_mixed,
             probes,
-            scores,
+            own_part,
             top,
             far_bias,
             route,

time: 25.1 us -> 25.1 us (level)
  no operation moved by 1% of the time
where the time goes in v18:
time: 25.1 us; the launch traced here: 24.9 us
  blocking collectives  13.4 us (53%)
  Pallas kernels  5.72 us (23%)
  starting transfers between devices  5.03 us (20%)
  between operations  0.72 us (3%)
    all_to_all x1, blocking collectives, per_device(): arrived = lax.all_to_all(payload.reshape(devices, BLOCK, LANES), AXES, 0, 0)  13.4 us
    pallas_call x3, Pallas kernels, call(): pl.pallas_call(kernel, out_shape=outputs, in_specs=[far_spec] * len(far)...  5.72 us
    ppermute x1, starting transfers between devices, per_device(): lax.ppermute(atom_feats, AXES, [(i, i ^ 1) for i in range(devices)])  4.36 us
    ppermute x1, starting transfers between devices, per_device(): lax.ppermute(atom_feats, AXES, across + [(j, i) for i, j in across])  0.66 us
  transfers between devices with their start and end apart: 2, of which 0 were waited for; matrix products, arithmetic and copies ran while one was open for 0% of the time, Pallas kernels for 9%

profile of v18, /device:TPU:0, one launch (start us, length us, event | category | flops | bytes accessed | tf_op | source)
XLA Modules:
  0.0 24.9 jit_solution(12176275154953185114)
XLA Ops:
  0.6 0.7 %collective-permute-start = (bf16[64,128]{1,0:T(8,128)(2,1)}, bf16[64,128]{1,0:T(8,128)(2,1)S(1)}, u32[]{:S(2)}, u32[]{:S(2)}) collective-permute-start(bf16[64,128]{1,0:T(8,128)(2,1)} %own_far.1), channel_id=1, source_target_pairs={{1,2},{3,4},{5,6},{7,8},{9,10},{11,12},{13,14},{15,16},{17,18},{19... | collective-permute-start | bytes 49160 | tf_op jit(solution)/shard_map/ppermute | solution.py:594
  1.3 4.4 %collective-permute-start.1 = (bf16[64,128]{1,0:T(8,128)(2,1)}, bf16[64,128]{1,0:T(8,128)(2,1)S(1)}, u32[]{:S(2)}, u32[]{:S(2)}) collective-permute-start(bf16[64,128]{1,0:T(8,128)(2,1)} %own_far.1), channel_id=1, source_target_pairs={{0,1},{1,0},{2,3},{3,2},{4,5},{5,4},{6,7},{7,6},{8,9},{9,8},{10,11... | collective-permute-start | bytes 49160 | tf_op jit(solution)/shard_map/ppermute | solution.py:595
  5.7 2.3 %ready.1 = (f32[64,128]{1,0:T(8,128)S(1)}, bf16[256,128]{1,0:T(8,128)(2,1)S(1)}, f32[256,256]{1,0:T(8,128)S(1)}, f32[256,1]{1,0:T(8,128)S(1)}, f32[64,128]{1,0:T...) custom-call(bf16[64,128]{1,0:T(8,128)(2,1)} %own_far.1, ...), custom_call_target="tpu_custom_call" | custom-call | tf_op jit(solution)/shard_map/ready/pallas_call | solution.py:553
  8.0 0.0 collective-permute-done.neighbour
  8.0 0.0 collective-permute-done.1.sibling
  8.0 0.0 copy-start.2
  8.0 0.0 copy-start.3
  8.0 1.2 %atoms.1 = (bf16[512,128]{1,0:T(8,128)(2,1)S(1)}, bf16[64,128]{1,0:T(8,128)(2,1)S(1)}, f32[16,128]{1,0:T(8,128)S(1)}) custom-call(bf16[64,128]{1,0:T(8,128)(2,1)S(1)} %collective-permute-done.neighbour, bf16[64,128]{1,0:T(8,128)(2,1)S(1)} %collective-permute-done.1.sibling, f32[64,128]{1,0:T(8,128)S(1)} %get-tuple-element.26.own_float, ...), custom_call_target="tpu_custom_call" | custom-call | tf_op jit(solution)/shard_map/atoms/pallas_call | solution.py:553
  9.3 0.0 copy-start
  9.3 0.0 copy-start.1
  9.3 13.4 %all_to_all.5 = bf16[32,16,128]{2,1,0:T(8,128)(2,1)S(1)} all-to-all(bf16[32,16,128]{2,1,0:T(8,128)(2,1)S(1)} %bitcast.10), channel_id=1, replica_groups=mesh['row'=8,'col'=4] {'row','col'}, dimensions={0} | all-to-all | bytes 262144 | tf_op jit(solution)/shard_map/all_to_all | solution.py:704
  22.7 0.0 copy-done.2
  22.7 0.0 copy-done.3
  22.7 0.0 copy-done
  22.8 0.0 copy-done.1
  22.8 2.2 %pairs.1 = (bf16[64,128]{1,0:T(8,128)(2,1)}, bf16[4,384]{1,0:T(4,128)(2,1)}, bf16[16,32,128]{2,1,0:T(8,128)(2,1)}) custom-call(bf16[512,128]{1,0:T(8,128)(2,1)S(1)} %bitcast.9, bf16[256,512]{1,0:T(8,128)(2,1)S(1)} %get-tuple-element.42.adder, bf16[64,128]{1,0:T(8,128)(2,1)S(1)} %get-tuple-element.43.updated, f32[16,128]{1,0:T(8,128)S(1)} %get-tuple-element.44.slot_back, ...), custom_call_target="tpu_custom_call" | custom-call | tf_op jit(solution)/shard_map/pairs/pallas_call | solution.py:553
Async XLA Ops:
  0.6 7.4 %collective-permute-start = (bf16[64,128]{1,0:T(8,128)(2,1)}, bf16[64,128]{1,0:T(8,128)(2,1)S(1)}, u32[]{:S(2)}, u32[]{:S(2)}) collective-permute-start(bf16[64,128]{1,0:T(8,128)(2,1)} %own_far.1), channel_id=1, source_target_pairs={{1,2},{3,4},{5,6},{7,8},{9,10},{11,12},{13,14},{15,16},{17,18},{19... | collective-permute-start | bytes 49160 | tf_op jit(solution)/shard_map/ppermute | solution.py:594
  1.3 6.7 %collective-permute-start.1 = (bf16[64,128]{1,0:T(8,128)(2,1)}, bf16[64,128]{1,0:T(8,128)(2,1)S(1)}, u32[]{:S(2)}, u32[]{:S(2)}) collective-permute-start(bf16[64,128]{1,0:T(8,128)(2,1)} %own_far.1), channel_id=1, source_target_pairs={{0,1},{1,0},{2,3},{3,2},{4,5},{5,4},{6,7},{7,6},{8,9},{9,8},{10,11... | collective-permute-start | bytes 49160 | tf_op jit(solution)/shard_map/ppermute | solution.py:595
  8.0 14.7 %copy-start.2 = (bf16[128,512]{1,0:T(8,128)(2,1)S(1)}, bf16[128,512]{1,0:T(8,128)(2,1)}, u32[]{:S(2)}) copy-start(bf16[128,512]{1,0:T(8,128)(2,1)} %w_lift.1) | copy-start | bytes 393220
  8.0 14.7 %copy-start.3 = (bf16[512,128]{1,0:T(8,128)(2,1)S(1)}, bf16[512,128]{1,0:T(8,128)(2,1)}, u32[]{:S(2)}) copy-start(bf16[512,128]{1,0:T(8,128)(2,1)} %w_drop.1) | copy-start | bytes 393220
  9.3 13.5 %copy-start = (bf16[16,32,128]{2,1,0:T(8,128)(2,1)S(1)}, bf16[16,32,128]{2,1,0:T(8,128)(2,1)}, u32[]{:S(2)}) copy-start(bf16[16,32,128]{2,1,0:T(8,128)(2,1)} %pair_state.1) | copy-start | bytes 393220
  9.3 13.4 %copy-start.1 = (bf16[128,512]{1,0:T(8,128)(2,1)S(1)}, bf16[128,512]{1,0:T(8,128)(2,1)}, u32[]{:S(2)}) copy-start(bf16[128,512]{1,0:T(8,128)(2,1)} %w_gate.1) | copy-start | bytes 393220

commit v19 on v16

--- a/solution.py
+++ b/solution.py
@@ -124,7 +124,7 @@
     w_mixed,
     w_pool,
     w_back,
-    w_sides,
+    w_turned,
     w_outer,
     own,
     key_starts,
@@ -134,6 +134,7 @@
     w_key,
     w_value,
     w_out,
+    w_sides,
     begins,
     ends,
     arrivals,
@@ -347,6 +348,9 @@
     top[...] = jnp.max(raw_scores, axis=-1, keepdims=True)
     for copy in copies[9:]:
         copy.wait()
+    channels = tiles * LANES
+    same = flag(iota((channels, channels), 0) == iota((channels, channels), 1))
+    w_turned[...] = dot_t(same, w_sides[...]).astype(BF)
     pair_width = w_outer_far.shape[1]
     average = jnp.full((pair_width, pair_width), 1.0 / pair_width, F32).astype(BF)
     w_outer[:, pair_width:] = dot(w_outer[:, :pair_width], average).astype(BF)
@@ -415,7 +419,7 @@
     slot_single = (
         dot(member[...], feature) * jnp.concatenate([slot_scale[...]] * tiles, axis=1)
     ).astype(BF)
-    sides = dot_t(slot_single, w_sides[...]).astype(BF)
+    sides = dot(slot_single, w_sides[...]).astype(BF)
     backs = dot(slot_single, w_back[...])
     slot_back[...] = backs
     to_before = jnp.sum(backs * before[...], axis=0, keepdims=True)
@@ -470,7 +474,7 @@
     col_scale = owned[SLOTS + row_tokens :]
     own_left = jnp.concatenate([part * row_scale for part in own[0::2]], axis=1).astype(BF)
     own_right = jnp.concatenate([part * col_scale for part in own[1::2]], axis=1).astype(BF)
-    own_sides = dot_t(jnp.concatenate([own_left, own_right], axis=0), w_sides[:LANES])
+    own_sides = dot(jnp.concatenate([own_left, own_right], axis=0), w_sides[:, :LANES])
     left = left_low[:, :opm] + left_high[:, 2 * opm : 3 * opm] + own_sides[:row_tokens, :opm]
     right = right_low[:, opm : 2 * opm] + right_high[:, 3 * opm : 4 * opm]
     right = right + own_sides[row_tokens:, opm : 2 * opm]
@@ -625,7 +629,7 @@
             held(width, HEADS * width, dtype=BF),
             held(width, channels, dtype=BF),
             held(channels, width, dtype=BF),
-            held(2 * LANES, channels, dtype=BF),
+            held(channels, 2 * LANES, dtype=BF),
             held(opm * opm, 2 * w_outer.shape[-1], dtype=BF),
         ),
         far=(
@@ -654,6 +658,7 @@
             pltpu.VMEM((width, width), BF),
             pltpu.VMEM((width, width), BF),
             pltpu.VMEM((width, width), BF),
+            pltpu.VMEM((2 * LANES, channels), BF),
             pltpu.VMEM((tokens, LANES), F32),
             pltpu.VMEM((tokens, LANES), F32),
             pltpu.SemaphoreType.DMA((17,)),

time: 25.1 us -> 25.1 us (level)
  transfers between devices with their start and end apart: 2 -> 2, of which waited for: 0 -> 0; matrix products, arithmetic and copies ran while one was open for 0% -> 0% of each run, Pallas kernels for 9% -> 10%
where the time goes in v19:
time: 25.1 us; the launch traced here: 24.9 us
  blocking collectives  13.3 us (53%)
  Pallas kernels  5.81 us (23%)
  starting transfers between devices  5.03 us (20%)
  between operations  0.72 us (3%)
    all_to_all x1, blocking collectives, per_device(): arrived = lax.all_to_all(payload.reshape(devices, BLOCK, LANES), AXES, 0, 0)  13.3 us
    pallas_call x3, Pallas kernels, call(): pl.pallas_call(kernel, out_shape=outputs, in_specs=[far_spec] * len(far)...  5.81 us
    ppermute x1, starting transfers between devices, per_device(): lax.ppermute(atom_feats, AXES, [(i, i ^ 1) for i in range(devices)])  4.36 us
    ppermute x1, starting transfers between devices, per_device(): lax.ppermute(atom_feats, AXES, across + [(j, i) for i, j in across])  0.66 us
  transfers between devices with their start and end apart: 2, of which 0 were waited for; matrix products, arithmetic and copies ran while one was open for 0% of the time, Pallas kernels for 10%

profile of v19, /device:TPU:0, one launch (start us, length us, event | category | flops | bytes accessed | tf_op | source)
XLA Modules:
  0.0 24.9 jit_solution(984252138218397110)
XLA Ops:
  0.6 0.7 %collective-permute-start = (bf16[64,128]{1,0:T(8,128)(2,1)}, bf16[64,128]{1,0:T(8,128)(2,1)S(1)}, u32[]{:S(2)}, u32[]{:S(2)}) collective-permute-start(bf16[64,128]{1,0:T(8,128)(2,1)} %own_far.1), channel_id=1, source_target_pairs={{1,2},{3,4},{5,6},{7,8},{9,10},{11,12},{13,14},{15,16},{17,18},{19... | collective-permute-start | bytes 49160 | tf_op jit(solution)/shard_map/ppermute | solution.py:599
  1.3 4.4 %collective-permute-start.1 = (bf16[64,128]{1,0:T(8,128)(2,1)}, bf16[64,128]{1,0:T(8,128)(2,1)S(1)}, u32[]{:S(2)}, u32[]{:S(2)}) collective-permute-start(bf16[64,128]{1,0:T(8,128)(2,1)} %own_far.1), channel_id=1, source_target_pairs={{0,1},{1,0},{2,3},{3,2},{4,5},{5,4},{6,7},{7,6},{8,9},{9,8},{10,11... | collective-permute-start | bytes 49160 | tf_op jit(solution)/shard_map/ppermute | solution.py:600
  5.7 2.4 %ready.1 = (f32[64,128]{1,0:T(8,128)S(1)}, bf16[64,512]{1,0:T(8,128)(2,1)S(1)}, bf16[256,128]{1,0:T(8,128)(2,1)S(1)}, f32[256,64]{1,0:T(8,128)S(1)}, f32[256,1]{...) custom-call(bf16[64,128]{1,0:T(8,128)(2,1)} %own_far.1, ...), custom_call_target="tpu_custom_call" | custom-call | tf_op jit(solution)/shard_map/ready/pallas_call | solution.py:558
  8.1 0.0 collective-permute-done.neighbour
  8.1 0.0 collective-permute-done.1.sibling
  8.1 0.0 copy-start.2
  8.1 0.0 copy-start.3
  8.1 1.2 %atoms.1 = (bf16[512,128]{1,0:T(8,128)(2,1)S(1)}, bf16[64,128]{1,0:T(8,128)(2,1)S(1)}, f32[16,128]{1,0:T(8,128)S(1)}) custom-call(bf16[64,128]{1,0:T(8,128)(2,1)S(1)} %collective-permute-done.neighbour, bf16[64,128]{1,0:T(8,128)(2,1)S(1)} %collective-permute-done.1.sibling, f32[64,128]{1,0:T(8,128)S(1)} %get-tuple-element.27.own_float, ...), custom_call_target="tpu_custom_call" | custom-call | tf_op jit(solution)/shard_map/atoms/pallas_call | solution.py:558
  9.4 0.0 copy-start
  9.4 0.0 copy-start.1
  9.4 13.3 %all_to_all.5 = bf16[32,16,128]{2,1,0:T(8,128)(2,1)S(1)} all-to-all(bf16[32,16,128]{2,1,0:T(8,128)(2,1)S(1)} %bitcast.10), channel_id=1, replica_groups=mesh['row'=8,'col'=4] {'row','col'}, dimensions={0} | all-to-all | bytes 262144 | tf_op jit(solution)/shard_map/all_to_all | solution.py:713
  22.7 0.0 copy-done.2
  22.7 0.0 copy-done.3
  22.7 0.0 copy-done
  22.7 0.0 copy-done.1
  22.7 2.2 %pairs.1 = (bf16[64,128]{1,0:T(8,128)(2,1)}, bf16[4,384]{1,0:T(4,128)(2,1)}, bf16[16,32,128]{2,1,0:T(8,128)(2,1)}) custom-call(bf16[512,128]{1,0:T(8,128)(2,1)S(1)} %bitcast.9, bf16[256,512]{1,0:T(8,128)(2,1)S(1)} %get-tuple-element.44.adder, bf16[64,128]{1,0:T(8,128)(2,1)S(1)} %get-tuple-element.45.updated, f32[16,128]{1,0:T(8,128)S(1)} %get-tuple-element.46.slot_back, ...), custom_call_target="tpu_custom_call" | custom-call | tf_op jit(solution)/shard_map/pairs/pallas_call | solution.py:558
Async XLA Ops:
  0.6 7.5 %collective-permute-start = (bf16[64,128]{1,0:T(8,128)(2,1)}, bf16[64,128]{1,0:T(8,128)(2,1)S(1)}, u32[]{:S(2)}, u32[]{:S(2)}) collective-permute-start(bf16[64,128]{1,0:T(8,128)(2,1)} %own_far.1), channel_id=1, source_target_pairs={{1,2},{3,4},{5,6},{7,8},{9,10},{11,12},{13,14},{15,16},{17,18},{19... | collective-permute-start | bytes 49160 | tf_op jit(solution)/shard_map/ppermute | solution.py:599
  1.3 6.8 %collective-permute-start.1 = (bf16[64,128]{1,0:T(8,128)(2,1)}, bf16[64,128]{1,0:T(8,128)(2,1)S(1)}, u32[]{:S(2)}, u32[]{:S(2)}) collective-permute-start(bf16[64,128]{1,0:T(8,128)(2,1)} %own_far.1), channel_id=1, source_target_pairs={{0,1},{1,0},{2,3},{3,2},{4,5},{5,4},{6,7},{7,6},{8,9},{9,8},{10,11... | collective-permute-start | bytes 49160 | tf_op jit(solution)/shard_map/ppermute | solution.py:600
  8.1 14.6 %copy-start.2 = (bf16[128,512]{1,0:T(8,128)(2,1)S(1)}, bf16[128,512]{1,0:T(8,128)(2,1)}, u32[]{:S(2)}) copy-start(bf16[128,512]{1,0:T(8,128)(2,1)} %w_lift.1) | copy-start | bytes 393220
  8.1 14.6 %copy-start.3 = (bf16[512,128]{1,0:T(8,128)(2,1)S(1)}, bf16[512,128]{1,0:T(8,128)(2,1)}, u32[]{:S(2)}) copy-start(bf16[512,128]{1,0:T(8,128)(2,1)} %w_drop.1) | copy-start | bytes 393220
  9.4 13.3 %copy-start = (bf16[16,32,128]{2,1,0:T(8,128)(2,1)S(1)}, bf16[16,32,128]{2,1,0:T(8,128)(2,1)}, u32[]{:S(2)}) copy-start(bf16[16,32,128]{2,1,0:T(8,128)(2,1)} %pair_state.1) | copy-start | bytes 393220
  9.4 13.3 %copy-start.1 = (bf16[128,512]{1,0:T(8,128)(2,1)S(1)}, bf16[128,512]{1,0:T(8,128)(2,1)}, u32[]{:S(2)}) copy-start(bf16[128,512]{1,0:T(8,128)(2,1)} %w_gate.1) | copy-start | bytes 393220

commit v20 on v16

--- a/solution.py
+++ b/solution.py
@@ -422,14 +422,18 @@
     to_after = jnp.sum(backs * goes_on[...], axis=0, keepdims=True)
     spot = iota((SLOTS, LANES), 0)
     edges = jnp.where(spot == 0, to_before, jnp.where(spot == 1, to_after, 0.0)).astype(BF)
-    spare = jnp.zeros((2 * LANES - tiles * rows - 3 * SLOTS, LANES), BF)
-    source = jnp.concatenate(
-        [feature_tiles, sides[:, :LANES], sides[:, LANES:], edges, spare], axis=0
+    ahead = tiles * rows - LANES
+    spare = jnp.zeros((LANES - ahead, LANES), BF)
+    source = jnp.concatenate([feature_tiles, spare], axis=0)
+    spare = jnp.zeros((LANES - ahead - 3 * SLOTS, LANES), BF)
+    slot_source = jnp.concatenate(
+        [jnp.zeros((ahead, LANES), BF), sides[:, :LANES], sides[:, LANES:], edges, spare], axis=0
     )
 
     def send_step(at):
         here = span(at, DESTS * BLOCK)
-        payload[here, :] = dot(route[here, :], source).astype(BF)
+        singles = dot(route[here, :], source)
+        payload[here, :] = (singles + dot(route[here, LANES:], slot_source)).astype(BF)
 
     repeat(devices // DESTS, send_step)
 

time: 25.1 us -> 25.1 us (level)
  no operation moved by 1% of the time
where the time goes in v20:
time: 25.1 us; the launch traced here: 25 us
  blocking collectives  13.4 us (53%)
  Pallas kernels  5.76 us (23%)
  starting transfers between devices  5.03 us (20%)
  between operations  0.71 us (3%)
    all_to_all x1, blocking collectives, per_device(): arrived = lax.all_to_all(payload.reshape(devices, BLOCK, LANES), AXES, 0, 0)  13.4 us
    pallas_call x3, Pallas kernels, call(): pl.pallas_call(kernel, out_shape=outputs, in_specs=[far_spec] * len(far)...  5.76 us
    ppermute x1, starting transfers between devices, per_device(): lax.ppermute(atom_feats, AXES, [(i, i ^ 1) for i in range(devices)])  4.36 us
    ppermute x1, starting transfers between devices, per_device(): lax.ppermute(atom_feats, AXES, across + [(j, i) for i, j in across])  0.66 us
  transfers between devices with their start and end apart: 2, of which 0 were waited for; matrix products, arithmetic and copies ran while one was open for 0% of the time, Pallas kernels for 9%

profile of v20, /device:TPU:0, one launch (start us, length us, event | category | flops | bytes accessed | tf_op | source)
XLA Modules:
  0.0 25.0 jit_solution(10970015218758211284)
XLA Ops:
  0.6 0.7 %collective-permute-start = (bf16[64,128]{1,0:T(8,128)(2,1)}, bf16[64,128]{1,0:T(8,128)(2,1)S(1)}, u32[]{:S(2)}, u32[]{:S(2)}) collective-permute-start(bf16[64,128]{1,0:T(8,128)(2,1)} %own_far.1), channel_id=1, source_target_pairs={{1,2},{3,4},{5,6},{7,8},{9,10},{11,12},{13,14},{15,16},{17,18},{19... | collective-permute-start | bytes 49160 | tf_op jit(solution)/shard_map/ppermute | solution.py:599
  1.3 4.4 %collective-permute-start.1 = (bf16[64,128]{1,0:T(8,128)(2,1)}, bf16[64,128]{1,0:T(8,128)(2,1)S(1)}, u32[]{:S(2)}, u32[]{:S(2)}) collective-permute-start(bf16[64,128]{1,0:T(8,128)(2,1)} %own_far.1), channel_id=1, source_target_pairs={{0,1},{1,0},{2,3},{3,2},{4,5},{5,4},{6,7},{7,6},{8,9},{9,8},{10,11... | collective-permute-start | bytes 49160 | tf_op jit(solution)/shard_map/ppermute | solution.py:600
  5.7 2.3 %ready.1 = (f32[64,128]{1,0:T(8,128)S(1)}, bf16[64,512]{1,0:T(8,128)(2,1)S(1)}, bf16[256,128]{1,0:T(8,128)(2,1)S(1)}, f32[256,64]{1,0:T(8,128)S(1)}, f32[256,1]{...) custom-call(bf16[64,128]{1,0:T(8,128)(2,1)} %own_far.1, ...), custom_call_target="tpu_custom_call" | custom-call | tf_op jit(solution)/shard_map/ready/pallas_call | solution.py:558
  8.0 0.0 collective-permute-done.neighbour
  8.0 0.0 collective-permute-done.1.sibling
  8.0 0.0 copy-start.2
  8.0 0.0 copy-start.3
  8.0 1.3 %atoms.1 = (bf16[512,128]{1,0:T(8,128)(2,1)S(1)}, bf16[64,128]{1,0:T(8,128)(2,1)S(1)}, f32[16,128]{1,0:T(8,128)S(1)}) custom-call(bf16[64,128]{1,0:T(8,128)(2,1)S(1)} %collective-permute-done.neighbour, bf16[64,128]{1,0:T(8,128)(2,1)S(1)} %collective-permute-done.1.sibling, f32[64,128]{1,0:T(8,128)S(1)} %get-tuple-element.27.own_float, ...), custom_call_target="tpu_custom_call" | custom-call | tf_op jit(solution)/shard_map/atoms/pallas_call | solution.py:558
  9.3 0.0 copy-start
  9.3 0.0 copy-start.1
  9.4 13.4 %all_to_all.5 = bf16[32,16,128]{2,1,0:T(8,128)(2,1)S(1)} all-to-all(bf16[32,16,128]{2,1,0:T(8,128)(2,1)S(1)} %bitcast.10), channel_id=1, replica_groups=mesh['row'=8,'col'=4] {'row','col'}, dimensions={0} | all-to-all | bytes 262144 | tf_op jit(solution)/shard_map/all_to_all | solution.py:712
  22.8 0.0 copy-done.2
  22.8 0.0 copy-done.3
  22.8 0.0 copy-done
  22.8 0.0 copy-done.1
  22.8 2.2 %pairs.1 = (bf16[64,128]{1,0:T(8,128)(2,1)}, bf16[4,384]{1,0:T(4,128)(2,1)}, bf16[16,32,128]{2,1,0:T(8,128)(2,1)}) custom-call(bf16[512,128]{1,0:T(8,128)(2,1)S(1)} %bitcast.9, bf16[256,512]{1,0:T(8,128)(2,1)S(1)} %get-tuple-element.44.adder, bf16[64,128]{1,0:T(8,128)(2,1)S(1)} %get-tuple-element.45.updated, f32[16,128]{1,0:T(8,128)S(1)} %get-tuple-element.46.slot_back, ...), custom_call_target="tpu_custom_call" | custom-call | tf_op jit(solution)/shard_map/pairs/pallas_call | solution.py:558
Async XLA Ops:
  0.6 7.4 %collective-permute-start = (bf16[64,128]{1,0:T(8,128)(2,1)}, bf16[64,128]{1,0:T(8,128)(2,1)S(1)}, u32[]{:S(2)}, u32[]{:S(2)}) collective-permute-start(bf16[64,128]{1,0:T(8,128)(2,1)} %own_far.1), channel_id=1, source_target_pairs={{1,2},{3,4},{5,6},{7,8},{9,10},{11,12},{13,14},{15,16},{17,18},{19... | collective-permute-start | bytes 49160 | tf_op jit(solution)/shard_map/ppermute | solution.py:599
  1.3 6.7 %collective-permute-start.1 = (bf16[64,128]{1,0:T(8,128)(2,1)}, bf16[64,128]{1,0:T(8,128)(2,1)S(1)}, u32[]{:S(2)}, u32[]{:S(2)}) collective-permute-start(bf16[64,128]{1,0:T(8,128)(2,1)} %own_far.1), channel_id=1, source_target_pairs={{0,1},{1,0},{2,3},{3,2},{4,5},{5,4},{6,7},{7,6},{8,9},{9,8},{10,11... | collective-permute-start | bytes 49160 | tf_op jit(solution)/shard_map/ppermute | solution.py:600
  8.0 14.8 %copy-start.2 = (bf16[128,512]{1,0:T(8,128)(2,1)S(1)}, bf16[128,512]{1,0:T(8,128)(2,1)}, u32[]{:S(2)}) copy-start(bf16[128,512]{1,0:T(8,128)(2,1)} %w_lift.1) | copy-start | bytes 393220
  8.0 14.8 %copy-start.3 = (bf16[512,128]{1,0:T(8,128)(2,1)S(1)}, bf16[512,128]{1,0:T(8,128)(2,1)}, u32[]{:S(2)}) copy-start(bf16[512,128]{1,0:T(8,128)(2,1)} %w_drop.1) | copy-start | bytes 393220
  9.3 13.5 %copy-start = (bf16[16,32,128]{2,1,0:T(8,128)(2,1)S(1)}, bf16[16,32,128]{2,1,0:T(8,128)(2,1)}, u32[]{:S(2)}) copy-start(bf16[16,32,128]{2,1,0:T(8,128)(2,1)} %pair_state.1) | copy-start | bytes 393220
  9.3 13.5 %copy-start.1 = (bf16[128,512]{1,0:T(8,128)(2,1)S(1)}, bf16[128,512]{1,0:T(8,128)(2,1)}, u32[]{:S(2)}) copy-start(bf16[128,512]{1,0:T(8,128)(2,1)} %w_gate.1) | copy-start | bytes 393220
